TPU v7x, 32 devices: a whole 2x2x4 slice. The times are simulated.
32 devices in a mesh: freq: 4 (over y, x), tm: 8 (over z, core).
Axes of the slice: x: 2, y: 2, z: 4, core: 2. Of those that a mesh axis runs over, the one named last changes fastest.
Arguments:
- voltages: bfloat16 [2048, 530432], P(('tm', 'freq')), may hold values from -128 to 127, as said below
- fir_taps: float32 [4, 2048], replicated, may hold values from -3 to 3
Outputs:
- coherence: bfloat16 [2, 32, 2048, 2048], P(None, 'freq', 'tm')
Inputs may be any that keep to these rules, and one draw needn't show every extreme that they name: `voltages`: every sample is a whole number.
All inputs are finite; a program needn't handle non-finite values.
Results may differ from a plain program's by a relative error of at most 0.0073.
Values may be sent and summed in bfloat16 or wider, within the bound.
No kernel may reach another device: no remote copies, remote signals or barrier semaphores. Data moves between devices by JAX's collectives and lax.ppermute only.
A program may use at most 384 MiB of HBM per device.

v0:
```python
import math

import jax
import jax.numpy as jnp
from jax import lax
from jax.sharding import PartitionSpec as P

P_SIZE = 2048
TAPS = 4
FIRST_BIN = 512
CH_DEV = 8
S = 256


def dft_table(channels):
    points = jnp.arange(P_SIZE, dtype=jnp.int32)
    bins = FIRST_BIN + jnp.arange(channels, dtype=jnp.int32)
    phase = points[:, None] * bins[None, :] % P_SIZE
    angle = 2.0 * math.pi / P_SIZE * phase.astype(jnp.float32)
    twiddle = jnp.stack([jnp.cos(angle), -jnp.sin(angle)], axis=2)
    return twiddle.reshape(P_SIZE, 2 * channels).astype(jnp.bfloat16)


def filter_frames(block, fir_taps):
    inputs_here = block.shape[0]
    samples = block.astype(jnp.float32).reshape(inputs_here, S + TAPS - 1, P_SIZE)
    frames = fir_taps[0] * samples[:, 0:S]
    for tap_index in range(1, TAPS):
        frames = frames + fir_taps[tap_index] * samples[:, tap_index : tap_index + S]
    return frames.astype(jnp.bfloat16).reshape(inputs_here * S, P_SIZE)


def correlate(own_spectra, column_block):
    slab = own_spectra.shape[0]
    rows_here = own_spectra.shape[2]
    width = column_block.shape[2]
    left_rows = own_spectra.reshape(slab, 2 * rows_here, S)
    right_rows = column_block.reshape(slab, 2 * width, S)
    products = lax.dot_general(
        left_rows, right_rows, (((2,), (2,)), ((0,), (0,))), preferred_element_type=jnp.float32
    )
    products = products.reshape(slab, 2, rows_here, 2, width)
    real_part = products[:, 0, :, 0] + products[:, 1, :, 1]
    imag_part = products[:, 1, :, 0] - products[:, 0, :, 1]
    return jnp.stack([real_part, imag_part])


def on_device(voltages, fir_taps):
    freq_count = lax.axis_size("freq")
    channels = CH_DEV * freq_count
    inputs_here = voltages.shape[0]
    frames = filter_frames(voltages, fir_taps)
    twiddle = dft_table(channels)
    spectra = lax.dot_general(
        twiddle, frames, (((0,), (1,)), ((), ())), preferred_element_type=jnp.float32
    )
    spectra = spectra.astype(jnp.bfloat16).reshape(channels, 2, inputs_here, S)
    own_spectra = lax.all_to_all(spectra, "freq", split_axis=0, concat_axis=2, tiled=True)
    all_spectra = lax.all_gather(own_spectra, "tm", axis=2, tiled=True)
    raw_sums = correlate(own_spectra, all_spectra)
    wide = own_spectra.astype(jnp.float32)
    powers = jnp.sum(wide * wide, axis=(1, 3)) / S + 1e-06
    powers_all = lax.all_gather(powers, "tm", axis=1, tiled=True)
    row_scale = lax.rsqrt(powers) / S
    column_scale = lax.rsqrt(powers_all)
    coherence = raw_sums * row_scale[None, :, :, None] * column_scale[None, :, None, :]
    return coherence.astype(jnp.bfloat16)


def solution(mesh):
    placed = (P(("tm", "freq"), None), P())
    return jax.shard_map(
        on_device,
        mesh=mesh,
        in_specs=placed,
        out_specs=P(None, "freq", "tm", None),
        check_vma=False,
    )
```

profile of v0, /device:TPU:0, one launch (start us, length us, event | category | flops | bytes accessed | tf_op | source)
XLA Modules:
  0.0 765.8 jit_solution(17581294262606451513)
XLA Ops:
  6.5 0.0 all-gather.2.cloned.1.call-start
  6.5 0.9 fusion.15
  7.5 101.5 %reshape.197 = f32[64,259,2048]{2,1,0:T(8,128)} reshape(bf16[64,530432]{1,0:T(8,128)(2,1)} %param.2) | data formatting | bytes 203685888 | tf_op jit(solution)/shard_map/reshape | solution.py:26
  109.0 1.2 cosine_convert_fusion
  110.3 0.3 copy.13
  110.6 0.8 convert_element_type.41
  111.4 0.0 copy-start
  111.4 186.6 %fusion.1 = bf16[64,256,2048]{2,1,0:T(8,128)(2,1)} fusion(f32[64,259,2048]{2,1,0:T(8,128)} %reshape.197, f32[2048]{0:T(1024)S(1)} %bitcast.35, f32[2048]{0:T(1024)S(1)} %bitcast.36, f32[2048]{0:T(1024)S(1)} %bitcast.34, f32[2048]{0:T(1024)S(1)} %bitcast.33), kind=kLoop, calls=%fused_computation.2 | loop fusion | flops 268435456 | bytes 604012544 | tf_op jit(solution)/shard_map/convert_element_type | solution.py:30
  297.9 0.0 copy-done
  297.9 27.5 %convolution_convert_fusion = bf16[64,16384]{1,0:T(8,128)(2,1)S(1)} fusion(bf16[2048,64]{0,1:T(8,128)(2,1)S(1)} %copy-done, bf16[16384,2048]{1,0:T(8,128)(2,1)} %bitcast.4), kind=kOutput, calls=%fused_computation.11 | convolution fusion | flops 4296015872 | bytes 69468160 | tf_op jit(solution)/shard_map/dot_general | solution.py:54
  325.5 0.5 copy.23
  326.0 30.3 %all_to_all.18 = bf16[32,2,64,256]{3,2,1,0:T(8,128)(2,1)S(1)} all-to-all(bf16[32,2,64,256]{3,2,1,0:T(8,128)(2,1)S(1)} %bitcast.32), channel_id=1, replica_groups=mesh['freq'=4,'tm'=8] {'freq'}, dimensions={0} | all-to-all | bytes 4194304 | tf_op jit(solution)/shard_map/all_to_all | solution.py:58
  356.4 1.5 copy.14
  357.8 0.0 all-gather.2.cloned.1.call-update
  357.8 0.5 multiply_reduce_fusion
  358.3 0.1 add.76
  358.4 14.4 %all_gather.7 = f32[8,2048]{1,0:T(8,128)S(1)} all-gather(f32[8,256]{1,0:T(8,128)S(1)} %add.76), channel_id=1, replica_groups=mesh['freq'=4,'tm'=8] {'tm'}, dimensions={1}, use_global_device_ids=true | all-gather | bytes 73728 | tf_op jit(solution)/shard_map/all_gather | solution.py:63
  372.8 136.1 %all-gather.2.cloned.1.call-done = bf16[8,2,2048,256]{3,2,1,0:T(8,128)(2,1)} async-done(((bf16[8,2,256,256]{3,2,1,0:T(8,128)(2,1)}), bf16[8,2,2048,256]{3,2,1,0:T(8,128)(2,1)}) %all-gather.2.cloned.1.call-update) | async-done | bytes 16777232 | tf_op jit(solution)/shard_map/all_gather | solution.py:59
  508.9 29.4 %fusion.16 = f32[8,512,4096]{2,1,0:T(8,128)} fusion(bf16[8,512,256]{2,1,0:T(8,128)(2,1)} %bitcast.29, bf16[8,4096,256]{2,1,0:T(8,128)(2,1)} %bitcast.30), kind=kOutput, calls=%fused_computation.34 | convolution fusion | flops 8589934592 | bytes 85983232 | tf_op jit(solution)/shard_map/dot_general | solution.py:39
  538.4 83.8 %reshape.195 = f32[8,2,256,2,2048]{4,3,2,1,0:T(2,128)} reshape(f32[8,512,4096]{2,1,0:T(8,128)} %fusion.16) | data formatting | bytes 134217728 | tf_op jit(solution)/shard_map/reshape | solution.py:42
  622.2 72.6 %fusion.14 = (f32[8,1,256,1,2048]{4,3,2,1,0:T(1,128)}, f32[8,1,256,1,2048]{4,3,2,1,0:T(1,128)}, f32[8,1,256,1,2048]{4,3,2,1,0:T(1,128)}, f32[8,1,256,1,2048]{4,3,2,1,0:T(1,128)}) fusion(f32[8,2,256,2,2048]{4,3,2,1,0:T(2,128)} %reshape.195), kind=kLoop, calls=%fused_computation.32 | loop fusion | bytes 134217728 | tf_op jit(solution)/shard_map/slice | solution.py:43
  694.8 45.3 %fusion.6 = (f32[1,8,256,2048]{3,2,1,0:T(8,128)}, f32[1,8,256,2048]{3,2,1,0:T(8,128)}) fusion(f32[8,1,256,1,2048]{4,3,2,1,0:T(1,128)} %get-tuple-element.8, f32[8,1,256,1,2048]{4,3,2,1,0:T(1,128)} %get-tuple-element.6, f32[8,1,256,1,2048]{4,3,2,1,0:T(1,128)} %get-tuple-element.7, f32[8,1,256,1,2048]{4,3,2,1,0:T(1,128)} %get-tuple-element.5), kind=kLoop, calls=%fused_computation.13 | loop fusion | flops 8388608 | bytes 100663296 | tf_op jit(solution)/shard_map/sub | solution.py:44
  740.1 18.8 %fusion.5 = bf16[2,8,256,2048]{3,2,1,0:T(8,128)(2,1)} fusion(f32[1,8,256,2048]{3,2,1,0:T(8,128)} %get-tuple-element.15, f32[1,8,256,2048]{3,2,1,0:T(8,128)} %get-tuple-element.16, f32[8,2048]{1,0:T(8,128)S(1)} %rsqrt.11, f32[8,256]{1,0:T(8,128)S(1)} %rsqrt_multiply_fusion), kind=kLoop, calls=%fused_computation.10 | loop fusion | flops 33554432 | bytes 50405376 | tf_op jit(solution)/shard_map/convert_element_type | solution.py:67
  (5 shorter events, 0.1 us)
Async XLA Ops:
  6.5 502.4 %all-gather.2.cloned.1.call-start = ((), (), s32[]{:S(2)}) async-start(), calls=%async_computation.1 | async-start | bytes 18874368 | tf_op jit(solution)/shard_map/all_gather | solution.py:59
  111.4 186.6 %copy-start = (bf16[2048,64]{0,1:T(8,128)(2,1)S(1)}, bf16[2048,64]{0,1:T(8,128)(2,1)}, u32[]{:S(2)}) copy-start(bf16[2048,64]{0,1:T(8,128)(2,1)} %convert_element_type.41) | copy-start | bytes 786436
Sparse Core Ops, SparseCore 0:
  358.0 150.9 all-gather.1
where the time goes:
time: 769 us; the launch traced here: 766 us
  local copies, waits for them, and re-layouts  262 us (34%)
  other arithmetic  252 us (33%)
  waiting for transfers between devices  136 us (18%)
  matrix products  57 us (7%)
  blocking collectives  44.7 us (6%)
  between operations  13.5 us (2%)
    convert_element_type x1, other arithmetic, filter_frames(): return frames.astype(jnp.bfloat16).reshape(inputs_here * S, P_SIZE)  187 us
    all_gather x1, waiting for transfers between devices, on_device(): all_spectra = lax.all_gather(own_spectra, 'tm', axis=2, tiled=True)  136 us
    reshape x1, local copies, waits for them, and re-layouts, filter_frames(): block.astype(jnp.float32).reshape(inputs_here, S + TAPS - 1, P_SIZE)  102 us
    reshape x1, local copies, waits for them, and re-layouts, correlate(): products = products.reshape(slab, 2, rows_here, 2, width)  83.8 us
    slice x1, local copies, waits for them, and re-layouts, correlate(): real_part = products[:, 0, :, 0] + products[:, 1, :, 1]  72.6 us
    sub x1, other arithmetic, correlate(): imag_part = products[:, 1, :, 0] - products[:, 0, :, 1]  45.3 us
    all_to_all x1, blocking collectives, on_device(): lax.all_to_all(spectra, 'freq', split_axis=0, concat_axis=2, tiled=True)  30.3 us
    dot_general x1, matrix products, correlate(): lax.dot_general(left_rows, right_rows, (((2,), (2,)), ((0,), (0,))), pref...  29.4 us
  transfers between devices with their start and end apart: 1, of which 1 were waited for; matrix products, arithmetic and copies ran while one was open for 0% of the time, Pallas kernels for 0%

commit v1 on v0

v1 whole, which is shorter than its diff:
```python
import functools
import math

import jax
import jax.numpy as jnp
from jax import lax
from jax.experimental import pallas as pl
from jax.experimental.pallas import tpu as pltpu
from jax.sharding import PartitionSpec as P

P_SIZE = 2048
TAPS = 4
FIRST_BIN = 512
CH_DEV = 8
S = 256
GROUP = 16
T_BLOCK = 37
CHUNK = 2


def folded_table(fir_taps, freq_count):
    channels = CH_DEV * freq_count
    points = jnp.arange(P_SIZE, dtype=jnp.int32)
    bins = FIRST_BIN + jnp.arange(channels, dtype=jnp.int32)
    phase = points[:, None] * bins[None, :] % P_SIZE
    angle = 2.0 * math.pi / P_SIZE * phase.astype(jnp.float32)
    twiddle = jnp.concatenate([jnp.cos(angle), -jnp.sin(angle)], axis=1)
    twiddle = twiddle.astype(jnp.bfloat16).astype(jnp.float32)
    folded = fir_taps.T[:, :, None] * twiddle[:, None, :]
    return folded.reshape(P_SIZE, TAPS * 2 * channels).astype(jnp.bfloat16)


def channelize_kernel(channels, x_ref, w_ref, o_ref, y_ref, u_ref, z_ref):
    step = pl.program_id(1)
    width = 2 * channels
    rows = jnp.concatenate(
        [x_ref[:, t * P_SIZE : (t + 1) * P_SIZE] for t in range(T_BLOCK)], axis=0
    )
    y = jnp.dot(rows, w_ref[...], preferred_element_type=jnp.float32)
    start = pl.multiple_of(step * T_BLOCK * GROUP, T_BLOCK * GROUP)
    y_ref[pl.ds(start, T_BLOCK * GROUP), :] = y

    @pl.when(step == pl.num_programs(1) - 1)
    def _():
        part = 32 * GROUP

        @pl.loop(0, S * GROUP // part)
        def _(i):
            base = i * part
            sums = {}
            for k in range(TAPS):
                lane, offset = k * width // 128 * 128, k * width % 128
                piece = y_ref[pl.ds(base + k * GROUP, part), lane : lane + max(width, 128)]
                sums[offset] = sums[offset] + piece if offset in sums else piece
            total = sums.pop(0)
            for offset, piece in sums.items():
                total = total + pltpu.roll(piece, 128 - offset, 1)
            u_ref[pl.ds(base, part), :] = total

        @pl.loop(0, GROUP)
        def _(a):
            spectra = u_ref[pl.ds(a, S, stride=GROUP), :].T
            real = spectra[:channels]
            imag = spectra[channels : 2 * channels]
            power = jnp.sum(real * real + imag * imag, axis=1, keepdims=True) / S + 1e-06
            scale = lax.rsqrt(power) * (1.0 / math.sqrt(S))
            for lane in range(0, S, 128):
                half = slice(lane, lane + 128)
                z_ref[lane // 128, pl.ds(a, channels, stride=GROUP), :] = real[:, half] * scale
                z_ref[(S + lane) // 128, pl.ds(a, channels, stride=GROUP), :] = imag[:, half] * scale

        for part in range(2 * S // 128):
            lanes = slice(part * 128, (part + 1) * 128)
            o_ref[:, :, lanes] = z_ref[part].astype(jnp.bfloat16).reshape(channels, GROUP, 128)


def channelize(voltages, table, freq_count):
    inputs_here, samples = voltages.shape
    channels = CH_DEV * freq_count
    columns = table.shape[1]
    groups = inputs_here // GROUP
    frames = samples // P_SIZE
    steps = frames // T_BLOCK
    return pl.pallas_call(
        functools.partial(channelize_kernel, channels),
        grid=(groups, steps),
        in_specs=[
            pl.BlockSpec((GROUP, T_BLOCK * P_SIZE), lambda g, t: (g, t)),
            pl.BlockSpec((P_SIZE, columns), lambda g, t: (0, 0)),
        ],
        out_specs=pl.BlockSpec((channels, GROUP, 2 * S), lambda g, t: (0, g, 0)),
        out_shape=jax.ShapeDtypeStruct((channels, inputs_here, 2 * S), jnp.bfloat16),
        scratch_shapes=[
            pltpu.VMEM((frames * GROUP, columns), jnp.float32),
            pltpu.VMEM((S * GROUP, max(128, 2 * channels)), jnp.float32),
            pltpu.VMEM((2 * S // 128, channels * GROUP, 128), jnp.float32),
        ],
        compiler_params=pltpu.CompilerParams(vmem_limit_bytes=48 * 1024 * 1024),
        cost_estimate=pl.CostEstimate(
            flops=2 * inputs_here * samples * columns,
            bytes_accessed=2 * inputs_here * samples,
            transcendentals=0,
        ),
        name="channelize",
    )(voltages, table)


def correlate(place, own, same, other, previous, first, total_columns):
    z_count, freq_count, chunk, block, depth = same.shape
    rows = freq_count * block
    slab = CH_DEV
    in_specs = [
        pl.BlockSpec((freq_count, None, block, depth), lambda c, p: (0, c, 0, 0)),
        pl.BlockSpec((z_count, freq_count, None, block, depth), lambda c, p: (0, 0, c, 0, 0)),
        pl.BlockSpec((z_count, freq_count, None, block, depth), lambda c, p: (0, 0, c, 0, 0)),
    ]
    args = [place, own, same, other]
    aliases = {}
    if previous is not None:
        in_specs.append(pl.BlockSpec(memory_space=pl.ANY))
        args.append(previous)
        aliases = {4: 0}

    def body(place_ref, own_ref, same_ref, other_ref, *rest):
        own = own_ref[...].reshape(rows, depth)
        core = place_ref[0]
        o_ref = rest[-1]
        turned = jnp.concatenate([own[:, S:], -own[:, :S]], axis=1)
        stacked = jnp.concatenate([own, turned], axis=0)
        for z in range(z_count):
            for source, parity in ((same_ref, core), (other_ref, 1 - core)):
                right = source[z].reshape(rows, depth)
                products = lax.dot_general(
                    stacked, right, (((1,), (1,)), ((), ())), preferred_element_type=jnp.float32
                ).astype(jnp.bfloat16)
                column = pl.multiple_of((2 * z + parity) * rows, rows)
                o_ref[0, 0, :, pl.ds(column, rows)] = products[:rows]
                o_ref[1, 0, :, pl.ds(column, rows)] = products[rows:]

    return pl.pallas_call(
        body,
        grid_spec=pltpu.PrefetchScalarGridSpec(
            num_scalar_prefetch=1,
            grid=(chunk,),
            in_specs=in_specs,
            out_specs=pl.BlockSpec(
                (2, 1, rows, total_columns), lambda c, p: (0, first + c, 0, 0)
            ),
        ),
        out_shape=jax.ShapeDtypeStruct((2, slab, rows, total_columns), jnp.bfloat16),
        input_output_aliases=aliases,
        compiler_params=pltpu.CompilerParams(vmem_limit_bytes=32 * 1024 * 1024),
        cost_estimate=pl.CostEstimate(
            flops=2 * chunk * 2 * rows * total_columns * depth,
            bytes_accessed=chunk * 2 * total_columns * (depth + 2 * rows),
            transcendentals=0,
        ),
        name="correlate",
    )(*args)


def on_device(voltages, fir_taps):
    freq_count = lax.axis_size("freq")
    tm_count = lax.axis_size("tm")
    inputs_here = voltages.shape[0]
    total_columns = inputs_here * freq_count * tm_count
    core = lax.axis_index("tm") % 2
    place = core.astype(jnp.int32).reshape(1)
    same_core = [list(range(c, tm_count, 2)) for c in range(2)]
    swap = [(i, i ^ 1) for i in range(tm_count)]

    table = folded_table(fir_taps, freq_count)
    spectra = channelize(voltages, table, freq_count)
    spectra = spectra.reshape(freq_count, CH_DEV, inputs_here, 2 * S)
    result = None
    for first in range(0, CH_DEV, CHUNK):
        piece = spectra[:, first : first + CHUNK]
        own = lax.all_to_all(piece, "freq", split_axis=0, concat_axis=0, tiled=True)
        same = lax.all_gather(own, "tm", axis=0, axis_index_groups=same_core)
        other = lax.ppermute(same, "tm", swap)
        result = correlate(place, own, same, other, result, first, total_columns)
    return result


def solution(mesh):
    placed = (P(("tm", "freq"), None), P())
    return jax.shard_map(
        on_device,
        mesh=mesh,
        in_specs=placed,
        out_specs=P(None, "freq", "tm", None),
        check_vma=False,
    )
```

time: 769 us -> 295 us (0.38)
  local copies, waits for them, and re-layouts: 262 us -> 2.32 us
  other arithmetic: 252 us -> 2.18 us
  Pallas kernels: 0 us -> 78.6 us
  matrix products: 57 us -> 0 us
  waiting for transfers between devices: 136 us -> 153 us
    convert_element_type x2, other arithmetic: 205 us -> 0.96 us  [the longest x1 0.92 us: folded_table(): return folded.reshape(P_SIZE, TAPS * 2 * channels).astype(jnp.bfloat16)]
    reshape x2 -> x0, local copies, waits for them, and re-layouts: 185 us -> none  [the longest x1 102 us: filter_frames(): block.astype(jnp.float32).reshape(inputs_here, S + TAPS - 1, P_SIZE)]
    pallas_call x0 -> x5, Pallas kernels: none -> 78.6 us  [the longest x1 56.4 us: channelize(): pl.pallas_call(functools.partial(channelize_kernel, channels), grid=(grou...]
    slice x2 -> x1, local copies, waits for them, and re-layouts: 73.5 us -> 0.19 us  [on_device(): piece = spectra[:, first:first + CHUNK]]
    dot_general x2 -> x0, matrix products: 57 us -> none  [the longest x1 29.4 us: correlate(): lax.dot_general(left_rows, right_rows, (((2,), (2,)), ((0,), (0,))), pref...]
    sub x1 -> x0, other arithmetic: 45.3 us -> none  [correlate(): imag_part = products[:, 1, :, 0] - products[:, 0, :, 1]]
    all_gather x1 -> x4, waiting for transfers between devices: 136 us -> 153 us  [on_device(): same = lax.all_gather(own, 'tm', axis=0, axis_index_groups=same_core)]
    all_gather x1 -> x0, blocking collectives: 14.4 us -> none  [on_device(): powers_all = lax.all_gather(powers, 'tm', axis=1, tiled=True)]
  transfers between devices with their start and end apart: 1 -> 8, of which waited for: 1 -> 4; matrix products, arithmetic and copies ran while one was open for 0% -> 0% of each run, Pallas kernels for 0% -> 6%
where the time goes in v1:
time: 295 us; the launch traced here: 294 us
  waiting for transfers between devices  153 us (52%)
  Pallas kernels  78.6 us (27%)
  blocking collectives  44.5 us (15%)
  between operations  13.2 us (4%)
    all_gather x4, waiting for transfers between devices, on_device(): same = lax.all_gather(own, 'tm', axis=0, axis_index_groups=same_core)  153 us
    pallas_call x1, Pallas kernels, channelize(): pl.pallas_call(functools.partial(channelize_kernel, channels), grid=(grou...  56.4 us
    all_to_all x4, blocking collectives, on_device(): own = lax.all_to_all(piece, 'freq', split_axis=0, concat_axis=0, tiled=True)  44.5 us
    pallas_call x4, Pallas kernels, correlate(): pl.pallas_call(body, grid_spec=pltpu.PrefetchScalarGridSpec(num_scalar_pr...  22.2 us
  transfers between devices with their start and end apart: 8, of which 4 were waited for; matrix products, arithmetic and copies ran while one was open for 0% of the time, Pallas kernels for 6%

profile of v1, /device:TPU:0, one launch (start us, length us, event | category | flops | bytes accessed | tf_op | source)
XLA Modules:
  0.0 294.4 jit_solution(3176474864200380106)
XLA Ops:
  6.5 1.2 cosine_convert_fusion
  7.8 0.9 multiply_convert_fusion
  8.7 0.5 copy.8.w_ref
  9.3 56.4 %channelize.1 = bf16[32,64,512]{2,1,0:T(8,128)(2,1)S(1)} custom-call(bf16[64,530432]{1,0:T(8,128)(2,1)} %x_ref.1, bf16[2048,256]{1,0:T(8,128)(2,1)S(1)} %copy.8.w_ref), custom_call_target="tpu_custom_call" | custom-call | flops 17381195776 | bytes 67895296 | tf_op jit(solution)/shard_map/channelize/pallas_call | solution.py:84
  65.7 0.2 fusion.6
  65.9 13.6 %all_to_all.20.own_ref = bf16[4,2,64,512]{3,2,1,0:T(8,128)(2,1)} all-to-all(bf16[4,2,64,512]{3,2,1,0:T(8,128)(2,1)S(1)} %get-tuple-element.5), channel_id=1, replica_groups=mesh['freq'=4,'tm'=8] {'freq'}, dimensions={0} | all-to-all | bytes 1048576 | tf_op jit(solution)/shard_map/all_to_all | solution.py:178
  79.5 0.0 all-gather.15.cloned.1.call-update
  79.5 0.0 all-gather.13.cloned.1.call-start
  79.6 10.3 %all_to_all.21.own_ref = bf16[4,2,64,512]{3,2,1,0:T(8,128)(2,1)} all-to-all(bf16[4,2,64,512]{3,2,1,0:T(8,128)(2,1)S(1)} %get-tuple-element.6), channel_id=1, replica_groups=mesh['freq'=4,'tm'=8] {'freq'}, dimensions={0} | all-to-all | bytes 1048576 | tf_op jit(solution)/shard_map/all_to_all | solution.py:178
  89.9 0.0 all-gather.13.cloned.1.call-update
  89.9 0.0 all-gather.11.cloned.1.call-start
  90.0 10.4 %all_to_all.22.own_ref = bf16[4,2,64,512]{3,2,1,0:T(8,128)(2,1)} all-to-all(bf16[4,2,64,512]{3,2,1,0:T(8,128)(2,1)S(1)} %get-tuple-element.7), channel_id=1, replica_groups=mesh['freq'=4,'tm'=8] {'freq'}, dimensions={0} | all-to-all | bytes 1048576 | tf_op jit(solution)/shard_map/all_to_all | solution.py:178
  100.3 0.0 all-gather.11.cloned.1.call-update
  100.4 0.0 all-gather.9.cloned.1.call-start
  100.4 10.2 %all_to_all.23.own_ref = bf16[4,2,64,512]{3,2,1,0:T(8,128)(2,1)} all-to-all(bf16[4,2,64,512]{3,2,1,0:T(8,128)(2,1)S(1)} %get-tuple-element.8), channel_id=1, replica_groups=mesh['freq'=4,'tm'=8] {'freq'}, dimensions={0} | all-to-all | bytes 1048576 | tf_op jit(solution)/shard_map/all_to_all | solution.py:178
  110.6 0.0 all-gather.9.cloned.1.call-update
  110.7 14.7 %all-gather.15.cloned.1.call-done = bf16[16,2,64,512]{3,2,1,0:T(8,128)(2,1)} async-done(((bf16[4,2,64,512]{3,2,1,0:T(8,128)(2,1)}), bf16[16,2,64,512]{3,2,1,0:T(8,128)(2,1)}) %all-gather.15.cloned.1.call-update) | async-done | bytes 2097168 | tf_op jit(solution)/shard_map/all_gather | solution.py:179
  125.3 0.0 collective-permute-start.3
  125.3 46.3 %all-gather.13.cloned.1.call-done = bf16[16,2,64,512]{3,2,1,0:T(8,128)(2,1)} async-done(((bf16[4,2,64,512]{3,2,1,0:T(8,128)(2,1)}), bf16[16,2,64,512]{3,2,1,0:T(8,128)(2,1)}) %all-gather.13.cloned.1.call-update) | async-done | bytes 2097168 | tf_op jit(solution)/shard_map/all_gather | solution.py:179
  171.6 0.0 collective-permute-start.2
  171.6 46.3 %all-gather.11.cloned.1.call-done = bf16[16,2,64,512]{3,2,1,0:T(8,128)(2,1)} async-done(((bf16[4,2,64,512]{3,2,1,0:T(8,128)(2,1)}), bf16[16,2,64,512]{3,2,1,0:T(8,128)(2,1)}) %all-gather.11.cloned.1.call-update) | async-done | bytes 2097168 | tf_op jit(solution)/shard_map/all_gather | solution.py:179
  217.9 0.0 collective-permute-start.1
  217.9 46.1 %all-gather.9.cloned.1.call-done = bf16[16,2,64,512]{3,2,1,0:T(8,128)(2,1)} async-done(((bf16[4,2,64,512]{3,2,1,0:T(8,128)(2,1)}), bf16[16,2,64,512]{3,2,1,0:T(8,128)(2,1)}) %all-gather.9.cloned.1.call-update) | async-done | bytes 2097168 | tf_op jit(solution)/shard_map/all_gather | solution.py:179
  264.0 0.0 collective-permute-start
  264.0 0.0 collective-permute-done.3.other_ref
  264.0 1.6 copy-done.4
  265.6 5.8 %correlate.4.rest_0_ = bf16[2,8,256,2048]{3,2,1,0:T(8,128)(2,1)} custom-call(s32[1]{0:T(128)} %bitcast.place_ref, bf16[4,2,64,512]{3,2,1,0:T(8,128)(2,1)S(1)} %copy-done.3, bf16[4,4,2,64,512]{4,3,2,1,0:T(8,128)(2,1)S(1)} %bitcast.10, bf16[4,4,2,64,512]{4,3,2,1,0:T(8,128)(2,1)} %collective-permute-done.3.other_ref), custom_call_target="tpu_custom_call" | custom-call | flops 2147483648 | bytes 8388608 | tf_op jit(solution)/shard_map/correlate/pallas_call | solution.py:140
  271.4 0.0 collective-permute-done.2.other_ref
  271.4 5.9 %correlate.5.rest_0_ = bf16[2,8,256,2048]{3,2,1,0:T(8,128)(2,1)} custom-call(s32[1]{0:T(128)} %bitcast.place_ref, bf16[4,2,64,512]{3,2,1,0:T(8,128)(2,1)S(1)} %copy-done, bf16[4,4,2,64,512]{4,3,2,1,0:T(8,128)(2,1)S(1)} %bitcast.12, bf16[4,4,2,64,512]{4,3,2,1,0:T(8,128)(2,1)} %collective-permute-done.2.other_ref, ...), custom_call_target="tpu_custom_call", output_to_operand_aliasing={{}: (4, {})} | custom-call | flops 2147483648 | bytes 8388608 | tf_op jit(solution)/shard_map/correlate/pallas_call | solution.py:140
  277.3 5.9 %correlate.6.rest_0_ = bf16[2,8,256,2048]{3,2,1,0:T(8,128)(2,1)} custom-call(s32[1]{0:T(128)} %bitcast.place_ref, bf16[4,2,64,512]{3,2,1,0:T(8,128)(2,1)S(1)} %copy-done.1, bf16[4,4,2,64,512]{4,3,2,1,0:T(8,128)(2,1)S(1)} %bitcast.14, bf16[4,4,2,64,512]{4,3,2,1,0:T(8,128)(2,1)} %collective-permute-done.1.other_ref, ...), custom_call_target="tpu_custom_call", output_to_operand_aliasing={{}: (4, {})} | custom-call | flops 2147483648 | bytes 8388608 | tf_op jit(solution)/shard_map/correlate/pallas_call | solution.py:140
  283.2 0.0 collective-permute-done.other_ref
  283.2 4.6 %correlate.7 = bf16[2,8,256,2048]{3,2,1,0:T(8,128)(2,1)} custom-call(s32[1]{0:T(128)} %bitcast.place_ref, bf16[4,2,64,512]{3,2,1,0:T(8,128)(2,1)S(1)} %copy-done.2, bf16[4,4,2,64,512]{4,3,2,1,0:T(8,128)(2,1)S(1)} %bitcast.16, bf16[4,4,2,64,512]{4,3,2,1,0:T(8,128)(2,1)S(1)} %collective-permute-done.other_ref, ...), custom_call_target="tpu_custom_call", output_to_operand_aliasing={{}: (4, {})} | custom-call | flops 2147483648 | bytes 8388608 | tf_op jit(solution)/shard_map/correlate/pallas_call | solution.py:140
  (19 shorter events, 0.1 us)
Async XLA Ops:
  6.5 118.8 %all-gather.15.cloned.1.call-start = ((), (), s32[]{:S(2)}) async-start(), calls=%async_computation.7 | async-start | bytes 2621440 | tf_op jit(solution)/shard_map/all_gather | solution.py:179
  79.5 92.1 %all-gather.13.cloned.1.call-start = ((), (), s32[]{:S(2)}) async-start(), calls=%async_computation.6 | async-start | bytes 2621440 | tf_op jit(solution)/shard_map/all_gather | solution.py:179
  89.9 174.1 %copy-start.3 = (bf16[4,2,64,512]{3,2,1,0:T(8,128)(2,1)S(1)}, bf16[4,2,64,512]{3,2,1,0:T(8,128)(2,1)}, u32[]{:S(2)}) copy-start(bf16[4,2,64,512]{3,2,1,0:T(8,128)(2,1)} %all_to_all.20.own_ref) | copy-start | bytes 1572868
  89.9 127.9 %all-gather.11.cloned.1.call-start = ((), (), s32[]{:S(2)}) async-start(), calls=%async_computation.5 | async-start | bytes 2621440 | tf_op jit(solution)/shard_map/all_gather | solution.py:179
  100.4 163.6 %all-gather.9.cloned.1.call-start = ((), (), s32[]{:S(2)}) async-start(), calls=%async_computation.4 | async-start | bytes 2621440 | tf_op jit(solution)/shard_map/all_gather | solution.py:179
  125.3 138.7 %collective-permute-start.3 = (bf16[4,4,2,64,512]{4,3,2,1,0:T(8,128)(2,1)}, bf16[4,4,2,64,512]{4,3,2,1,0:T(8,128)(2,1)}, u32[]{:S(2)}, u32[]{:S(2)}) collective-permute-start(bf16[4,4,2,64,512]{4,3,2,1,0:T(8,128)(2,1)} %bitcast.9), channel_id=1, source_target_pairs={{0,1},{1,0},{2,3},{3,2},{4,5},{5,4},{6,7},{7,6},{8,9},{9,8},{10,11... | collective-permute-start | bytes 6291464 | tf_op jit(solution)/shard_map/ppermute | solution.py:180
  171.6 99.8 %collective-permute-start.2 = (bf16[4,4,2,64,512]{4,3,2,1,0:T(8,128)(2,1)}, bf16[4,4,2,64,512]{4,3,2,1,0:T(8,128)(2,1)}, u32[]{:S(2)}, u32[]{:S(2)}) collective-permute-start(bf16[4,4,2,64,512]{4,3,2,1,0:T(8,128)(2,1)} %bitcast.11), channel_id=1, source_target_pairs={{0,1},{1,0},{2,3},{3,2},{4,5},{5,4},{6,7},{7,6},{8,9},{9,8},{10,11... | collective-permute-start | bytes 6291464 | tf_op jit(solution)/shard_map/ppermute | solution.py:180
  217.9 59.4 %collective-permute-start.1 = (bf16[4,4,2,64,512]{4,3,2,1,0:T(8,128)(2,1)}, bf16[4,4,2,64,512]{4,3,2,1,0:T(8,128)(2,1)}, u32[]{:S(2)}, u32[]{:S(2)}) collective-permute-start(bf16[4,4,2,64,512]{4,3,2,1,0:T(8,128)(2,1)} %bitcast.13), channel_id=1, source_target_pairs={{0,1},{1,0},{2,3},{3,2},{4,5},{5,4},{6,7},{7,6},{8,9},{9,8},{10,11... | collective-permute-start | bytes 6291464 | tf_op jit(solution)/shard_map/ppermute | solution.py:180
  264.0 19.2 %collective-permute-start = (bf16[4,4,2,64,512]{4,3,2,1,0:T(8,128)(2,1)}, bf16[4,4,2,64,512]{4,3,2,1,0:T(8,128)(2,1)S(1)}, u32[]{:S(2)}, u32[]{:S(2)}) collective-permute-start(bf16[4,4,2,64,512]{4,3,2,1,0:T(8,128)(2,1)} %bitcast.15), channel_id=1, source_target_pairs={{0,1},{1,0},{2,3},{3,2},{4,5},{5,4},{6,7},{7,6},{8,9},{9,8},{10,11... | collective-permute-start | bytes 6291464 | tf_op jit(solution)/shard_map/ppermute | solution.py:180
  264.0 1.6 copy-start.4
  265.6 5.8 %copy-start = (bf16[4,2,64,512]{3,2,1,0:T(8,128)(2,1)S(1)}, bf16[4,2,64,512]{3,2,1,0:T(8,128)(2,1)}, u32[]{:S(2)}) copy-start(bf16[4,2,64,512]{3,2,1,0:T(8,128)(2,1)} %all_to_all.21.own_ref) | copy-start | bytes 1572868
  265.6 5.8 %copy-start.5 = (bf16[16,2,64,512]{3,2,1,0:T(8,128)(2,1)S(1)}, bf16[16,2,64,512]{3,2,1,0:T(8,128)(2,1)}, u32[]{:S(2)}) copy-start(bf16[16,2,64,512]{3,2,1,0:T(8,128)(2,1)} %all-gather.13.cloned.1.call-done) | copy-start | bytes 6291460
  271.4 5.9 %copy-start.1 = (bf16[4,2,64,512]{3,2,1,0:T(8,128)(2,1)S(1)}, bf16[4,2,64,512]{3,2,1,0:T(8,128)(2,1)}, u32[]{:S(2)}) copy-start(bf16[4,2,64,512]{3,2,1,0:T(8,128)(2,1)} %all_to_all.22.own_ref) | copy-start | bytes 1572868
  271.4 5.9 %copy-start.6 = (bf16[16,2,64,512]{3,2,1,0:T(8,128)(2,1)S(1)}, bf16[16,2,64,512]{3,2,1,0:T(8,128)(2,1)}, u32[]{:S(2)}) copy-start(bf16[16,2,64,512]{3,2,1,0:T(8,128)(2,1)} %all-gather.11.cloned.1.call-done) | copy-start | bytes 6291460
  277.3 5.9 %copy-start.2 = (bf16[4,2,64,512]{3,2,1,0:T(8,128)(2,1)S(1)}, bf16[4,2,64,512]{3,2,1,0:T(8,128)(2,1)}, u32[]{:S(2)}) copy-start(bf16[4,2,64,512]{3,2,1,0:T(8,128)(2,1)} %all_to_all.23.own_ref) | copy-start | bytes 1572868
  277.3 5.9 %copy-start.7 = (bf16[16,2,64,512]{3,2,1,0:T(8,128)(2,1)S(1)}, bf16[16,2,64,512]{3,2,1,0:T(8,128)(2,1)}, u32[]{:S(2)}) copy-start(bf16[16,2,64,512]{3,2,1,0:T(8,128)(2,1)} %all-gather.9.cloned.1.call-done) | copy-start | bytes 6291460
Sparse Core Ops, SparseCore 0:
  79.7 45.6 all-gather.14
  126.9 44.6 all-gather.12
  173.2 44.6 all-gather.10
  219.3 44.6 all-gather.8

commit v2 on v0

v2 whole, which is shorter than its diff:
```python
import functools
import math

import jax
import jax.numpy as jnp
from jax import lax
from jax.experimental import pallas as pl
from jax.experimental.pallas import tpu as pltpu
from jax.sharding import PartitionSpec as P

P_SIZE = 2048
TAPS = 4
FIRST_BIN = 512
CH_DEV = 8
S = 256
GROUP = 16
T_BLOCK = 37
T_PARTS = (13, 12, 12)
LANES = 128


def folded_table(fir_taps, freq_count):
    slabs = jnp.arange(freq_count, dtype=jnp.int32) ^ lax.axis_index("freq").astype(jnp.int32)
    channel = slabs[:, None] * CH_DEV + jnp.arange(CH_DEV, dtype=jnp.int32)[None, :]
    bins = FIRST_BIN + channel.reshape(-1)
    points = jnp.arange(P_SIZE, dtype=jnp.int32)
    phase = points[:, None] * bins[None, :] % P_SIZE
    angle = 2.0 * math.pi / P_SIZE * phase.astype(jnp.float32)
    twiddle = jnp.concatenate([jnp.cos(angle), -jnp.sin(angle)], axis=1)
    twiddle = twiddle.astype(jnp.bfloat16).astype(jnp.float32)
    folded = fir_taps.T[:, :, None] * twiddle[:, None, :]
    return folded.reshape(P_SIZE, -1).astype(jnp.bfloat16)


def channelize_kernel(channels, x_ref, w_ref, after_ref, o_ref, y_ref, u_ref, s_ref, z_ref):
    step = pl.program_id(0)
    width = 2 * channels
    halves = LANES // width
    depth = S // halves
    table = w_ref[...]
    done = 0
    for count in T_PARTS:
        rows = jnp.concatenate(
            [x_ref[:, t * P_SIZE : (t + 1) * P_SIZE] for t in range(done, done + count)], axis=0
        )
        start = pl.multiple_of((step * T_BLOCK + done) * GROUP, GROUP)
        y_ref[pl.ds(start, count * GROUP), :] = jnp.dot(
            rows, table, preferred_element_type=jnp.float32
        )
        done += count

    @pl.when(step == pl.num_programs(0) - 1)
    def _():
        part = 8

        def taps_sum(s, count):
            if halves == 1:
                total = y_ref[pl.ds(s * GROUP, count * GROUP), :LANES]
                for k in range(1, TAPS):
                    lanes = slice(k * LANES, (k + 1) * LANES)
                    total = total + y_ref[pl.ds((s + k) * GROUP, count * GROUP), lanes]
                return total
            low = y_ref[pl.ds(s * GROUP, count * GROUP), :LANES]
            return low + y_ref[pl.ds((s + 2) * GROUP, count * GROUP), LANES:]

        def combine(i, power):
            s = i * part
            size = part * GROUP
            if halves == 1:
                both = taps_sum(s, part)
            else:
                first = taps_sum(s, part + 1)
                second = taps_sum(s + depth, part + 1)
                lane = lax.broadcasted_iota(jnp.int32, (size, LANES), 1)
                low = first[:size] + pltpu.roll(first[GROUP:], width, 1)
                high = pltpu.roll(second[:size], width, 1) + second[GROUP:]
                both = jnp.where(lane < width, low, high)
            u_ref[pl.ds(pl.multiple_of(s * GROUP, size), size), :] = both
            return power + jnp.sum((both * both).reshape(part, GROUP, LANES), axis=0)

        power = lax.fori_loop(
            0, depth // part, combine, jnp.zeros((GROUP, LANES), jnp.float32)
        )
        shift = channels
        while shift < LANES:
            power = power + pltpu.roll(power, shift, 1)
            shift *= 2
        s_ref[...] = lax.rsqrt(power / S + 1e-06) * (1.0 / math.sqrt(S))

        per_half = depth // LANES
        for a in range(GROUP):
            spectra = (u_ref[pl.ds(a, depth, stride=GROUP), :] * s_ref[a : a + 1, :]).T
            for h in range(halves):
                for r in range(2):
                    first = (2 * h + r) * channels
                    for j in range(per_half):
                        z_ref[
                            r * (S // LANES) + h * per_half + j,
                            pl.ds(a, channels, stride=GROUP),
                            :,
                        ] = spectra[first : first + channels, j * LANES : (j + 1) * LANES]
        for part in range(2 * S // LANES):
            lanes = slice(part * LANES, (part + 1) * LANES)
            o_ref[:, :, lanes] = z_ref[part].astype(jnp.bfloat16).reshape(channels, GROUP, LANES)


def channelize(voltages, table, after, group):
    samples = voltages.shape[1]
    columns = table.shape[1]
    channels = columns // (2 * TAPS)
    frames = samples // P_SIZE
    return pl.pallas_call(
        functools.partial(channelize_kernel, channels),
        grid=(frames // T_BLOCK,),
        in_specs=[
            pl.BlockSpec((GROUP, T_BLOCK * P_SIZE), lambda t: (group, t)),
            pl.BlockSpec((P_SIZE, columns), lambda t: (0, 0)),
            pl.BlockSpec(memory_space=pl.ANY),
        ],
        out_specs=pl.BlockSpec((channels, GROUP, 2 * S), lambda t: (0, 0, 0)),
        out_shape=jax.ShapeDtypeStruct((channels, GROUP, 2 * S), jnp.bfloat16),
        scratch_shapes=[
            pltpu.VMEM((frames * GROUP, columns), jnp.float32),
            pltpu.VMEM((S * 2 * channels // LANES * GROUP, LANES), jnp.float32),
            pltpu.VMEM((GROUP, LANES), jnp.float32),
            pltpu.VMEM((2 * S // LANES, channels * GROUP, LANES), jnp.float32),
        ],
        compiler_params=pltpu.CompilerParams(vmem_limit_bytes=40 * 1024 * 1024),
        cost_estimate=pl.CostEstimate(
            flops=2 * GROUP * samples * columns,
            bytes_accessed=2 * GROUP * samples,
            transcendentals=0,
        ),
        name="channelize",
    )(voltages, table, after)


def correlate_kernel(groups, place_ref, *refs):
    o_ref, token_ref = refs[-2:]
    token_ref[...] = jnp.zeros_like(token_ref)
    own, same, other = (refs[i * groups : (i + 1) * groups] for i in range(3))
    freq_count = own[0].shape[0]
    freq, core = place_ref[0], place_ref[1]
    rows = freq_count * groups * GROUP

    def inputs_of(sources):
        return jnp.concatenate(
            [source[f ^ freq] for f in range(freq_count) for source in sources], axis=0
        )

    left = inputs_of(own)
    turned = jnp.concatenate([left[:, S:], -left[:, :S]], axis=1)
    stacked = jnp.concatenate([left, turned], axis=0)
    for sources, parity in ((same, core), (other, 1 - core)):
        products = lax.dot_general(
            stacked,
            inputs_of(sources),
            (((1,), (1,)), ((), ())),
            preferred_element_type=jnp.float32,
        ).astype(jnp.bfloat16)
        column = pl.multiple_of(parity * rows, rows)
        o_ref[0, :, pl.ds(column, rows)] = products[:rows]
        o_ref[1, :, pl.ds(column, rows)] = products[rows:]


def correlate(place, own, same, other, previous, total_columns):
    groups = len(own)
    freq_count, slab, block, depth = own[0].shape
    rows = freq_count * groups * block
    piece = pl.BlockSpec((freq_count, None, block, depth), lambda c, p: (0, c, 0, 0))
    in_specs = [piece] * (3 * groups)
    args = [place, *own, *same, *other]
    aliases = {}
    if previous is not None:
        aliases = {len(args): 0}
        in_specs.append(pl.BlockSpec(memory_space=pl.ANY))
        args.append(previous)
    return pl.pallas_call(
        functools.partial(correlate_kernel, groups),
        grid_spec=pltpu.PrefetchScalarGridSpec(
            num_scalar_prefetch=1,
            grid=(slab,),
            in_specs=in_specs,
            out_specs=[
                pl.BlockSpec((2, None, rows, 2 * rows), lambda c, p: (0, c, 0, p[2])),
                pl.BlockSpec((8, LANES), lambda c, p: (0, 0)),
            ],
        ),
        out_shape=[
            jax.ShapeDtypeStruct((2, slab, rows, total_columns), jnp.bfloat16),
            jax.ShapeDtypeStruct((8, LANES), jnp.float32),
        ],
        input_output_aliases=aliases,
        compiler_params=pltpu.CompilerParams(vmem_limit_bytes=32 * 1024 * 1024),
        cost_estimate=pl.CostEstimate(
            flops=2 * slab * 2 * rows * 2 * rows * depth,
            bytes_accessed=slab * 2 * rows * (3 * depth + 4 * rows),
            transcendentals=0,
        ),
        name="correlate",
    )(*args)


def on_device(voltages, fir_taps):
    freq_count = lax.axis_size("freq")
    tm_count = lax.axis_size("tm")
    inputs_here = voltages.shape[0]
    total_columns = inputs_here * freq_count * tm_count
    groups = inputs_here // GROUP
    ring = tm_count // 2
    tm = lax.axis_index("tm").astype(jnp.int32)
    freq = lax.axis_index("freq").astype(jnp.int32)
    swap = [(i, i ^ 1) for i in range(tm_count)]
    onward = [(i, (i + 2) % tm_count) for i in range(tm_count)]

    table = folded_table(fir_taps, freq_count)
    token = jnp.zeros((8, LANES), jnp.float32)
    held = [[None] * groups for _ in range(ring)]

    def after(token, *arrays):
        return lax.optimization_barrier((token, *arrays))

    def move_on(step, group, token=None):
        piece = held[step - 1][group]
        if token is not None:
            piece, _ = lax.optimization_barrier((piece, token))
        held[step][group] = lax.ppermute(piece, "tm", onward)

    for group in range(groups):
        if group == 2:
            token, held[0][0] = after(token, held[0][0])
        elif group >= 3:
            if held[1][group - 3] is None:
                move_on(1, group - 3)
            token, held[0][group - 2], held[0][group - 1], held[1][group - 3] = after(
                token, held[0][group - 2], held[0][group - 1], held[1][group - 3]
            )
        spectra = channelize(voltages, table, token, group)
        token, spectra = after(token, spectra)
        if group == groups - 1 and groups >= 4 and ring >= 3:
            move_on(1, group - 2)
            move_on(2, group - 3)
            spectra, held[1][group - 2], held[2][group - 3] = lax.optimization_barrier(
                (spectra, held[1][group - 2], held[2][group - 3])
            )
        spectra = spectra.reshape(freq_count, CH_DEV, GROUP, 2 * S)
        parts = [spectra[0]]
        for k in range(1, freq_count):
            partners = [(i, i ^ k) for i in range(freq_count)]
            parts.append(lax.ppermute(spectra[k], "freq", partners))
        held[0][group] = jnp.stack(parts)

    result, tokens = None, []
    for step in range(ring):
        for group in range(groups):
            if held[step][group] is None:
                late = step >= 2 and group >= groups // 2
                move_on(step, group, tokens[step - 2] if late else None)
        other = []
        for group in range(groups):
            piece = held[step][group]
            if step == ring - 1 and step >= 1 and group >= groups // 2:
                piece, _ = lax.optimization_barrier((piece, tokens[step - 1]))
            other.append(lax.ppermute(piece, "tm", swap))
        source = (tm // 2 + ring - step) % ring
        place = jnp.stack([freq, tm % 2, source])
        result, token = correlate(place, held[0], held[step], other, result, total_columns)
        tokens.append(token)
    return result


def solution(mesh):
    placed = (P(("tm", "freq"), None), P())
    return jax.shard_map(
        on_device,
        mesh=mesh,
        in_specs=placed,
        out_specs=P(None, "freq", "tm", None),
        check_vma=False,
    )
```

time: 769 us -> 209 us (0.27)
  local copies, waits for them, and re-layouts: 262 us -> 3.64 us
  other arithmetic: 252 us -> 2.68 us
  Pallas kernels: 0 us -> 80.4 us
  matrix products: 57 us -> 0 us
  blocking collectives: 44.7 us -> 0 us
  waiting for transfers between devices: 136 us -> 95.2 us
  starting transfers between devices: 0.01 us -> 25.6 us
  between operations: 13.5 us -> 0.26 us
    convert_element_type x2, other arithmetic: 205 us -> 0.96 us  [the longest x1 0.92 us: folded_table(): return folded.reshape(P_SIZE, -1).astype(jnp.bfloat16)]
    reshape x2 -> x0, local copies, waits for them, and re-layouts: 185 us -> none  [the longest x1 102 us: filter_frames(): block.astype(jnp.float32).reshape(inputs_here, S + TAPS - 1, P_SIZE)]
    all_gather x1 -> x0, waiting for transfers between devices: 136 us -> none  [on_device(): all_spectra = lax.all_gather(own_spectra, 'tm', axis=2, tiled=True)]
    ppermute x0 -> x40, waiting for transfers between devices: none -> 95.2 us  [the longest x12 83.9 us: move_on(): held[step][group] = lax.ppermute(piece, 'tm', onward)]
    pallas_call x0 -> x8, Pallas kernels: none -> 80.4 us  [the longest x4 50.3 us: channelize(): pl.pallas_call(functools.partial(channelize_kernel, channels), grid=(fram...]
    slice x2 -> x4, local copies, waits for them, and re-layouts: 73.5 us -> 0.15 us  [on_device(): parts = [spectra[0]]]
    dot_general x2 -> x0, matrix products: 57 us -> none  [the longest x1 29.4 us: correlate(): lax.dot_general(left_rows, right_rows, (((2,), (2,)), ((0,), (0,))), pref...]
    sub x1 -> x0, other arithmetic: 45.3 us -> none  [correlate(): imag_part = products[:, 1, :, 0] - products[:, 0, :, 1]]
  transfers between devices with their start and end apart: 1 -> 40, of which waited for: 1 -> 19; matrix products, arithmetic and copies ran while one was open for 0% -> 0% of each run, Pallas kernels for 0% -> 29%
where the time goes in v2:
time: 209 us; the launch traced here: 208 us
  waiting for transfers between devices  95.2 us (46%)
  Pallas kernels  80.4 us (38%)
  starting transfers between devices  25.6 us (12%)
  local copies, waits for them, and re-layouts  3.64 us (2%)
  other arithmetic  2.68 us (1%)
    ppermute x12, waiting for transfers between devices, move_on(): held[step][group] = lax.ppermute(piece, 'tm', onward)  83.9 us
    pallas_call x4, Pallas kernels, channelize(): pl.pallas_call(functools.partial(channelize_kernel, channels), grid=(fram...  50.3 us
    pallas_call x4, Pallas kernels, correlate(): pl.pallas_call(functools.partial(correlate_kernel, groups), grid_spec=plt...  30.1 us
    ppermute x12, starting transfers between devices, on_device(): parts.append(lax.ppermute(spectra[k], 'freq', partners))  15.2 us
    ppermute x12, starting transfers between devices, move_on(): held[step][group] = lax.ppermute(piece, 'tm', onward)  8.72 us
    ppermute x12, waiting for transfers between devices, on_device(): parts.append(lax.ppermute(spectra[k], 'freq', partners))  8.28 us
  transfers between devices with their start and end apart: 40, of which 19 were waited for; matrix products, arithmetic and copies ran while one was open for 0% of the time, Pallas kernels for 29%

profile of v2, /device:TPU:0, one launch (start us, length us, event | category | flops | bytes accessed | tf_op | source)
XLA Modules:
  0.0 207.8 jit_solution(12576007541396537244)
XLA Ops:
  2.9 12.6 %channelize.4 = bf16[32,16,512]{2,1,0:T(8,128)(2,1)S(1)} custom-call(bf16[64,530432]{1,0:T(8,128)(2,1)} %x_ref.7, bf16[2048,256]{1,0:T(8,128)(2,1)S(1)} %copy.7.w_ref, f32[8,128]{1,0:T(8,128)S(1)} %broadcast_in_dim.2.after_ref), custom_call_target="tpu_custom_call" | custom-call | flops 4345298944 | bytes 16973824 | tf_op jit(solution)/shard_map/channelize/pallas_call | solution.py:112
  15.6 3.0 %collective-permute-start = (bf16[8,16,512]{2,1,0:T(8,128)(2,1)S(1)}, bf16[8,16,512]{2,1,0:T(8,128)(2,1)S(1)}, u32[]{:S(2)}, u32[]{:S(2)}) collective-permute-start(bf16[8,16,512]{2,1,0:T(8,128)(2,1)S(1)} %get-tuple-element.80), channel_id=1, source_target_pairs={{0,8},{8,0},{16,24},{24,16},{1,9},{9,1},{17,25},{25,17},{2,10},{10... | collective-permute-start | bytes 393224 | tf_op jit(solution)/shard_map/ppermute | solution.py:250
  18.6 1.5 collective-permute-start.1
  20.1 12.6 %channelize.5 = bf16[32,16,512]{2,1,0:T(8,128)(2,1)S(1)} custom-call(bf16[64,530432]{1,0:T(8,128)(2,1)} %x_ref.7, bf16[2048,256]{1,0:T(8,128)(2,1)S(1)} %copy.7.w_ref, f32[8,128]{1,0:T(8,128)S(1)} %broadcast_in_dim.2.after_ref), custom_call_target="tpu_custom_call" | custom-call | flops 4345298944 | bytes 16973824 | tf_op jit(solution)/shard_map/channelize/pallas_call | solution.py:112
  32.7 2.0 collective-permute-start.3
  34.7 1.5 collective-permute-start.4
  36.4 2.1 %collective-permute-start.9 = (bf16[4,8,16,512]{3,2,1,0:T(8,128)(2,1)S(1)}, bf16[4,8,16,512]{3,2,1,0:T(8,128)(2,1)S(1)}, u32[]{:S(2)}, u32[]{:S(2)}) collective-permute-start(bf16[4,8,16,512]{3,2,1,0:T(8,128)(2,1)S(1)} %pad_maximum_fusion.refs_0_.refs_4_), channel_id=1, source_target_pairs={{0,2},{1,3},{2,4},{3,5},{4,6},{5,7},{6,0},{7,1},{8,10},{9,11},{10,... | collective-permute-start | bytes 1572872 | tf_op jit(solution)/shard_map/ppermute | solution.py:227
  38.5 12.6 %channelize.6 = bf16[32,16,512]{2,1,0:T(8,128)(2,1)S(1)} custom-call(bf16[64,530432]{1,0:T(8,128)(2,1)} %x_ref.7, bf16[2048,256]{1,0:T(8,128)(2,1)S(1)} %copy.7.w_ref, f32[8,128]{1,0:T(8,128)S(1)} %broadcast_in_dim.2.after_ref), custom_call_target="tpu_custom_call" | custom-call | flops 4345298944 | bytes 16973824 | tf_op jit(solution)/shard_map/channelize/pallas_call | solution.py:112
  51.1 1.6 collective-permute-start.6
  52.6 1.5 collective-permute-start.7
  54.7 2.1 %collective-permute-done.6 = bf16[8,16,512]{2,1,0:T(8,128)(2,1)S(1)} collective-permute-done((bf16[8,16,512]{2,1,0:T(8,128)(2,1)S(1)}, bf16[8,16,512]{2,1,0:T(8,128)(2,1)S(1)}, u32[]{:S(2)}, u32[]{:S(2)}) %collective-permute-start.6) | collective-permute-done | bytes 131104 | tf_op jit(solution)/shard_map/ppermute | solution.py:250
  58.1 2.0 collective-permute-done.8
  60.1 1.6 collective-permute-start.10
  61.7 1.6 collective-permute-start.11
  63.3 12.6 %channelize.7 = bf16[32,16,512]{2,1,0:T(8,128)(2,1)S(1)} custom-call(bf16[64,530432]{1,0:T(8,128)(2,1)} %x_ref.7, bf16[2048,256]{1,0:T(8,128)(2,1)S(1)} %copy.7.w_ref, f32[8,128]{1,0:T(8,128)S(1)} %broadcast_in_dim.2.after_ref), custom_call_target="tpu_custom_call" | custom-call | flops 4345298944 | bytes 16973824 | tf_op jit(solution)/shard_map/channelize/pallas_call | solution.py:112
  76.8 7.1 %collective-permute-done.11.refs_4_ = bf16[4,8,16,512]{3,2,1,0:T(8,128)(2,1)S(1)} collective-permute-done((bf16[4,8,16,512]{3,2,1,0:T(8,128)(2,1)S(1)}, bf16[4,8,16,512]{3,2,1,0:T(8,128)(2,1)S(1)}, u32[]{:S(2)}, u32[]{:S(2)}) %collective-permute-start.11) | collective-permute-done | bytes 524320 | tf_op jit(solution)/shard_map/ppermute | solution.py:227
  84.6 2.9 %collective-permute-start.14 = (bf16[8,16,512]{2,1,0:T(8,128)(2,1)S(1)}, bf16[8,16,512]{2,1,0:T(8,128)(2,1)S(1)}, u32[]{:S(2)}, u32[]{:S(2)}) collective-permute-start(bf16[8,16,512]{2,1,0:T(8,128)(2,1)S(1)} %get-tuple-element.66), channel_id=1, source_target_pairs={{0,24},{8,16},{16,8},{24,0},{1,25},{9,17},{17,9},{25,1},{2,26},{10... | collective-permute-start | bytes 393224 | tf_op jit(solution)/shard_map/ppermute | solution.py:250
  87.6 1.5 collective-permute-done.12
  92.1 13.6 %collective-permute-done.18.refs_6_ = bf16[4,8,16,512]{3,2,1,0:T(8,128)(2,1)} collective-permute-done((bf16[4,8,16,512]{3,2,1,0:T(8,128)(2,1)S(1)}, bf16[4,8,16,512]{3,2,1,0:T(8,128)(2,1)}, u32[]{:S(2)}, u32[]{:S(2)}) %collective-permute-start.18) | collective-permute-done | bytes 524320 | tf_op jit(solution)/shard_map/ppermute | solution.py:227
  105.8 11.1 %collective-permute-done.24.refs_7_ = bf16[4,8,16,512]{3,2,1,0:T(8,128)(2,1)} collective-permute-done((bf16[4,8,16,512]{3,2,1,0:T(8,128)(2,1)S(1)}, bf16[4,8,16,512]{3,2,1,0:T(8,128)(2,1)}, u32[]{:S(2)}, u32[]{:S(2)}) %collective-permute-start.24) | collective-permute-done | bytes 524320 | tf_op jit(solution)/shard_map/ppermute | solution.py:227
  118.1 8.3 %correlate.4 = (bf16[2,8,256,2048]{3,2,1,0:T(8,128)(2,1)}, f32[8,128]{1,0:T(8,128)}) custom-call(s32[3]{0:T(128)S(1)} %get-tuple-element.82.place_ref, bf16[4,8,16,512]{3,2,1,0:T(8,128)(2,1)S(1)} %pad_maximum_fusion.refs_0_.refs_4_, bf16[4,8,16,512]{3,2,1,0:T(8,128)(2,1)S(1)} %pad_maximum_fusion.1.refs_1_.refs_5_, ...), custom_call_target="tpu_custom_call" | custom-call | flops 2147483648 | bytes 10485760 | tf_op jit(solution)/shard_map/correlate/pallas_call | solution.py:178
  128.7 3.3 %collective-permute-start.17 = (bf16[4,8,16,512]{3,2,1,0:T(8,128)(2,1)S(1)}, bf16[4,8,16,512]{3,2,1,0:T(8,128)(2,1)S(1)}, u32[]{:S(2)}, u32[]{:S(2)}) collective-permute-start(bf16[4,8,16,512]{3,2,1,0:T(8,128)(2,1)S(1)} %collective-permute-done.16.refs_5_), channel_id=1, source_target_pairs={{0,2},{1,3},{2,4},{3,5},{4,6},{5,7},{6,0},{7,1},{8,10},{9,11},{10,... | collective-permute-start | bytes 1572872 | tf_op jit(solution)/shard_map/ppermute | solution.py:227
  132.0 11.8 %collective-permute-done.30.refs_7_ = bf16[4,8,16,512]{3,2,1,0:T(8,128)(2,1)S(1)} collective-permute-done((bf16[4,8,16,512]{3,2,1,0:T(8,128)(2,1)}, bf16[4,8,16,512]{3,2,1,0:T(8,128)(2,1)S(1)}, u32[]{:S(2)}, u32[]{:S(2)}) %collective-permute-start.30) | collective-permute-done | bytes 524320 | tf_op jit(solution)/shard_map/ppermute | solution.py:227
  143.8 11.2 %collective-permute-done.23.refs_6_ = bf16[4,8,16,512]{3,2,1,0:T(8,128)(2,1)S(1)} collective-permute-done((bf16[4,8,16,512]{3,2,1,0:T(8,128)(2,1)}, bf16[4,8,16,512]{3,2,1,0:T(8,128)(2,1)S(1)}, u32[]{:S(2)}, u32[]{:S(2)}) %collective-permute-start.23) | collective-permute-done | bytes 524320 | tf_op jit(solution)/shard_map/ppermute | solution.py:227
  156.1 8.1 %correlate.5 = (bf16[2,8,256,2048]{3,2,1,0:T(8,128)(2,1)}, f32[8,128]{1,0:T(8,128)}) custom-call(s32[3]{0:T(128)S(1)} %get-tuple-element.81.place_ref, bf16[4,8,16,512]{3,2,1,0:T(8,128)(2,1)S(1)} %pad_maximum_fusion.refs_0_.refs_4_, bf16[4,8,16,512]{3,2,1,0:T(8,128)(2,1)S(1)} %pad_maximum_fusion.1.refs_1_.refs_5_, ...), custom_call_target="tpu_custom_call", output_to_operand_aliasing={{0}: (13, {})} | custom-call | flops 2147483648 | bytes 10485760 | tf_op jit(solution)/shard_map/correlate/pallas_call | solution.py:178
  164.2 2.1 collective-permute-done.15.refs_4_
  166.3 11.2 %collective-permute-done.17.refs_5_ = bf16[4,8,16,512]{3,2,1,0:T(8,128)(2,1)S(1)} collective-permute-done((bf16[4,8,16,512]{3,2,1,0:T(8,128)(2,1)S(1)}, bf16[4,8,16,512]{3,2,1,0:T(8,128)(2,1)S(1)}, u32[]{:S(2)}, u32[]{:S(2)}) %collective-permute-start.17) | collective-permute-done | bytes 524320 | tf_op jit(solution)/shard_map/ppermute | solution.py:227
  178.0 6.8 %correlate.6 = (bf16[2,8,256,2048]{3,2,1,0:T(8,128)(2,1)}, f32[8,128]{1,0:T(8,128)}) custom-call(s32[3]{0:T(128)S(1)} %get-tuple-element.63.place_ref, bf16[4,8,16,512]{3,2,1,0:T(8,128)(2,1)S(1)} %pad_maximum_fusion.refs_0_.refs_4_, bf16[4,8,16,512]{3,2,1,0:T(8,128)(2,1)S(1)} %pad_maximum_fusion.1.refs_1_.refs_5_, ...), custom_call_target="tpu_custom_call", output_to_operand_aliasing={{0}: (13, {})} | custom-call | flops 2147483648 | bytes 10485760 | tf_op jit(solution)/shard_map/correlate/pallas_call | solution.py:178
  184.8 3.9 %collective-permute-done.31.refs_7_ = bf16[4,8,16,512]{3,2,1,0:T(8,128)(2,1)S(1)} collective-permute-done((bf16[4,8,16,512]{3,2,1,0:T(8,128)(2,1)S(1)}, bf16[4,8,16,512]{3,2,1,0:T(8,128)(2,1)S(1)}, u32[]{:S(2)}, u32[]{:S(2)}) %collective-permute-start.31) | collective-permute-done | bytes 524320 | tf_op jit(solution)/shard_map/ppermute | solution.py:227
  188.7 10.4 %collective-permute-done.29.refs_6_ = bf16[4,8,16,512]{3,2,1,0:T(8,128)(2,1)S(1)} collective-permute-done((bf16[4,8,16,512]{3,2,1,0:T(8,128)(2,1)S(1)}, bf16[4,8,16,512]{3,2,1,0:T(8,128)(2,1)S(1)}, u32[]{:S(2)}, u32[]{:S(2)}) %collective-permute-start.29) | collective-permute-done | bytes 524320 | tf_op jit(solution)/shard_map/ppermute | solution.py:227
  199.1 1.9 collective-permute-done.38.refs_10_
  201.0 6.8 %correlate.7 = (bf16[2,8,256,2048]{3,2,1,0:T(8,128)(2,1)}, f32[8,128]{1,0:T(8,128)}) custom-call(s32[3]{0:T(128)S(1)} %get-tuple-element.83.place_ref, bf16[4,8,16,512]{3,2,1,0:T(8,128)(2,1)S(1)} %pad_maximum_fusion.refs_0_.refs_4_, bf16[4,8,16,512]{3,2,1,0:T(8,128)(2,1)S(1)} %pad_maximum_fusion.1.refs_1_.refs_5_, ...), custom_call_target="tpu_custom_call", output_to_operand_aliasing={{0}: (13, {})} | custom-call | flops 2147483648 | bytes 10485760 | tf_op jit(solution)/shard_map/correlate/pallas_call | solution.py:178
  (86 shorter events, 14.7 us)
Async XLA Ops:
  15.6 20.7 %collective-permute-start = (bf16[8,16,512]{2,1,0:T(8,128)(2,1)S(1)}, bf16[8,16,512]{2,1,0:T(8,128)(2,1)S(1)}, u32[]{:S(2)}, u32[]{:S(2)}) collective-permute-start(bf16[8,16,512]{2,1,0:T(8,128)(2,1)S(1)} %get-tuple-element.80), channel_id=1, source_target_pairs={{0,8},{8,0},{16,24},{24,16},{1,9},{9,1},{17,25},{25,17},{2,10},{10... | collective-permute-start | bytes 393224 | tf_op jit(solution)/shard_map/ppermute | solution.py:250
  18.6 17.7 %collective-permute-start.1 = (bf16[8,16,512]{2,1,0:T(8,128)(2,1)S(1)}, bf16[8,16,512]{2,1,0:T(8,128)(2,1)S(1)}, u32[]{:S(2)}, u32[]{:S(2)}) collective-permute-start(bf16[8,16,512]{2,1,0:T(8,128)(2,1)S(1)} %get-tuple-element.79), channel_id=1, source_target_pairs={{0,16},{8,24},{16,0},{24,8},{1,17},{9,25},{17,1},{25,9},{2,18},{10... | collective-permute-start | bytes 393224 | tf_op jit(solution)/shard_map/ppermute | solution.py:250
  20.1 16.2 %collective-permute-start.2 = (bf16[8,16,512]{2,1,0:T(8,128)(2,1)S(1)}, bf16[8,16,512]{2,1,0:T(8,128)(2,1)S(1)}, u32[]{:S(2)}, u32[]{:S(2)}) collective-permute-start(bf16[8,16,512]{2,1,0:T(8,128)(2,1)S(1)} %get-tuple-element.78), channel_id=1, source_target_pairs={{0,24},{8,16},{16,8},{24,0},{1,25},{9,17},{17,9},{25,1},{2,26},{10... | collective-permute-start | bytes 393224 | tf_op jit(solution)/shard_map/ppermute | solution.py:250
  32.7 19.9 %collective-permute-start.3 = (bf16[8,16,512]{2,1,0:T(8,128)(2,1)S(1)}, bf16[8,16,512]{2,1,0:T(8,128)(2,1)S(1)}, u32[]{:S(2)}, u32[]{:S(2)}) collective-permute-start(bf16[8,16,512]{2,1,0:T(8,128)(2,1)S(1)} %get-tuple-element.76), channel_id=1, source_target_pairs={{0,8},{8,0},{16,24},{24,16},{1,9},{9,1},{17,25},{25,17},{2,10},{10... | collective-permute-start | bytes 393224 | tf_op jit(solution)/shard_map/ppermute | solution.py:250
  34.7 19.4 %collective-permute-start.4 = (bf16[8,16,512]{2,1,0:T(8,128)(2,1)S(1)}, bf16[8,16,512]{2,1,0:T(8,128)(2,1)S(1)}, u32[]{:S(2)}, u32[]{:S(2)}) collective-permute-start(bf16[8,16,512]{2,1,0:T(8,128)(2,1)S(1)} %get-tuple-element.75), channel_id=1, source_target_pairs={{0,16},{8,24},{16,0},{24,8},{1,17},{9,25},{17,1},{25,9},{2,18},{10... | collective-permute-start | bytes 393224 | tf_op jit(solution)/shard_map/ppermute | solution.py:250
  36.3 18.4 %collective-permute-start.5 = (bf16[8,16,512]{2,1,0:T(8,128)(2,1)S(1)}, bf16[8,16,512]{2,1,0:T(8,128)(2,1)S(1)}, u32[]{:S(2)}, u32[]{:S(2)}) collective-permute-start(bf16[8,16,512]{2,1,0:T(8,128)(2,1)S(1)} %get-tuple-element.74), channel_id=1, source_target_pairs={{0,24},{8,16},{16,8},{24,0},{1,25},{9,17},{17,9},{25,1},{2,26},{10... | collective-permute-start | bytes 393224 | tf_op jit(solution)/shard_map/ppermute | solution.py:250
  36.4 23.7 %collective-permute-start.9 = (bf16[4,8,16,512]{3,2,1,0:T(8,128)(2,1)S(1)}, bf16[4,8,16,512]{3,2,1,0:T(8,128)(2,1)S(1)}, u32[]{:S(2)}, u32[]{:S(2)}) collective-permute-start(bf16[4,8,16,512]{3,2,1,0:T(8,128)(2,1)S(1)} %pad_maximum_fusion.refs_0_.refs_4_), channel_id=1, source_target_pairs={{0,2},{1,3},{2,4},{3,5},{4,6},{5,7},{6,0},{7,1},{8,10},{9,11},{10,... | collective-permute-start | bytes 1572872 | tf_op jit(solution)/shard_map/ppermute | solution.py:227
  54.2 5.9 %collective-permute-start.8 = (bf16[8,16,512]{2,1,0:T(8,128)(2,1)S(1)}, bf16[8,16,512]{2,1,0:T(8,128)(2,1)S(1)}, u32[]{:S(2)}, u32[]{:S(2)}) collective-permute-start(bf16[8,16,512]{2,1,0:T(8,128)(2,1)S(1)} %get-tuple-element.70), channel_id=1, source_target_pairs={{0,24},{8,16},{16,8},{24,0},{1,25},{9,17},{17,9},{25,1},{2,26},{10... | collective-permute-start | bytes 393224 | tf_op jit(solution)/shard_map/ppermute | solution.py:250
  60.1 16.7 %collective-permute-start.10 = (bf16[4,8,16,512]{3,2,1,0:T(8,128)(2,1)S(1)}, bf16[4,8,16,512]{3,2,1,0:T(8,128)(2,1)S(1)}, u32[]{:S(2)}, u32[]{:S(2)}) collective-permute-start(bf16[4,8,16,512]{3,2,1,0:T(8,128)(2,1)S(1)} %pad_maximum_fusion.1.refs_1_.refs_5_), channel_id=1, source_target_pairs={{0,2},{1,3},{2,4},{3,5},{4,6},{5,7},{6,0},{7,1},{8,10},{9,11},{10,... | collective-permute-start | bytes 1572872 | tf_op jit(solution)/shard_map/ppermute | solution.py:227
  61.7 22.2 %collective-permute-start.11 = (bf16[4,8,16,512]{3,2,1,0:T(8,128)(2,1)S(1)}, bf16[4,8,16,512]{3,2,1,0:T(8,128)(2,1)S(1)}, u32[]{:S(2)}, u32[]{:S(2)}) collective-permute-start(bf16[4,8,16,512]{3,2,1,0:T(8,128)(2,1)S(1)} %collective-permute-done.9.refs_4_), channel_id=1, source_target_pairs={{0,2},{1,3},{2,4},{3,5},{4,6},{5,7},{6,0},{7,1},{8,10},{9,11},{10,... | collective-permute-start | bytes 1572872 | tf_op jit(solution)/shard_map/ppermute | solution.py:227
  63.3 27.3 %collective-permute-start.19 = (bf16[4,8,16,512]{3,2,1,0:T(8,128)(2,1)S(1)}, bf16[4,8,16,512]{3,2,1,0:T(8,128)(2,1)S(1)}, u32[]{:S(2)}, u32[]{:S(2)}) collective-permute-start(bf16[4,8,16,512]{3,2,1,0:T(8,128)(2,1)S(1)} %pad_maximum_fusion.refs_0_.refs_4_), channel_id=1, source_target_pairs={{0,1},{1,0},{2,3},{3,2},{4,5},{5,4},{6,7},{7,6},{8,9},{9,8},{10,11... | collective-permute-start | bytes 1572872 | tf_op jit(solution)/shard_map/ppermute | solution.py:264
  84.6 5.9 %collective-permute-start.14 = (bf16[8,16,512]{2,1,0:T(8,128)(2,1)S(1)}, bf16[8,16,512]{2,1,0:T(8,128)(2,1)S(1)}, u32[]{:S(2)}, u32[]{:S(2)}) collective-permute-start(bf16[8,16,512]{2,1,0:T(8,128)(2,1)S(1)} %get-tuple-element.66), channel_id=1, source_target_pairs={{0,24},{8,16},{16,8},{24,0},{1,25},{9,17},{17,9},{25,1},{2,26},{10... | collective-permute-start | bytes 393224 | tf_op jit(solution)/shard_map/ppermute | solution.py:250
  89.1 16.6 %collective-permute-start.18 = (bf16[4,8,16,512]{3,2,1,0:T(8,128)(2,1)S(1)}, bf16[4,8,16,512]{3,2,1,0:T(8,128)(2,1)}, u32[]{:S(2)}, u32[]{:S(2)}) collective-permute-start(bf16[4,8,16,512]{3,2,1,0:T(8,128)(2,1)S(1)} %pad_maximum_fusion.2.refs_2_.refs_6_), channel_id=1, source_target_pairs={{0,2},{1,3},{2,4},{3,5},{4,6},{5,7},{6,0},{7,1},{8,10},{9,11},{10,... | collective-permute-start | bytes 1572872 | tf_op jit(solution)/shard_map/ppermute | solution.py:227
  90.6 15.2 %collective-permute-start.22 = (bf16[4,8,16,512]{3,2,1,0:T(8,128)(2,1)S(1)}, bf16[4,8,16,512]{3,2,1,0:T(8,128)(2,1)}, u32[]{:S(2)}, u32[]{:S(2)}) collective-permute-start(bf16[4,8,16,512]{3,2,1,0:T(8,128)(2,1)S(1)} %pad_maximum_fusion.3.refs_3_.refs_7_), channel_id=1, source_target_pairs={{0,1},{1,0},{2,3},{3,2},{4,5},{5,4},{6,7},{7,6},{8,9},{9,8},{10,11... | collective-permute-start | bytes 1572872 | tf_op jit(solution)/shard_map/ppermute | solution.py:264
  91.5 25.5 %collective-permute-start.24 = (bf16[4,8,16,512]{3,2,1,0:T(8,128)(2,1)S(1)}, bf16[4,8,16,512]{3,2,1,0:T(8,128)(2,1)}, u32[]{:S(2)}, u32[]{:S(2)}) collective-permute-start(bf16[4,8,16,512]{3,2,1,0:T(8,128)(2,1)S(1)} %pad_maximum_fusion.3.refs_3_.refs_7_), channel_id=1, source_target_pairs={{0,2},{1,3},{2,4},{3,5},{4,6},{5,7},{6,0},{7,1},{8,10},{9,11},{10,... | collective-permute-start | bytes 1572872 | tf_op jit(solution)/shard_map/ppermute | solution.py:227
  91.6 34.9 %collective-permute-start.25 = (bf16[4,8,16,512]{3,2,1,0:T(8,128)(2,1)S(1)}, bf16[4,8,16,512]{3,2,1,0:T(8,128)(2,1)S(1)}, u32[]{:S(2)}, u32[]{:S(2)}) collective-permute-start(bf16[4,8,16,512]{3,2,1,0:T(8,128)(2,1)S(1)} %collective-permute-done.9.refs_4_), channel_id=1, source_target_pairs={{0,1},{1,0},{2,3},{3,2},{4,5},{5,4},{6,7},{7,6},{8,9},{9,8},{10,11... | collective-permute-start | bytes 1572872 | tf_op jit(solution)/shard_map/ppermute | solution.py:264
  92.0 34.9 %collective-permute-start.26 = (bf16[4,8,16,512]{3,2,1,0:T(8,128)(2,1)}, bf16[4,8,16,512]{3,2,1,0:T(8,128)(2,1)S(1)}, u32[]{:S(2)}, u32[]{:S(2)}) collective-permute-start(bf16[4,8,16,512]{3,2,1,0:T(8,128)(2,1)} %copy-done.2), channel_id=1, source_target_pairs={{0,1},{1,0},{2,3},{3,2},{4,5},{5,4},{6,7},{7,6},{8,9},{9,8},{10,11... | collective-permute-start | bytes 1572872 | tf_op jit(solution)/shard_map/ppermute | solution.py:264
  105.7 21.3 %collective-permute-start.27 = (bf16[4,8,16,512]{3,2,1,0:T(8,128)(2,1)}, bf16[4,8,16,512]{3,2,1,0:T(8,128)(2,1)S(1)}, u32[]{:S(2)}, u32[]{:S(2)}) collective-permute-start(bf16[4,8,16,512]{3,2,1,0:T(8,128)(2,1)} %collective-permute-done.18.refs_6_), channel_id=1, source_target_pairs={{0,1},{1,0},{2,3},{3,2},{4,5},{5,4},{6,7},{7,6},{8,9},{9,8},{10,11... | collective-permute-start | bytes 1572872 | tf_op jit(solution)/shard_map/ppermute | solution.py:264
  105.8 21.8 %collective-permute-start.16 = (bf16[4,8,16,512]{3,2,1,0:T(8,128)(2,1)}, bf16[4,8,16,512]{3,2,1,0:T(8,128)(2,1)S(1)}, u32[]{:S(2)}, u32[]{:S(2)}) collective-permute-start(bf16[4,8,16,512]{3,2,1,0:T(8,128)(2,1)} %copy-done.2), channel_id=1, source_target_pairs={{0,2},{1,3},{2,4},{3,5},{4,6},{5,7},{6,0},{7,1},{8,10},{9,11},{10,... | collective-permute-start | bytes 1572872 | tf_op jit(solution)/shard_map/ppermute | solution.py:227
  117.0 10.7 %collective-permute-start.34 = (bf16[4,8,16,512]{3,2,1,0:T(8,128)(2,1)}, bf16[4,8,16,512]{3,2,1,0:T(8,128)(2,1)S(1)}, u32[]{:S(2)}, u32[]{:S(2)}) collective-permute-start(bf16[4,8,16,512]{3,2,1,0:T(8,128)(2,1)} %copy-done), channel_id=1, source_target_pairs={{0,1},{1,0},{2,3},{3,2},{4,5},{5,4},{6,7},{7,6},{8,9},{9,8},{10,11... | collective-permute-start | bytes 1572872 | tf_op jit(solution)/shard_map/ppermute | solution.py:264
  127.0 16.8 %collective-permute-start.30 = (bf16[4,8,16,512]{3,2,1,0:T(8,128)(2,1)}, bf16[4,8,16,512]{3,2,1,0:T(8,128)(2,1)S(1)}, u32[]{:S(2)}, u32[]{:S(2)}) collective-permute-start(bf16[4,8,16,512]{3,2,1,0:T(8,128)(2,1)} %collective-permute-done.24.refs_7_), channel_id=1, source_target_pairs={{0,2},{1,3},{2,4},{3,5},{4,6},{5,7},{6,0},{7,1},{8,10},{9,11},{10,... | collective-permute-start | bytes 1572872 | tf_op jit(solution)/shard_map/ppermute | solution.py:227
  127.0 28.0 %collective-permute-start.23 = (bf16[4,8,16,512]{3,2,1,0:T(8,128)(2,1)}, bf16[4,8,16,512]{3,2,1,0:T(8,128)(2,1)S(1)}, u32[]{:S(2)}, u32[]{:S(2)}) collective-permute-start(bf16[4,8,16,512]{3,2,1,0:T(8,128)(2,1)} %collective-permute-done.18.refs_6_), channel_id=1, source_target_pairs={{0,2},{1,3},{2,4},{3,5},{4,6},{5,7},{6,0},{7,1},{8,10},{9,11},{10,... | collective-permute-start | bytes 1572872 | tf_op jit(solution)/shard_map/ppermute | solution.py:227
  127.6 38.6 %collective-permute-start.15 = (bf16[4,8,16,512]{3,2,1,0:T(8,128)(2,1)}, bf16[4,8,16,512]{3,2,1,0:T(8,128)(2,1)S(1)}, u32[]{:S(2)}, u32[]{:S(2)}) collective-permute-start(bf16[4,8,16,512]{3,2,1,0:T(8,128)(2,1)} %copy-done), channel_id=1, source_target_pairs={{0,2},{1,3},{2,4},{3,5},{4,6},{5,7},{6,0},{7,1},{8,10},{9,11},{10,... | collective-permute-start | bytes 1572872 | tf_op jit(solution)/shard_map/ppermute | solution.py:227
  127.6 38.6 %collective-permute-start.35 = (bf16[4,8,16,512]{3,2,1,0:T(8,128)(2,1)S(1)}, bf16[4,8,16,512]{3,2,1,0:T(8,128)(2,1)S(1)}, u32[]{:S(2)}, u32[]{:S(2)}) collective-permute-start(bf16[4,8,16,512]{3,2,1,0:T(8,128)(2,1)S(1)} %collective-permute-done.16.refs_5_), channel_id=1, source_target_pairs={{0,1},{1,0},{2,3},{3,2},{4,5},{5,4},{6,7},{7,6},{8,9},{9,8},{10,11... | collective-permute-start | bytes 1572872 | tf_op jit(solution)/shard_map/ppermute | solution.py:264
  128.7 48.7 %collective-permute-start.17 = (bf16[4,8,16,512]{3,2,1,0:T(8,128)(2,1)S(1)}, bf16[4,8,16,512]{3,2,1,0:T(8,128)(2,1)S(1)}, u32[]{:S(2)}, u32[]{:S(2)}) collective-permute-start(bf16[4,8,16,512]{3,2,1,0:T(8,128)(2,1)S(1)} %collective-permute-done.16.refs_5_), channel_id=1, source_target_pairs={{0,2},{1,3},{2,4},{3,5},{4,6},{5,7},{6,0},{7,1},{8,10},{9,11},{10,... | collective-permute-start | bytes 1572872 | tf_op jit(solution)/shard_map/ppermute | solution.py:227
  143.8 33.7 %collective-permute-start.37 = (bf16[4,8,16,512]{3,2,1,0:T(8,128)(2,1)S(1)}, bf16[4,8,16,512]{3,2,1,0:T(8,128)(2,1)S(1)}, u32[]{:S(2)}, u32[]{:S(2)}) collective-permute-start(bf16[4,8,16,512]{3,2,1,0:T(8,128)(2,1)S(1)} %collective-permute-done.30.refs_7_), channel_id=1, source_target_pairs={{0,1},{1,0},{2,3},{3,2},{4,5},{5,4},{6,7},{7,6},{8,9},{9,8},{10,11... | collective-permute-start | bytes 1572872 | tf_op jit(solution)/shard_map/ppermute | solution.py:264
  155.0 23.0 %collective-permute-start.36 = (bf16[4,8,16,512]{3,2,1,0:T(8,128)(2,1)S(1)}, bf16[4,8,16,512]{3,2,1,0:T(8,128)(2,1)S(1)}, u32[]{:S(2)}, u32[]{:S(2)}) collective-permute-start(bf16[4,8,16,512]{3,2,1,0:T(8,128)(2,1)S(1)} %collective-permute-done.23.refs_6_), channel_id=1, source_target_pairs={{0,1},{1,0},{2,3},{3,2},{4,5},{5,4},{6,7},{7,6},{8,9},{9,8},{10,11... | collective-permute-start | bytes 1572872 | tf_op jit(solution)/shard_map/ppermute | solution.py:264
  166.2 22.5 %collective-permute-start.31 = (bf16[4,8,16,512]{3,2,1,0:T(8,128)(2,1)S(1)}, bf16[4,8,16,512]{3,2,1,0:T(8,128)(2,1)S(1)}, u32[]{:S(2)}, u32[]{:S(2)}) collective-permute-start(bf16[4,8,16,512]{3,2,1,0:T(8,128)(2,1)S(1)} %collective-permute-done.30.refs_7_), channel_id=1, source_target_pairs={{0,2},{1,3},{2,4},{3,5},{4,6},{5,7},{6,0},{7,1},{8,10},{9,11},{10,... | collective-permute-start | bytes 1572872 | tf_op jit(solution)/shard_map/ppermute | solution.py:227
  166.3 32.8 %collective-permute-start.29 = (bf16[4,8,16,512]{3,2,1,0:T(8,128)(2,1)S(1)}, bf16[4,8,16,512]{3,2,1,0:T(8,128)(2,1)S(1)}, u32[]{:S(2)}, u32[]{:S(2)}) collective-permute-start(bf16[4,8,16,512]{3,2,1,0:T(8,128)(2,1)S(1)} %collective-permute-done.23.refs_6_), channel_id=1, source_target_pairs={{0,2},{1,3},{2,4},{3,5},{4,6},{5,7},{6,0},{7,1},{8,10},{9,11},{10,... | collective-permute-start | bytes 1572872 | tf_op jit(solution)/shard_map/ppermute | solution.py:227
  177.5 21.6 %collective-permute-start.32 = (bf16[4,8,16,512]{3,2,1,0:T(8,128)(2,1)S(1)}, bf16[4,8,16,512]{3,2,1,0:T(8,128)(2,1)S(1)}, u32[]{:S(2)}, u32[]{:S(2)}) collective-permute-start(bf16[4,8,16,512]{3,2,1,0:T(8,128)(2,1)S(1)} %collective-permute-done.15.refs_4_), channel_id=1, source_target_pairs={{0,1},{1,0},{2,3},{3,2},{4,5},{5,4},{6,7},{7,6},{8,9},{9,8},{10,11... | collective-permute-start | bytes 1572872 | tf_op jit(solution)/shard_map/ppermute | solution.py:264
  177.5 21.6 %collective-permute-start.33 = (bf16[4,8,16,512]{3,2,1,0:T(8,128)(2,1)S(1)}, bf16[4,8,16,512]{3,2,1,0:T(8,128)(2,1)S(1)}, u32[]{:S(2)}, u32[]{:S(2)}) collective-permute-start(bf16[4,8,16,512]{3,2,1,0:T(8,128)(2,1)S(1)} %collective-permute-done.17.refs_5_), channel_id=1, source_target_pairs={{0,1},{1,0},{2,3},{3,2},{4,5},{5,4},{6,7},{7,6},{8,9},{9,8},{10,11... | collective-permute-start | bytes 1572872 | tf_op jit(solution)/shard_map/ppermute | solution.py:264
  188.7 10.4 %collective-permute-start.39 = (bf16[4,8,16,512]{3,2,1,0:T(8,128)(2,1)S(1)}, bf16[4,8,16,512]{3,2,1,0:T(8,128)(2,1)S(1)}, u32[]{:S(2)}, u32[]{:S(2)}) collective-permute-start(bf16[4,8,16,512]{3,2,1,0:T(8,128)(2,1)S(1)} %collective-permute-done.31.refs_7_), channel_id=1, source_target_pairs={{0,1},{1,0},{2,3},{3,2},{4,5},{5,4},{6,7},{7,6},{8,9},{9,8},{10,11... | collective-permute-start | bytes 1572872 | tf_op jit(solution)/shard_map/ppermute | solution.py:264
  (14 other events, 142.4 us)

commit v3 on v2

--- a/solution.py
+++ b/solution.py
@@ -215,56 +215,67 @@
 
     table = folded_table(fir_taps, freq_count)
     token = jnp.zeros((8, LANES), jnp.float32)
-    held = [[None] * groups for _ in range(ring)]
-
-    def after(token, *arrays):
-        return lax.optimization_barrier((token, *arrays))
-
-    def move_on(step, group, token=None):
-        piece = held[step - 1][group]
-        if token is not None:
-            piece, _ = lax.optimization_barrier((piece, token))
-        held[step][group] = lax.ppermute(piece, "tm", onward)
+    held, swapped = {}, {}
+
+    def behind(array, *others):
+        for other in others:
+            array, _ = lax.optimization_barrier((array, other))
+        return array
+
+    def move_on(step, group, *others):
+        if (step, group) not in held:
+            piece = behind(held[step - 1, group], *others)
+            held[step, group] = lax.ppermute(piece, "tm", onward)
+        return held[step, group]
+
+    def swap_cores(step, group, *others):
+        if (step, group) not in swapped:
+            piece = behind(held[step, group], *others)
+            swapped[step, group] = lax.ppermute(piece, "tm", swap)
+        return swapped[step, group]
 
     for group in range(groups):
-        if group == 2:
-            token, held[0][0] = after(token, held[0][0])
-        elif group >= 3:
-            if held[1][group - 3] is None:
-                move_on(1, group - 3)
-            token, held[0][group - 2], held[0][group - 1], held[1][group - 3] = after(
-                token, held[0][group - 2], held[0][group - 1], held[1][group - 3]
-            )
+        if group:
+            token = behind(token, held[0, group - 1])
         spectra = channelize(voltages, table, token, group)
-        token, spectra = after(token, spectra)
-        if group == groups - 1 and groups >= 4 and ring >= 3:
-            move_on(1, group - 2)
-            move_on(2, group - 3)
-            spectra, held[1][group - 2], held[2][group - 3] = lax.optimization_barrier(
-                (spectra, held[1][group - 2], held[2][group - 3])
+        if group:
+            spectra = behind(
+                spectra,
+                swap_cores(0, group - 1),
+                *([move_on(group, 0)] if group < ring else []),
+                *([move_on(1, group - 1)] if ring > 1 else []),
             )
         spectra = spectra.reshape(freq_count, CH_DEV, GROUP, 2 * S)
         parts = [spectra[0]]
         for k in range(1, freq_count):
             partners = [(i, i ^ k) for i in range(freq_count)]
             parts.append(lax.ppermute(spectra[k], "freq", partners))
-        held[0][group] = jnp.stack(parts)
+        if group >= 3 and ring > 2:
+            parts[-1] = behind(parts[-1], move_on(2, group - 2))
+        held[0, group] = jnp.stack(parts)
 
     result, tokens = None, []
     for step in range(ring):
         for group in range(groups):
-            if held[step][group] is None:
-                late = step >= 2 and group >= groups // 2
-                move_on(step, group, tokens[step - 2] if late else None)
-        other = []
+            others = []
+            if step >= 2 and group == groups - 1:
+                others.append(tokens[step - 2])
+            if step >= 2 and group >= 1:
+                others.append(swap_cores(step - 1, group - 1))
+            move_on(step, group, *others)
         for group in range(groups):
-            piece = held[step][group]
-            if step == ring - 1 and step >= 1 and group >= groups // 2:
-                piece, _ = lax.optimization_barrier((piece, tokens[step - 1]))
-            other.append(lax.ppermute(piece, "tm", swap))
+            late = step == ring - 1 and step >= 1 and group >= groups // 2
+            swap_cores(step, group, *([tokens[step - 1]] if late else []))
         source = (tm // 2 + ring - step) % ring
         place = jnp.stack([freq, tm % 2, source])
-        result, token = correlate(place, held[0], held[step], other, result, total_columns)
+        result, token = correlate(
+            place,
+            [held[0, group] for group in range(groups)],
+            [held[step, group] for group in range(groups)],
+            [swapped[step, group] for group in range(groups)],
+            result,
+            total_columns,
+        )
         tokens.append(token)
     return result
 

time: 209 us -> 212 us (1.014)
  local copies, waits for them, and re-layouts: 3.64 us -> 9.69 us
  starting transfers between devices: 25.6 us -> 22.3 us
  waiting for transfers between devices: 95.2 us -> 92.5 us
    ppermute x28, waiting for transfers between devices: 86.9 us -> 75.7 us  [the longest x12 73.5 us: move_on(): held[step, group] = lax.ppermute(piece, 'tm', onward)]
    ppermute x12, waiting for transfers between devices: 8.28 us -> 16.9 us  [on_device(): parts.append(lax.ppermute(spectra[k], 'freq', partners))]
    unnamed x12 -> x40, local copies, waits for them, and re-layouts: 2.88 us -> 8.94 us
    ppermute x28, starting transfers between devices: 10.4 us -> 7.1 us  [the longest x12 4.46 us: move_on(): held[step, group] = lax.ppermute(piece, 'tm', onward)]
  transfers between devices with their start and end apart: 40 -> 40, of which waited for: 19 -> 17; matrix products, arithmetic and copies ran while one was open for 0% -> 0% of each run, Pallas kernels for 29% -> 30%
where the time goes in v3:
time: 212 us; the launch traced here: 210 us
  waiting for transfers between devices  92.5 us (44%)
  Pallas kernels  81.9 us (39%)
  starting transfers between devices  22.3 us (11%)
  local copies, waits for them, and re-layouts  9.69 us (5%)
  other arithmetic  2.68 us (1%)
    ppermute x12, waiting for transfers between devices, move_on(): held[step, group] = lax.ppermute(piece, 'tm', onward)  73.5 us
    pallas_call x4, Pallas kernels, channelize(): pl.pallas_call(functools.partial(channelize_kernel, channels), grid=(fram...  50.3 us
    pallas_call x4, Pallas kernels, correlate(): pl.pallas_call(functools.partial(correlate_kernel, groups), grid_spec=plt...  31.6 us
    ppermute x12, waiting for transfers between devices, on_device(): parts.append(lax.ppermute(spectra[k], 'freq', partners))  16.9 us
    ppermute x12, starting transfers between devices, on_device(): parts.append(lax.ppermute(spectra[k], 'freq', partners))  15.2 us
    unnamed x40, local copies, waits for them, and re-layouts  8.94 us
    ppermute x12, starting transfers between devices, move_on(): held[step, group] = lax.ppermute(piece, 'tm', onward)  4.46 us
  transfers between devices with their start and end apart: 40, of which 17 were waited for; matrix products, arithmetic and copies ran while one was open for 0% of the time, Pallas kernels for 30%

profile of v3, /device:TPU:0, one launch (start us, length us, event | category | flops | bytes accessed | tf_op | source)
XLA Modules:
  0.0 209.5 jit_solution(1670538331112081277)
XLA Ops:
  2.9 12.6 %channelize.4 = bf16[32,16,512]{2,1,0:T(8,128)(2,1)S(1)} custom-call(bf16[64,530432]{1,0:T(8,128)(2,1)} %x_ref.7, bf16[2048,256]{1,0:T(8,128)(2,1)S(1)} %copy.7.w_ref, f32[8,128]{1,0:T(8,128)S(1)} %broadcast_in_dim.2.after_ref), custom_call_target="tpu_custom_call" | custom-call | flops 4345298944 | bytes 16973824 | tf_op jit(solution)/shard_map/channelize/pallas_call | solution.py:112
  15.6 3.0 %collective-permute-start = (bf16[8,16,512]{2,1,0:T(8,128)(2,1)S(1)}, bf16[8,16,512]{2,1,0:T(8,128)(2,1)S(1)}, u32[]{:S(2)}, u32[]{:S(2)}) collective-permute-start(bf16[8,16,512]{2,1,0:T(8,128)(2,1)S(1)} %get-tuple-element.72), channel_id=1, source_target_pairs={{0,8},{8,0},{16,24},{24,16},{1,9},{9,1},{17,25},{25,17},{2,10},{10... | collective-permute-start | bytes 393224 | tf_op jit(solution)/shard_map/ppermute | solution.py:252
  18.6 1.5 collective-permute-start.1
  20.1 2.4 %collective-permute-done = bf16[8,16,512]{2,1,0:T(8,128)(2,1)S(1)} collective-permute-done((bf16[8,16,512]{2,1,0:T(8,128)(2,1)S(1)}, bf16[8,16,512]{2,1,0:T(8,128)(2,1)S(1)}, u32[]{:S(2)}, u32[]{:S(2)}) %collective-permute-start) | collective-permute-done | bytes 131104 | tf_op jit(solution)/shard_map/ppermute | solution.py:252
  22.5 3.9 %collective-permute-done.1 = bf16[8,16,512]{2,1,0:T(8,128)(2,1)S(1)} collective-permute-done((bf16[8,16,512]{2,1,0:T(8,128)(2,1)S(1)}, bf16[8,16,512]{2,1,0:T(8,128)(2,1)S(1)}, u32[]{:S(2)}, u32[]{:S(2)}) %collective-permute-start.1) | collective-permute-done | bytes 131104 | tf_op jit(solution)/shard_map/ppermute | solution.py:252
  26.5 1.6 collective-permute-start.4
  28.1 12.6 %channelize.5 = bf16[32,16,512]{2,1,0:T(8,128)(2,1)S(1)} custom-call(bf16[64,530432]{1,0:T(8,128)(2,1)} %x_ref.7, bf16[2048,256]{1,0:T(8,128)(2,1)S(1)} %copy.7.w_ref, f32[8,128]{1,0:T(8,128)S(1)} %broadcast_in_dim.2.after_ref), custom_call_target="tpu_custom_call" | custom-call | flops 4345298944 | bytes 16973824 | tf_op jit(solution)/shard_map/channelize/pallas_call | solution.py:112
  40.7 1.9 collective-permute-done.4.refs_4_
  44.8 1.4 collective-permute-start.7
  46.3 2.3 %collective-permute-done.5 = bf16[8,16,512]{2,1,0:T(8,128)(2,1)S(1)} collective-permute-done((bf16[8,16,512]{2,1,0:T(8,128)(2,1)S(1)}, bf16[8,16,512]{2,1,0:T(8,128)(2,1)S(1)}, u32[]{:S(2)}, u32[]{:S(2)}) %collective-permute-start.5) | collective-permute-done | bytes 131104 | tf_op jit(solution)/shard_map/ppermute | solution.py:252
  48.6 3.2 %collective-permute-done.6 = bf16[8,16,512]{2,1,0:T(8,128)(2,1)S(1)} collective-permute-done((bf16[8,16,512]{2,1,0:T(8,128)(2,1)S(1)}, bf16[8,16,512]{2,1,0:T(8,128)(2,1)S(1)}, u32[]{:S(2)}, u32[]{:S(2)}) %collective-permute-start.6) | collective-permute-done | bytes 131104 | tf_op jit(solution)/shard_map/ppermute | solution.py:252
  52.0 1.5 collective-permute-start.10
  53.5 12.6 %channelize.6 = bf16[32,16,512]{2,1,0:T(8,128)(2,1)S(1)} custom-call(bf16[64,530432]{1,0:T(8,128)(2,1)} %x_ref.7, bf16[2048,256]{1,0:T(8,128)(2,1)S(1)} %copy.7.w_ref, f32[8,128]{1,0:T(8,128)S(1)} %broadcast_in_dim.2.after_ref), custom_call_target="tpu_custom_call" | custom-call | flops 4345298944 | bytes 16973824 | tf_op jit(solution)/shard_map/channelize/pallas_call | solution.py:112
  66.1 2.4 %collective-permute-done.9.refs_4_ = bf16[4,8,16,512]{3,2,1,0:T(8,128)(2,1)S(1)} collective-permute-done((bf16[4,8,16,512]{3,2,1,0:T(8,128)(2,1)S(1)}, bf16[4,8,16,512]{3,2,1,0:T(8,128)(2,1)S(1)}, u32[]{:S(2)}, u32[]{:S(2)}) %collective-permute-start.9) | collective-permute-done | bytes 524320 | tf_op jit(solution)/shard_map/ppermute | solution.py:228
  68.5 10.8 %collective-permute-done.10.refs_5_ = bf16[4,8,16,512]{3,2,1,0:T(8,128)(2,1)S(1)} collective-permute-done((bf16[4,8,16,512]{3,2,1,0:T(8,128)(2,1)S(1)}, bf16[4,8,16,512]{3,2,1,0:T(8,128)(2,1)S(1)}, u32[]{:S(2)}, u32[]{:S(2)}) %collective-permute-start.10) | collective-permute-done | bytes 524320 | tf_op jit(solution)/shard_map/ppermute | solution.py:228
  80.2 1.4 collective-permute-start.12
  81.6 1.3 collective-permute-start.13
  82.9 2.7 %collective-permute-done.11 = bf16[8,16,512]{2,1,0:T(8,128)(2,1)S(1)} collective-permute-done((bf16[8,16,512]{2,1,0:T(8,128)(2,1)S(1)}, bf16[8,16,512]{2,1,0:T(8,128)(2,1)S(1)}, u32[]{:S(2)}, u32[]{:S(2)}) %collective-permute-start.11) | collective-permute-done | bytes 131104 | tf_op jit(solution)/shard_map/ppermute | solution.py:252
  85.6 2.4 %collective-permute-done.12 = bf16[8,16,512]{2,1,0:T(8,128)(2,1)S(1)} collective-permute-done((bf16[8,16,512]{2,1,0:T(8,128)(2,1)S(1)}, bf16[8,16,512]{2,1,0:T(8,128)(2,1)S(1)}, u32[]{:S(2)}, u32[]{:S(2)}) %collective-permute-start.12) | collective-permute-done | bytes 131104 | tf_op jit(solution)/shard_map/ppermute | solution.py:252
  89.3 12.6 %channelize.7 = bf16[32,16,512]{2,1,0:T(8,128)(2,1)S(1)} custom-call(bf16[64,530432]{1,0:T(8,128)(2,1)} %x_ref.7, bf16[2048,256]{1,0:T(8,128)(2,1)S(1)} %copy.7.w_ref, f32[8,128]{1,0:T(8,128)S(1)} %broadcast_in_dim.2.after_ref), custom_call_target="tpu_custom_call" | custom-call | flops 4345298944 | bytes 16973824 | tf_op jit(solution)/shard_map/channelize/pallas_call | solution.py:112
  101.9 2.8 %collective-permute-done.15.refs_4_ = bf16[4,8,16,512]{3,2,1,0:T(8,128)(2,1)S(1)} collective-permute-done((bf16[4,8,16,512]{3,2,1,0:T(8,128)(2,1)S(1)}, bf16[4,8,16,512]{3,2,1,0:T(8,128)(2,1)S(1)}, u32[]{:S(2)}, u32[]{:S(2)}) %collective-permute-start.15) | collective-permute-done | bytes 524320 | tf_op jit(solution)/shard_map/ppermute | solution.py:228
  104.7 11.2 %collective-permute-done.16.refs_6_ = bf16[4,8,16,512]{3,2,1,0:T(8,128)(2,1)S(1)} collective-permute-done((bf16[4,8,16,512]{3,2,1,0:T(8,128)(2,1)S(1)}, bf16[4,8,16,512]{3,2,1,0:T(8,128)(2,1)S(1)}, u32[]{:S(2)}, u32[]{:S(2)}) %collective-permute-start.16) | collective-permute-done | bytes 524320 | tf_op jit(solution)/shard_map/ppermute | solution.py:228
  116.0 1.5 collective-permute-start.19
  119.6 7.7 %collective-permute-done.20.refs_5_ = bf16[4,8,16,512]{3,2,1,0:T(8,128)(2,1)} collective-permute-done((bf16[4,8,16,512]{3,2,1,0:T(8,128)(2,1)S(1)}, bf16[4,8,16,512]{3,2,1,0:T(8,128)(2,1)}, u32[]{:S(2)}, u32[]{:S(2)}) %collective-permute-start.20) | collective-permute-done | bytes 524320 | tf_op jit(solution)/shard_map/ppermute | solution.py:228
  128.1 10.4 %collective-permute-done.24.refs_6_ = bf16[4,8,16,512]{3,2,1,0:T(8,128)(2,1)} collective-permute-done((bf16[4,8,16,512]{3,2,1,0:T(8,128)(2,1)S(1)}, bf16[4,8,16,512]{3,2,1,0:T(8,128)(2,1)}, u32[]{:S(2)}, u32[]{:S(2)}) %collective-permute-start.24) | collective-permute-done | bytes 524320 | tf_op jit(solution)/shard_map/ppermute | solution.py:228
  138.5 10.8 %collective-permute-done.27.refs_7_ = bf16[4,8,16,512]{3,2,1,0:T(8,128)(2,1)} collective-permute-done((bf16[4,8,16,512]{3,2,1,0:T(8,128)(2,1)S(1)}, bf16[4,8,16,512]{3,2,1,0:T(8,128)(2,1)}, u32[]{:S(2)}, u32[]{:S(2)}) %collective-permute-start.27) | collective-permute-done | bytes 524320 | tf_op jit(solution)/shard_map/ppermute | solution.py:228
  151.7 15.4 %collective-permute-done.29.refs_7_ = bf16[4,8,16,512]{3,2,1,0:T(8,128)(2,1)} collective-permute-done((bf16[4,8,16,512]{3,2,1,0:T(8,128)(2,1)}, bf16[4,8,16,512]{3,2,1,0:T(8,128)(2,1)}, u32[]{:S(2)}, u32[]{:S(2)}) %collective-permute-start.29) | collective-permute-done | bytes 524320 | tf_op jit(solution)/shard_map/ppermute | solution.py:228
  170.4 8.1 %correlate.4 = (bf16[2,8,256,2048]{3,2,1,0:T(8,128)(2,1)}, f32[8,128]{1,0:T(8,128)}) custom-call(s32[3]{0:T(128)S(1)} %get-tuple-element.55.place_ref, bf16[4,8,16,512]{3,2,1,0:T(8,128)(2,1)S(1)} %pad_maximum_fusion.refs_0_.refs_4_, bf16[4,8,16,512]{3,2,1,0:T(8,128)(2,1)S(1)} %pad_maximum_fusion.1.refs_1_.refs_5_, ...), custom_call_target="tpu_custom_call" | custom-call | flops 2147483648 | bytes 10485760 | tf_op jit(solution)/shard_map/correlate/pallas_call | solution.py:178
  183.2 8.2 %correlate.5 = (bf16[2,8,256,2048]{3,2,1,0:T(8,128)(2,1)}, f32[8,128]{1,0:T(8,128)}) custom-call(s32[3]{0:T(128)S(1)} %get-tuple-element.73.place_ref, bf16[4,8,16,512]{3,2,1,0:T(8,128)(2,1)S(1)} %pad_maximum_fusion.refs_0_.refs_4_, bf16[4,8,16,512]{3,2,1,0:T(8,128)(2,1)S(1)} %pad_maximum_fusion.1.refs_1_.refs_5_, ...), custom_call_target="tpu_custom_call", output_to_operand_aliasing={{0}: (13, {})} | custom-call | flops 2147483648 | bytes 10485760 | tf_op jit(solution)/shard_map/correlate/pallas_call | solution.py:178
  191.4 8.6 %correlate.6 = (bf16[2,8,256,2048]{3,2,1,0:T(8,128)(2,1)}, f32[8,128]{1,0:T(8,128)}) custom-call(s32[3]{0:T(128)S(1)} %get-tuple-element.74.place_ref, bf16[4,8,16,512]{3,2,1,0:T(8,128)(2,1)S(1)} %pad_maximum_fusion.refs_0_.refs_4_, bf16[4,8,16,512]{3,2,1,0:T(8,128)(2,1)S(1)} %pad_maximum_fusion.1.refs_1_.refs_5_, ...), custom_call_target="tpu_custom_call", output_to_operand_aliasing={{0}: (13, {})} | custom-call | flops 2147483648 | bytes 10485760 | tf_op jit(solution)/shard_map/correlate/pallas_call | solution.py:178
  200.6 1.4 collective-permute-done.39.refs_11_
  202.7 6.8 %correlate.7 = (bf16[2,8,256,2048]{3,2,1,0:T(8,128)(2,1)}, f32[8,128]{1,0:T(8,128)}) custom-call(s32[3]{0:T(128)S(1)} %get-tuple-element.75.place_ref, bf16[4,8,16,512]{3,2,1,0:T(8,128)(2,1)S(1)} %pad_maximum_fusion.refs_0_.refs_4_, bf16[4,8,16,512]{3,2,1,0:T(8,128)(2,1)S(1)} %pad_maximum_fusion.1.refs_1_.refs_5_, ...), custom_call_target="tpu_custom_call", output_to_operand_aliasing={{0}: (13, {})} | custom-call | flops 2147483648 | bytes 10485760 | tf_op jit(solution)/shard_map/correlate/pallas_call | solution.py:178
  (114 shorter events, 22.1 us)
Async XLA Ops:
  18.6 7.8 %collective-permute-start.1 = (bf16[8,16,512]{2,1,0:T(8,128)(2,1)S(1)}, bf16[8,16,512]{2,1,0:T(8,128)(2,1)S(1)}, u32[]{:S(2)}, u32[]{:S(2)}) collective-permute-start(bf16[8,16,512]{2,1,0:T(8,128)(2,1)S(1)} %get-tuple-element.71), channel_id=1, source_target_pairs={{0,16},{8,24},{16,0},{24,8},{1,17},{9,25},{17,1},{25,9},{2,18},{10... | collective-permute-start | bytes 393224 | tf_op jit(solution)/shard_map/ppermute | solution.py:252
  26.4 14.3 %collective-permute-start.3 = (bf16[4,8,16,512]{3,2,1,0:T(8,128)(2,1)S(1)}, bf16[4,8,16,512]{3,2,1,0:T(8,128)(2,1)S(1)}, u32[]{:S(2)}, u32[]{:S(2)}) collective-permute-start(bf16[4,8,16,512]{3,2,1,0:T(8,128)(2,1)S(1)} %pad_maximum_fusion.refs_0_.refs_4_), channel_id=1, source_target_pairs={{0,1},{1,0},{2,3},{3,2},{4,5},{5,4},{6,7},{7,6},{8,9},{9,8},{10,11... | collective-permute-start | bytes 1572872 | tf_op jit(solution)/shard_map/ppermute | solution.py:234
  26.5 16.2 %collective-permute-start.4 = (bf16[4,8,16,512]{3,2,1,0:T(8,128)(2,1)S(1)}, bf16[4,8,16,512]{3,2,1,0:T(8,128)(2,1)S(1)}, u32[]{:S(2)}, u32[]{:S(2)}) collective-permute-start(bf16[4,8,16,512]{3,2,1,0:T(8,128)(2,1)S(1)} %pad_maximum_fusion.refs_0_.refs_4_), channel_id=1, source_target_pairs={{0,2},{1,3},{2,4},{3,5},{4,6},{5,7},{6,0},{7,1},{8,10},{9,11},{10,... | collective-permute-start | bytes 1572872 | tf_op jit(solution)/shard_map/ppermute | solution.py:228
  44.0 7.8 %collective-permute-start.6 = (bf16[8,16,512]{2,1,0:T(8,128)(2,1)S(1)}, bf16[8,16,512]{2,1,0:T(8,128)(2,1)S(1)}, u32[]{:S(2)}, u32[]{:S(2)}) collective-permute-start(bf16[8,16,512]{2,1,0:T(8,128)(2,1)S(1)} %get-tuple-element.67), channel_id=1, source_target_pairs={{0,16},{8,24},{16,0},{24,8},{1,17},{9,25},{17,1},{25,9},{2,18},{10... | collective-permute-start | bytes 393224 | tf_op jit(solution)/shard_map/ppermute | solution.py:252
  51.9 14.3 %collective-permute-start.8 = (bf16[4,8,16,512]{3,2,1,0:T(8,128)(2,1)S(1)}, bf16[4,8,16,512]{3,2,1,0:T(8,128)(2,1)S(1)}, u32[]{:S(2)}, u32[]{:S(2)}) collective-permute-start(bf16[4,8,16,512]{3,2,1,0:T(8,128)(2,1)S(1)} %pad_maximum_fusion.1.refs_1_.refs_5_), channel_id=1, source_target_pairs={{0,1},{1,0},{2,3},{3,2},{4,5},{5,4},{6,7},{7,6},{8,9},{9,8},{10,11... | collective-permute-start | bytes 1572872 | tf_op jit(solution)/shard_map/ppermute | solution.py:234
  51.9 16.6 %collective-permute-start.9 = (bf16[4,8,16,512]{3,2,1,0:T(8,128)(2,1)S(1)}, bf16[4,8,16,512]{3,2,1,0:T(8,128)(2,1)S(1)}, u32[]{:S(2)}, u32[]{:S(2)}) collective-permute-start(bf16[4,8,16,512]{3,2,1,0:T(8,128)(2,1)S(1)} %collective-permute-done.4.refs_4_), channel_id=1, source_target_pairs={{0,2},{1,3},{2,4},{3,5},{4,6},{5,7},{6,0},{7,1},{8,10},{9,11},{10,... | collective-permute-start | bytes 1572872 | tf_op jit(solution)/shard_map/ppermute | solution.py:228
  52.0 27.3 %collective-permute-start.10 = (bf16[4,8,16,512]{3,2,1,0:T(8,128)(2,1)S(1)}, bf16[4,8,16,512]{3,2,1,0:T(8,128)(2,1)S(1)}, u32[]{:S(2)}, u32[]{:S(2)}) collective-permute-start(bf16[4,8,16,512]{3,2,1,0:T(8,128)(2,1)S(1)} %pad_maximum_fusion.1.refs_1_.refs_5_), channel_id=1, source_target_pairs={{0,2},{1,3},{2,4},{3,5},{4,6},{5,7},{6,0},{7,1},{8,10},{9,11},{10,... | collective-permute-start | bytes 1572872 | tf_op jit(solution)/shard_map/ppermute | solution.py:228
  80.2 7.8 %collective-permute-start.12 = (bf16[8,16,512]{2,1,0:T(8,128)(2,1)S(1)}, bf16[8,16,512]{2,1,0:T(8,128)(2,1)S(1)}, u32[]{:S(2)}, u32[]{:S(2)}) collective-permute-start(bf16[8,16,512]{2,1,0:T(8,128)(2,1)S(1)} %get-tuple-element.63), channel_id=1, source_target_pairs={{0,16},{8,24},{16,0},{24,8},{1,17},{9,25},{17,1},{25,9},{2,18},{10... | collective-permute-start | bytes 393224 | tf_op jit(solution)/shard_map/ppermute | solution.py:252
  88.1 13.8 %collective-permute-start.14 = (bf16[4,8,16,512]{3,2,1,0:T(8,128)(2,1)S(1)}, bf16[4,8,16,512]{3,2,1,0:T(8,128)(2,1)S(1)}, u32[]{:S(2)}, u32[]{:S(2)}) collective-permute-start(bf16[4,8,16,512]{3,2,1,0:T(8,128)(2,1)S(1)} %pad_maximum_fusion.2.refs_2_.refs_6_), channel_id=1, source_target_pairs={{0,1},{1,0},{2,3},{3,2},{4,5},{5,4},{6,7},{7,6},{8,9},{9,8},{10,11... | collective-permute-start | bytes 1572872 | tf_op jit(solution)/shard_map/ppermute | solution.py:234
  88.1 16.6 %collective-permute-start.15 = (bf16[4,8,16,512]{3,2,1,0:T(8,128)(2,1)S(1)}, bf16[4,8,16,512]{3,2,1,0:T(8,128)(2,1)S(1)}, u32[]{:S(2)}, u32[]{:S(2)}) collective-permute-start(bf16[4,8,16,512]{3,2,1,0:T(8,128)(2,1)S(1)} %collective-permute-done.9.refs_4_), channel_id=1, source_target_pairs={{0,2},{1,3},{2,4},{3,5},{4,6},{5,7},{6,0},{7,1},{8,10},{9,11},{10,... | collective-permute-start | bytes 1572872 | tf_op jit(solution)/shard_map/ppermute | solution.py:228
  88.2 27.7 %collective-permute-start.16 = (bf16[4,8,16,512]{3,2,1,0:T(8,128)(2,1)S(1)}, bf16[4,8,16,512]{3,2,1,0:T(8,128)(2,1)S(1)}, u32[]{:S(2)}, u32[]{:S(2)}) collective-permute-start(bf16[4,8,16,512]{3,2,1,0:T(8,128)(2,1)S(1)} %pad_maximum_fusion.2.refs_2_.refs_6_), channel_id=1, source_target_pairs={{0,2},{1,3},{2,4},{3,5},{4,6},{5,7},{6,0},{7,1},{8,10},{9,11},{10,... | collective-permute-start | bytes 1572872 | tf_op jit(solution)/shard_map/ppermute | solution.py:228
  88.3 39.0 %collective-permute-start.20 = (bf16[4,8,16,512]{3,2,1,0:T(8,128)(2,1)S(1)}, bf16[4,8,16,512]{3,2,1,0:T(8,128)(2,1)}, u32[]{:S(2)}, u32[]{:S(2)}) collective-permute-start(bf16[4,8,16,512]{3,2,1,0:T(8,128)(2,1)S(1)} %collective-permute-done.10.refs_5_), channel_id=1, source_target_pairs={{0,2},{1,3},{2,4},{3,5},{4,6},{5,7},{6,0},{7,1},{8,10},{9,11},{10,... | collective-permute-start | bytes 1572872 | tf_op jit(solution)/shard_map/ppermute | solution.py:228
  89.3 30.3 %collective-permute-start.23 = (bf16[4,8,16,512]{3,2,1,0:T(8,128)(2,1)S(1)}, bf16[4,8,16,512]{3,2,1,0:T(8,128)(2,1)S(1)}, u32[]{:S(2)}, u32[]{:S(2)}) collective-permute-start(bf16[4,8,16,512]{3,2,1,0:T(8,128)(2,1)S(1)} %collective-permute-done.10.refs_5_), channel_id=1, source_target_pairs={{0,1},{1,0},{2,3},{3,2},{4,5},{5,4},{6,7},{7,6},{8,9},{9,8},{10,11... | collective-permute-start | bytes 1572872 | tf_op jit(solution)/shard_map/ppermute | solution.py:234
  116.0 11.3 %collective-permute-start.19 = (bf16[8,16,512]{2,1,0:T(8,128)(2,1)S(1)}, bf16[8,16,512]{2,1,0:T(8,128)(2,1)S(1)}, u32[]{:S(2)}, u32[]{:S(2)}) collective-permute-start(bf16[8,16,512]{2,1,0:T(8,128)(2,1)S(1)} %get-tuple-element.58), channel_id=1, source_target_pairs={{0,24},{8,16},{16,8},{24,0},{1,25},{9,17},{17,9},{25,1},{2,26},{10... | collective-permute-start | bytes 393224 | tf_op jit(solution)/shard_map/ppermute | solution.py:252
  117.5 9.8 %collective-permute-start.17 = (bf16[8,16,512]{2,1,0:T(8,128)(2,1)S(1)}, bf16[8,16,512]{2,1,0:T(8,128)(2,1)S(1)}, u32[]{:S(2)}, u32[]{:S(2)}) collective-permute-start(bf16[8,16,512]{2,1,0:T(8,128)(2,1)S(1)} %get-tuple-element.60), channel_id=1, source_target_pairs={{0,8},{8,0},{16,24},{24,16},{1,9},{9,1},{17,25},{25,17},{2,10},{10... | collective-permute-start | bytes 393224 | tf_op jit(solution)/shard_map/ppermute | solution.py:252
  118.7 8.6 %collective-permute-start.18 = (bf16[8,16,512]{2,1,0:T(8,128)(2,1)S(1)}, bf16[8,16,512]{2,1,0:T(8,128)(2,1)S(1)}, u32[]{:S(2)}, u32[]{:S(2)}) collective-permute-start(bf16[8,16,512]{2,1,0:T(8,128)(2,1)S(1)} %get-tuple-element.59), channel_id=1, source_target_pairs={{0,16},{8,24},{16,0},{24,8},{1,17},{9,25},{17,1},{25,9},{2,18},{10... | collective-permute-start | bytes 393224 | tf_op jit(solution)/shard_map/ppermute | solution.py:252
  119.6 19.0 %collective-permute-start.24 = (bf16[4,8,16,512]{3,2,1,0:T(8,128)(2,1)S(1)}, bf16[4,8,16,512]{3,2,1,0:T(8,128)(2,1)}, u32[]{:S(2)}, u32[]{:S(2)}) collective-permute-start(bf16[4,8,16,512]{3,2,1,0:T(8,128)(2,1)S(1)} %collective-permute-done.16.refs_6_), channel_id=1, source_target_pairs={{0,2},{1,3},{2,4},{3,5},{4,6},{5,7},{6,0},{7,1},{8,10},{9,11},{10,... | collective-permute-start | bytes 1572872 | tf_op jit(solution)/shard_map/ppermute | solution.py:228
  127.4 21.9 %collective-permute-start.27 = (bf16[4,8,16,512]{3,2,1,0:T(8,128)(2,1)S(1)}, bf16[4,8,16,512]{3,2,1,0:T(8,128)(2,1)}, u32[]{:S(2)}, u32[]{:S(2)}) collective-permute-start(bf16[4,8,16,512]{3,2,1,0:T(8,128)(2,1)S(1)} %pad_maximum_fusion.3.refs_3_.refs_7_), channel_id=1, source_target_pairs={{0,2},{1,3},{2,4},{3,5},{4,6},{5,7},{6,0},{7,1},{8,10},{9,11},{10,... | collective-permute-start | bytes 1572872 | tf_op jit(solution)/shard_map/ppermute | solution.py:228
  127.5 21.9 %collective-permute-start.28 = (bf16[4,8,16,512]{3,2,1,0:T(8,128)(2,1)S(1)}, bf16[4,8,16,512]{3,2,1,0:T(8,128)(2,1)S(1)}, u32[]{:S(2)}, u32[]{:S(2)}) collective-permute-start(bf16[4,8,16,512]{3,2,1,0:T(8,128)(2,1)S(1)} %collective-permute-done.16.refs_6_), channel_id=1, source_target_pairs={{0,1},{1,0},{2,3},{3,2},{4,5},{5,4},{6,7},{7,6},{8,9},{9,8},{10,11... | collective-permute-start | bytes 1572872 | tf_op jit(solution)/shard_map/ppermute | solution.py:234
  127.5 22.6 %collective-permute-start.21 = (bf16[4,8,16,512]{3,2,1,0:T(8,128)(2,1)S(1)}, bf16[4,8,16,512]{3,2,1,0:T(8,128)(2,1)S(1)}, u32[]{:S(2)}, u32[]{:S(2)}) collective-permute-start(bf16[4,8,16,512]{3,2,1,0:T(8,128)(2,1)S(1)} %collective-permute-done.9.refs_4_), channel_id=1, source_target_pairs={{0,1},{1,0},{2,3},{3,2},{4,5},{5,4},{6,7},{7,6},{8,9},{9,8},{10,11... | collective-permute-start | bytes 1572872 | tf_op jit(solution)/shard_map/ppermute | solution.py:234
  128.0 23.4 %collective-permute-start.25 = (bf16[4,8,16,512]{3,2,1,0:T(8,128)(2,1)}, bf16[4,8,16,512]{3,2,1,0:T(8,128)(2,1)}, u32[]{:S(2)}, u32[]{:S(2)}) collective-permute-start(bf16[4,8,16,512]{3,2,1,0:T(8,128)(2,1)} %collective-permute-done.20.refs_5_), channel_id=1, source_target_pairs={{0,1},{1,0},{2,3},{3,2},{4,5},{5,4},{6,7},{7,6},{8,9},{9,8},{10,11... | collective-permute-start | bytes 1572872 | tf_op jit(solution)/shard_map/ppermute | solution.py:234
  138.5 13.0 %collective-permute-start.30 = (bf16[4,8,16,512]{3,2,1,0:T(8,128)(2,1)}, bf16[4,8,16,512]{3,2,1,0:T(8,128)(2,1)}, u32[]{:S(2)}, u32[]{:S(2)}) collective-permute-start(bf16[4,8,16,512]{3,2,1,0:T(8,128)(2,1)} %collective-permute-done.24.refs_6_), channel_id=1, source_target_pairs={{0,1},{1,0},{2,3},{3,2},{4,5},{5,4},{6,7},{7,6},{8,9},{9,8},{10,11... | collective-permute-start | bytes 1572872 | tf_op jit(solution)/shard_map/ppermute | solution.py:234
  150.2 16.9 %collective-permute-start.29 = (bf16[4,8,16,512]{3,2,1,0:T(8,128)(2,1)}, bf16[4,8,16,512]{3,2,1,0:T(8,128)(2,1)}, u32[]{:S(2)}, u32[]{:S(2)}) collective-permute-start(bf16[4,8,16,512]{3,2,1,0:T(8,128)(2,1)} %collective-permute-done.27.refs_7_), channel_id=1, source_target_pairs={{0,2},{1,3},{2,4},{3,5},{4,6},{5,7},{6,0},{7,1},{8,10},{9,11},{10,... | collective-permute-start | bytes 1572872 | tf_op jit(solution)/shard_map/ppermute | solution.py:228
  150.2 17.0 %collective-permute-start.35 = (bf16[4,8,16,512]{3,2,1,0:T(8,128)(2,1)S(1)}, bf16[4,8,16,512]{3,2,1,0:T(8,128)(2,1)}, u32[]{:S(2)}, u32[]{:S(2)}) collective-permute-start(bf16[4,8,16,512]{3,2,1,0:T(8,128)(2,1)S(1)} %collective-permute-done.4.refs_4_), channel_id=1, source_target_pairs={{0,1},{1,0},{2,3},{3,2},{4,5},{5,4},{6,7},{7,6},{8,9},{9,8},{10,11... | collective-permute-start | bytes 1572872 | tf_op jit(solution)/shard_map/ppermute | solution.py:234
  151.0 16.2 %collective-permute-start.37 = (bf16[4,8,16,512]{3,2,1,0:T(8,128)(2,1)S(1)}, bf16[4,8,16,512]{3,2,1,0:T(8,128)(2,1)}, u32[]{:S(2)}, u32[]{:S(2)}) collective-permute-start(bf16[4,8,16,512]{3,2,1,0:T(8,128)(2,1)S(1)} %pad_maximum_fusion.3.refs_3_.refs_7_), channel_id=1, source_target_pairs={{0,1},{1,0},{2,3},{3,2},{4,5},{5,4},{6,7},{7,6},{8,9},{9,8},{10,11... | collective-permute-start | bytes 1572872 | tf_op jit(solution)/shard_map/ppermute | solution.py:234
  151.5 27.0 %collective-permute-start.22 = (bf16[4,8,16,512]{3,2,1,0:T(8,128)(2,1)}, bf16[4,8,16,512]{3,2,1,0:T(8,128)(2,1)S(1)}, u32[]{:S(2)}, u32[]{:S(2)}) collective-permute-start(bf16[4,8,16,512]{3,2,1,0:T(8,128)(2,1)} %collective-permute-done.20.refs_5_), channel_id=1, source_target_pairs={{0,2},{1,3},{2,4},{3,5},{4,6},{5,7},{6,0},{7,1},{8,10},{9,11},{10,... | collective-permute-start | bytes 1572872 | tf_op jit(solution)/shard_map/ppermute | solution.py:228
  151.5 27.5 %collective-permute-start.36 = (bf16[4,8,16,512]{3,2,1,0:T(8,128)(2,1)}, bf16[4,8,16,512]{3,2,1,0:T(8,128)(2,1)S(1)}, u32[]{:S(2)}, u32[]{:S(2)}) collective-permute-start(bf16[4,8,16,512]{3,2,1,0:T(8,128)(2,1)} %collective-permute-done.27.refs_7_), channel_id=1, source_target_pairs={{0,1},{1,0},{2,3},{3,2},{4,5},{5,4},{6,7},{7,6},{8,9},{9,8},{10,11... | collective-permute-start | bytes 1572872 | tf_op jit(solution)/shard_map/ppermute | solution.py:234
  167.1 24.3 %collective-permute-start.34 = (bf16[4,8,16,512]{3,2,1,0:T(8,128)(2,1)}, bf16[4,8,16,512]{3,2,1,0:T(8,128)(2,1)S(1)}, u32[]{:S(2)}, u32[]{:S(2)}) collective-permute-start(bf16[4,8,16,512]{3,2,1,0:T(8,128)(2,1)} %collective-permute-done.29.refs_7_), channel_id=1, source_target_pairs={{0,1},{1,0},{2,3},{3,2},{4,5},{5,4},{6,7},{7,6},{8,9},{9,8},{10,11... | collective-permute-start | bytes 1572872 | tf_op jit(solution)/shard_map/ppermute | solution.py:234
  167.2 33.3 %collective-permute-start.26 = (bf16[4,8,16,512]{3,2,1,0:T(8,128)(2,1)}, bf16[4,8,16,512]{3,2,1,0:T(8,128)(2,1)S(1)}, u32[]{:S(2)}, u32[]{:S(2)}) collective-permute-start(bf16[4,8,16,512]{3,2,1,0:T(8,128)(2,1)} %collective-permute-done.24.refs_6_), channel_id=1, source_target_pairs={{0,2},{1,3},{2,4},{3,5},{4,6},{5,7},{6,0},{7,1},{8,10},{9,11},{10,... | collective-permute-start | bytes 1572872 | tf_op jit(solution)/shard_map/ppermute | solution.py:228
  167.2 32.8 %collective-permute-start.31 = (bf16[4,8,16,512]{3,2,1,0:T(8,128)(2,1)}, bf16[4,8,16,512]{3,2,1,0:T(8,128)(2,1)S(1)}, u32[]{:S(2)}, u32[]{:S(2)}) collective-permute-start(bf16[4,8,16,512]{3,2,1,0:T(8,128)(2,1)} %collective-permute-done.29.refs_7_), channel_id=1, source_target_pairs={{0,2},{1,3},{2,4},{3,5},{4,6},{5,7},{6,0},{7,1},{8,10},{9,11},{10,... | collective-permute-start | bytes 1572872 | tf_op jit(solution)/shard_map/ppermute | solution.py:228
  178.5 22.1 %collective-permute-start.32 = (bf16[4,8,16,512]{3,2,1,0:T(8,128)(2,1)}, bf16[4,8,16,512]{3,2,1,0:T(8,128)(2,1)S(1)}, u32[]{:S(2)}, u32[]{:S(2)}) collective-permute-start(bf16[4,8,16,512]{3,2,1,0:T(8,128)(2,1)} %copy-done.2), channel_id=1, source_target_pairs={{0,1},{1,0},{2,3},{3,2},{4,5},{5,4},{6,7},{7,6},{8,9},{9,8},{10,11... | collective-permute-start | bytes 1572872 | tf_op jit(solution)/shard_map/ppermute | solution.py:234
  179.0 21.6 %collective-permute-start.33 = (bf16[4,8,16,512]{3,2,1,0:T(8,128)(2,1)S(1)}, bf16[4,8,16,512]{3,2,1,0:T(8,128)(2,1)S(1)}, u32[]{:S(2)}, u32[]{:S(2)}) collective-permute-start(bf16[4,8,16,512]{3,2,1,0:T(8,128)(2,1)S(1)} %collective-permute-done.22.refs_5_), channel_id=1, source_target_pairs={{0,1},{1,0},{2,3},{3,2},{4,5},{5,4},{6,7},{7,6},{8,9},{9,8},{10,11... | collective-permute-start | bytes 1572872 | tf_op jit(solution)/shard_map/ppermute | solution.py:234
  (28 other events, 416.8 us)

commit v4 on v3

--- a/solution.py
+++ b/solution.py
@@ -15,7 +15,7 @@
 S = 256
 GROUP = 16
 T_BLOCK = 37
-T_PARTS = (13, 12, 12)
+MXU = 256
 LANES = 128
 
 
@@ -32,22 +32,47 @@
     return folded.reshape(P_SIZE, -1).astype(jnp.bfloat16)
 
 
+def unit_shares(columns):
+    if columns == MXU:
+        half = T_BLOCK // 2
+        return [(0, half, 0), (half, T_BLOCK, 0)]
+    return [(0, T_BLOCK, 0), (0, T_BLOCK, MXU)]
+
+
 def channelize_kernel(channels, x_ref, w_ref, after_ref, o_ref, y_ref, u_ref, s_ref, z_ref):
     step = pl.program_id(0)
     width = 2 * channels
     halves = LANES // width
     depth = S // halves
-    table = w_ref[...]
-    done = 0
-    for count in T_PARTS:
-        rows = jnp.concatenate(
-            [x_ref[:, t * P_SIZE : (t + 1) * P_SIZE] for t in range(done, done + count)], axis=0
-        )
-        start = pl.multiple_of((step * T_BLOCK + done) * GROUP, GROUP)
-        y_ref[pl.ds(start, count * GROUP), :] = jnp.dot(
-            rows, table, preferred_element_type=jnp.float32
-        )
-        done += count
+    shares = unit_shares(w_ref.shape[1])
+
+    def multiply(*sums):
+        for k in range(P_SIZE // MXU):
+            depths = slice(k * MXU, (k + 1) * MXU)
+            for unit, (begin, end, column) in enumerate(shares):
+                pltpu.matmul_push_rhs(w_ref[depths, column : column + MXU], k % 2, unit)
+            for unit, (begin, end, column) in enumerate(shares):
+                rows = jnp.concatenate(
+                    [
+                        x_ref[:, t * P_SIZE + k * MXU : t * P_SIZE + (k + 1) * MXU]
+                        for t in range(begin, end)
+                    ],
+                    axis=0,
+                )
+                pltpu.matmul_acc_lhs(sums[unit], rows, load_staged_rhs=k % 2)
+        for unit, (begin, end, column) in enumerate(shares):
+            start = pl.multiple_of((step * T_BLOCK + begin) * GROUP, GROUP)
+            y_ref[pl.ds(start, (end - begin) * GROUP), column : column + MXU] = (
+                pltpu.matmul_pop(sums[unit])
+            )
+
+    pl.run_scoped(
+        multiply,
+        *[
+            pltpu.ACC(unit)(((end - begin) * GROUP, MXU), jnp.float32)
+            for unit, (begin, end, column) in enumerate(shares)
+        ],
+    )
 
     @pl.when(step == pl.num_programs(0) - 1)
     def _():
@@ -151,16 +176,34 @@
     left = inputs_of(own)
     turned = jnp.concatenate([left[:, S:], -left[:, :S]], axis=1)
     stacked = jnp.concatenate([left, turned], axis=0)
-    for sources, parity in ((same, core), (other, 1 - core)):
-        products = lax.dot_general(
-            stacked,
-            inputs_of(sources),
-            (((1,), (1,)), ((), ())),
-            preferred_element_type=jnp.float32,
-        ).astype(jnp.bfloat16)
+    rights = [inputs_of(same), inputs_of(other)]
+
+    def keep(products, parity):
+        products = products.astype(jnp.bfloat16)
         column = pl.multiple_of(parity * rows, rows)
         o_ref[0, :, pl.ds(column, rows)] = products[:rows]
         o_ref[1, :, pl.ds(column, rows)] = products[rows:]
+
+    def multiply(*sums):
+        for k in range(2 * S // MXU):
+            depths = slice(k * MXU, (k + 1) * MXU)
+            for unit, right in enumerate(rights):
+                pltpu.matmul_push_rhs(right[:, depths], k % 2, unit, transpose=True)
+            for unit in range(2):
+                pltpu.matmul_acc_lhs(sums[unit], stacked[:, depths], load_staged_rhs=k % 2)
+        for unit, parity in enumerate((core, 1 - core)):
+            keep(pltpu.matmul_pop(sums[unit]), parity)
+
+    if rows == MXU:
+        pl.run_scoped(
+            multiply, *[pltpu.ACC(unit)((2 * rows, MXU), jnp.float32) for unit in range(2)]
+        )
+    else:
+        for right, parity in zip(rights, (core, 1 - core)):
+            products = lax.dot_general(
+                stacked, right, (((1,), (1,)), ((), ())), preferred_element_type=jnp.float32
+            )
+            keep(products, parity)
 
 
 def correlate(place, own, same, other, previous, total_columns):
@@ -234,24 +277,24 @@
             swapped[step, group] = lax.ppermute(piece, "tm", swap)
         return swapped[step, group]
 
+    deep = groups == 4 and ring >= 3
     for group in range(groups):
-        if group:
-            token = behind(token, held[0, group - 1])
+        if deep and group == 2:
+            token = behind(token, held[0, 0])
+        if deep and group == 3:
+            token = behind(token, held[0, 1], held[0, 2], move_on(1, 0))
         spectra = channelize(voltages, table, token, group)
-        if group:
-            spectra = behind(
-                spectra,
-                swap_cores(0, group - 1),
-                *([move_on(group, 0)] if group < ring else []),
-                *([move_on(1, group - 1)] if ring > 1 else []),
-            )
+        token = behind(token, spectra)
+        if deep and group == 3:
+            closed = [swap_cores(0, 0), swap_cores(0, 1)]
+            spectra = behind(spectra, move_on(1, 1), move_on(2, 0), *closed)
         spectra = spectra.reshape(freq_count, CH_DEV, GROUP, 2 * S)
         parts = [spectra[0]]
         for k in range(1, freq_count):
             partners = [(i, i ^ k) for i in range(freq_count)]
             parts.append(lax.ppermute(spectra[k], "freq", partners))
-        if group >= 3 and ring > 2:
-            parts[-1] = behind(parts[-1], move_on(2, group - 2))
+        if deep and group == 3:
+            parts[-1] = behind(parts[-1], move_on(1, 2))
         held[0, group] = jnp.stack(parts)
 
     result, tokens = None, []

time: 212 us -> 205 us (0.967)
  waiting for transfers between devices: 92.5 us -> 73.9 us
  starting transfers between devices: 22.3 us -> 29.3 us
  local copies, waits for them, and re-layouts: 9.69 us -> 12.4 us
    ppermute x12, waiting for transfers between devices: 73.5 us -> 54.3 us  [move_on(): held[step, group] = lax.ppermute(piece, 'tm', onward)]
    ppermute x12, starting transfers between devices: 4.46 us -> 11.8 us  [move_on(): held[step, group] = lax.ppermute(piece, 'tm', onward)]
    unnamed x40, local copies, waits for them, and re-layouts: 8.94 us -> 11.6 us
  transfers between devices with their start and end apart: 40 -> 40, of which waited for: 17 -> 16; matrix products, arithmetic and copies ran while one was open for 0% -> 0% of each run, Pallas kernels for 30% -> 31%
where the time goes in v4:
time: 205 us; the launch traced here: 202 us
  Pallas kernels  83.3 us (41%)
  waiting for transfers between devices  73.9 us (36%)
  starting transfers between devices  29.3 us (14%)
  local copies, waits for them, and re-layouts  12.4 us (6%)
  other arithmetic  2.68 us (1%)
    ppermute x12, waiting for transfers between devices, move_on(): held[step, group] = lax.ppermute(piece, 'tm', onward)  54.3 us
    pallas_call x4, Pallas kernels, channelize(): pl.pallas_call(functools.partial(channelize_kernel, channels), grid=(fram...  50.5 us
    pallas_call x4, Pallas kernels, correlate(): pl.pallas_call(functools.partial(correlate_kernel, groups), grid_spec=plt...  32.8 us
    ppermute x12, waiting for transfers between devices, on_device(): parts.append(lax.ppermute(spectra[k], 'freq', partners))  17.4 us
    ppermute x12, starting transfers between devices, on_device(): parts.append(lax.ppermute(spectra[k], 'freq', partners))  15.2 us
    ppermute x12, starting transfers between devices, move_on(): held[step, group] = lax.ppermute(piece, 'tm', onward)  11.8 us
    unnamed x40, local copies, waits for them, and re-layouts  11.6 us
  transfers between devices with their start and end apart: 40, of which 16 were waited for; matrix products, arithmetic and copies ran while one was open for 0% of the time, Pallas kernels for 31%

profile of v4, /device:TPU:0, one launch (start us, length us, event | category | flops | bytes accessed | tf_op | source)
XLA Modules:
  0.0 201.8 jit_solution(12177727031777949080)
XLA Ops:
  2.9 12.6 %channelize.4 = bf16[32,16,512]{2,1,0:T(8,128)(2,1)S(1)} custom-call(bf16[64,530432]{1,0:T(8,128)(2,1)} %x_ref.7, bf16[2048,256]{1,0:T(8,128)(2,1)S(1)} %copy.7.w_ref, f32[8,128]{1,0:T(8,128)S(1)} %broadcast_in_dim.2.after_ref), custom_call_target="tpu_custom_call" | custom-call | flops 4345298944 | bytes 16973824 | tf_op jit(solution)/shard_map/channelize/pallas_call | solution.py:137
  15.6 3.0 %collective-permute-start = (bf16[8,16,512]{2,1,0:T(8,128)(2,1)S(1)}, bf16[8,16,512]{2,1,0:T(8,128)(2,1)S(1)}, u32[]{:S(2)}, u32[]{:S(2)}) collective-permute-start(bf16[8,16,512]{2,1,0:T(8,128)(2,1)S(1)} %get-tuple-element.72), channel_id=1, source_target_pairs={{0,8},{8,0},{16,24},{24,16},{1,9},{9,1},{17,25},{25,17},{2,10},{10... | collective-permute-start | bytes 393224 | tf_op jit(solution)/shard_map/ppermute | solution.py:295
  18.6 1.5 collective-permute-start.1
  20.1 2.4 %collective-permute-done = bf16[8,16,512]{2,1,0:T(8,128)(2,1)S(1)} collective-permute-done((bf16[8,16,512]{2,1,0:T(8,128)(2,1)S(1)}, bf16[8,16,512]{2,1,0:T(8,128)(2,1)S(1)}, u32[]{:S(2)}, u32[]{:S(2)}) %collective-permute-start) | collective-permute-done | bytes 131104 | tf_op jit(solution)/shard_map/ppermute | solution.py:295
  22.5 3.9 %collective-permute-done.1 = bf16[8,16,512]{2,1,0:T(8,128)(2,1)S(1)} collective-permute-done((bf16[8,16,512]{2,1,0:T(8,128)(2,1)S(1)}, bf16[8,16,512]{2,1,0:T(8,128)(2,1)S(1)}, u32[]{:S(2)}, u32[]{:S(2)}) %collective-permute-start.1) | collective-permute-done | bytes 131104 | tf_op jit(solution)/shard_map/ppermute | solution.py:295
  26.5 1.6 collective-permute-start.9
  28.1 12.6 %channelize.5 = bf16[32,16,512]{2,1,0:T(8,128)(2,1)S(1)} custom-call(bf16[64,530432]{1,0:T(8,128)(2,1)} %x_ref.7, bf16[2048,256]{1,0:T(8,128)(2,1)S(1)} %copy.7.w_ref, f32[8,128]{1,0:T(8,128)S(1)} %broadcast_in_dim.2.after_ref), custom_call_target="tpu_custom_call" | custom-call | flops 4345298944 | bytes 16973824 | tf_op jit(solution)/shard_map/channelize/pallas_call | solution.py:137
  42.9 1.4 collective-permute-start.5
  44.3 2.7 %collective-permute-done.3 = bf16[8,16,512]{2,1,0:T(8,128)(2,1)S(1)} collective-permute-done((bf16[8,16,512]{2,1,0:T(8,128)(2,1)S(1)}, bf16[8,16,512]{2,1,0:T(8,128)(2,1)S(1)}, u32[]{:S(2)}, u32[]{:S(2)}) %collective-permute-start.3) | collective-permute-done | bytes 131104 | tf_op jit(solution)/shard_map/ppermute | solution.py:295
  47.3 1.5 collective-permute-done.5
  48.8 1.6 collective-permute-start.10
  50.4 1.6 collective-permute-start.11
  52.0 12.6 %channelize.6 = bf16[32,16,512]{2,1,0:T(8,128)(2,1)S(1)} custom-call(bf16[64,530432]{1,0:T(8,128)(2,1)} %x_ref.7, bf16[2048,256]{1,0:T(8,128)(2,1)S(1)} %copy.7.w_ref, f32[8,128]{1,0:T(8,128)S(1)} %broadcast_in_dim.2.after_ref), custom_call_target="tpu_custom_call" | custom-call | flops 4345298944 | bytes 16973824 | tf_op jit(solution)/shard_map/channelize/pallas_call | solution.py:137
  64.7 1.6 collective-permute-start.6
  68.3 1.5 collective-permute-done.6
  69.7 1.5 collective-permute-done.7
  71.2 1.4 collective-permute-done.8
  73.6 12.6 %channelize.7 = bf16[32,16,512]{2,1,0:T(8,128)(2,1)S(1)} custom-call(bf16[64,530432]{1,0:T(8,128)(2,1)} %x_ref.7, bf16[2048,256]{1,0:T(8,128)(2,1)S(1)} %copy.7.w_ref, f32[8,128]{1,0:T(8,128)S(1)} %broadcast_in_dim.2.after_ref), custom_call_target="tpu_custom_call" | custom-call | flops 4345298944 | bytes 16973824 | tf_op jit(solution)/shard_map/channelize/pallas_call | solution.py:137
  87.8 1.7 collective-permute-start.14
  90.7 1.5 collective-permute-start.24
  92.2 1.6 collective-permute-start.20
  93.9 2.4 %collective-permute-done.14 = bf16[8,16,512]{2,1,0:T(8,128)(2,1)S(1)} collective-permute-done((bf16[8,16,512]{2,1,0:T(8,128)(2,1)S(1)}, bf16[8,16,512]{2,1,0:T(8,128)(2,1)S(1)}, u32[]{:S(2)}, u32[]{:S(2)}) %collective-permute-start.14) | collective-permute-done | bytes 131104 | tf_op jit(solution)/shard_map/ppermute | solution.py:295
  97.8 9.7 %collective-permute-done.24.refs_6_ = bf16[4,8,16,512]{3,2,1,0:T(8,128)(2,1)} collective-permute-done((bf16[4,8,16,512]{3,2,1,0:T(8,128)(2,1)S(1)}, bf16[4,8,16,512]{3,2,1,0:T(8,128)(2,1)}, u32[]{:S(2)}, u32[]{:S(2)}) %collective-permute-start.24) | collective-permute-done | bytes 524320 | tf_op jit(solution)/shard_map/ppermute | solution.py:271
  107.5 11.1 %collective-permute-done.20.refs_5_ = bf16[4,8,16,512]{3,2,1,0:T(8,128)(2,1)S(1)} collective-permute-done((bf16[4,8,16,512]{3,2,1,0:T(8,128)(2,1)S(1)}, bf16[4,8,16,512]{3,2,1,0:T(8,128)(2,1)S(1)}, u32[]{:S(2)}, u32[]{:S(2)}) %collective-permute-start.20) | collective-permute-done | bytes 524320 | tf_op jit(solution)/shard_map/ppermute | solution.py:271
  118.6 9.9 %collective-permute-done.27.refs_7_ = bf16[4,8,16,512]{3,2,1,0:T(8,128)(2,1)} collective-permute-done((bf16[4,8,16,512]{3,2,1,0:T(8,128)(2,1)S(1)}, bf16[4,8,16,512]{3,2,1,0:T(8,128)(2,1)}, u32[]{:S(2)}, u32[]{:S(2)}) %collective-permute-start.27) | collective-permute-done | bytes 524320 | tf_op jit(solution)/shard_map/ppermute | solution.py:271
  131.9 1.6 collective-permute-start.22
  133.8 12.4 %collective-permute-done.29.refs_7_ = bf16[4,8,16,512]{3,2,1,0:T(8,128)(2,1)} collective-permute-done((bf16[4,8,16,512]{3,2,1,0:T(8,128)(2,1)}, bf16[4,8,16,512]{3,2,1,0:T(8,128)(2,1)}, u32[]{:S(2)}, u32[]{:S(2)}) %collective-permute-start.29) | collective-permute-done | bytes 524320 | tf_op jit(solution)/shard_map/ppermute | solution.py:271
  146.3 11.2 %collective-permute-done.18.refs_4_ = bf16[4,8,16,512]{3,2,1,0:T(8,128)(2,1)} collective-permute-done((bf16[4,8,16,512]{3,2,1,0:T(8,128)(2,1)}, bf16[4,8,16,512]{3,2,1,0:T(8,128)(2,1)}, u32[]{:S(2)}, u32[]{:S(2)}) %collective-permute-start.18) | collective-permute-done | bytes 524320 | tf_op jit(solution)/shard_map/ppermute | solution.py:271
  160.6 8.1 %correlate.4 = (bf16[2,8,256,2048]{3,2,1,0:T(8,128)(2,1)}, f32[8,128]{1,0:T(8,128)}) custom-call(s32[3]{0:T(128)S(1)} %get-tuple-element.55.place_ref, bf16[4,8,16,512]{3,2,1,0:T(8,128)(2,1)S(1)} %pad_maximum_fusion.refs_0_.refs_4_, bf16[4,8,16,512]{3,2,1,0:T(8,128)(2,1)S(1)} %pad_maximum_fusion.1.refs_1_.refs_5_, ...), custom_call_target="tpu_custom_call" | custom-call | flops 2147483648 | bytes 10485760 | tf_op jit(solution)/shard_map/correlate/pallas_call | solution.py:221
  174.4 8.1 %correlate.5 = (bf16[2,8,256,2048]{3,2,1,0:T(8,128)(2,1)}, f32[8,128]{1,0:T(8,128)}) custom-call(s32[3]{0:T(128)S(1)} %get-tuple-element.73.place_ref, bf16[4,8,16,512]{3,2,1,0:T(8,128)(2,1)S(1)} %pad_maximum_fusion.refs_0_.refs_4_, bf16[4,8,16,512]{3,2,1,0:T(8,128)(2,1)S(1)} %pad_maximum_fusion.1.refs_1_.refs_5_, ...), custom_call_target="tpu_custom_call", output_to_operand_aliasing={{0}: (13, {})} | custom-call | flops 2147483648 | bytes 10485760 | tf_op jit(solution)/shard_map/correlate/pallas_call | solution.py:221
  182.5 8.6 %correlate.6 = (bf16[2,8,256,2048]{3,2,1,0:T(8,128)(2,1)}, f32[8,128]{1,0:T(8,128)}) custom-call(s32[3]{0:T(128)S(1)} %get-tuple-element.74.place_ref, bf16[4,8,16,512]{3,2,1,0:T(8,128)(2,1)S(1)} %pad_maximum_fusion.refs_0_.refs_4_, bf16[4,8,16,512]{3,2,1,0:T(8,128)(2,1)S(1)} %pad_maximum_fusion.1.refs_1_.refs_5_, ...), custom_call_target="tpu_custom_call", output_to_operand_aliasing={{0}: (13, {})} | custom-call | flops 2147483648 | bytes 10485760 | tf_op jit(solution)/shard_map/correlate/pallas_call | solution.py:221
  193.8 8.0 %correlate.7 = (bf16[2,8,256,2048]{3,2,1,0:T(8,128)(2,1)}, f32[8,128]{1,0:T(8,128)}) custom-call(s32[3]{0:T(128)S(1)} %get-tuple-element.75.place_ref, bf16[4,8,16,512]{3,2,1,0:T(8,128)(2,1)S(1)} %pad_maximum_fusion.refs_0_.refs_4_, bf16[4,8,16,512]{3,2,1,0:T(8,128)(2,1)S(1)} %pad_maximum_fusion.1.refs_1_.refs_5_, ...), custom_call_target="tpu_custom_call", output_to_operand_aliasing={{0}: (13, {})} | custom-call | flops 2147483648 | bytes 10485760 | tf_op jit(solution)/shard_map/correlate/pallas_call | solution.py:221
  (114 shorter events, 27.9 us)
Async XLA Ops:
  15.6 6.9 %collective-permute-start = (bf16[8,16,512]{2,1,0:T(8,128)(2,1)S(1)}, bf16[8,16,512]{2,1,0:T(8,128)(2,1)S(1)}, u32[]{:S(2)}, u32[]{:S(2)}) collective-permute-start(bf16[8,16,512]{2,1,0:T(8,128)(2,1)S(1)} %get-tuple-element.72), channel_id=1, source_target_pairs={{0,8},{8,0},{16,24},{24,16},{1,9},{9,1},{17,25},{25,17},{2,10},{10... | collective-permute-start | bytes 393224 | tf_op jit(solution)/shard_map/ppermute | solution.py:295
  18.6 7.8 %collective-permute-start.1 = (bf16[8,16,512]{2,1,0:T(8,128)(2,1)S(1)}, bf16[8,16,512]{2,1,0:T(8,128)(2,1)S(1)}, u32[]{:S(2)}, u32[]{:S(2)}) collective-permute-start(bf16[8,16,512]{2,1,0:T(8,128)(2,1)S(1)} %get-tuple-element.71), channel_id=1, source_target_pairs={{0,16},{8,24},{16,0},{24,8},{1,17},{9,25},{17,1},{25,9},{2,18},{10... | collective-permute-start | bytes 393224 | tf_op jit(solution)/shard_map/ppermute | solution.py:295
  20.1 6.3 %collective-permute-start.2 = (bf16[8,16,512]{2,1,0:T(8,128)(2,1)S(1)}, bf16[8,16,512]{2,1,0:T(8,128)(2,1)S(1)}, u32[]{:S(2)}, u32[]{:S(2)}) collective-permute-start(bf16[8,16,512]{2,1,0:T(8,128)(2,1)S(1)} %get-tuple-element.70), channel_id=1, source_target_pairs={{0,24},{8,16},{16,8},{24,0},{1,25},{9,17},{17,9},{25,1},{2,26},{10... | collective-permute-start | bytes 393224 | tf_op jit(solution)/shard_map/ppermute | solution.py:295
  26.5 24.0 %collective-permute-start.9 = (bf16[4,8,16,512]{3,2,1,0:T(8,128)(2,1)S(1)}, bf16[4,8,16,512]{3,2,1,0:T(8,128)(2,1)S(1)}, u32[]{:S(2)}, u32[]{:S(2)}) collective-permute-start(bf16[4,8,16,512]{3,2,1,0:T(8,128)(2,1)S(1)} %pad_maximum_fusion.refs_0_.refs_4_), channel_id=1, source_target_pairs={{0,2},{1,3},{2,4},{3,5},{4,6},{5,7},{6,0},{7,1},{8,10},{9,11},{10,... | collective-permute-start | bytes 1572872 | tf_op jit(solution)/shard_map/ppermute | solution.py:271
  40.8 6.3 %collective-permute-start.3 = (bf16[8,16,512]{2,1,0:T(8,128)(2,1)S(1)}, bf16[8,16,512]{2,1,0:T(8,128)(2,1)S(1)}, u32[]{:S(2)}, u32[]{:S(2)}) collective-permute-start(bf16[8,16,512]{2,1,0:T(8,128)(2,1)S(1)} %get-tuple-element.68), channel_id=1, source_target_pairs={{0,8},{8,0},{16,24},{24,16},{1,9},{9,1},{17,25},{25,17},{2,10},{10... | collective-permute-start | bytes 393224 | tf_op jit(solution)/shard_map/ppermute | solution.py:295
  48.8 24.3 %collective-permute-start.10 = (bf16[4,8,16,512]{3,2,1,0:T(8,128)(2,1)S(1)}, bf16[4,8,16,512]{3,2,1,0:T(8,128)(2,1)S(1)}, u32[]{:S(2)}, u32[]{:S(2)}) collective-permute-start(bf16[4,8,16,512]{3,2,1,0:T(8,128)(2,1)S(1)} %pad_maximum_fusion.1.refs_1_.refs_5_), channel_id=1, source_target_pairs={{0,2},{1,3},{2,4},{3,5},{4,6},{5,7},{6,0},{7,1},{8,10},{9,11},{10,... | collective-permute-start | bytes 1572872 | tf_op jit(solution)/shard_map/ppermute | solution.py:271
  50.4 22.7 %collective-permute-start.11 = (bf16[4,8,16,512]{3,2,1,0:T(8,128)(2,1)S(1)}, bf16[4,8,16,512]{3,2,1,0:T(8,128)(2,1)}, u32[]{:S(2)}, u32[]{:S(2)}) collective-permute-start(bf16[4,8,16,512]{3,2,1,0:T(8,128)(2,1)S(1)} %collective-permute-done.9.refs_4_), channel_id=1, source_target_pairs={{0,2},{1,3},{2,4},{3,5},{4,6},{5,7},{6,0},{7,1},{8,10},{9,11},{10,... | collective-permute-start | bytes 1572872 | tf_op jit(solution)/shard_map/ppermute | solution.py:271
  69.7 16.5 %collective-permute-start.12 = (bf16[4,8,16,512]{3,2,1,0:T(8,128)(2,1)S(1)}, bf16[4,8,16,512]{3,2,1,0:T(8,128)(2,1)S(1)}, u32[]{:S(2)}, u32[]{:S(2)}) collective-permute-start(bf16[4,8,16,512]{3,2,1,0:T(8,128)(2,1)S(1)} %pad_maximum_fusion.refs_0_.refs_4_), channel_id=1, source_target_pairs={{0,1},{1,0},{2,3},{3,2},{4,5},{5,4},{6,7},{7,6},{8,9},{9,8},{10,11... | collective-permute-start | bytes 1572872 | tf_op jit(solution)/shard_map/ppermute | solution.py:277
  71.2 15.1 %collective-permute-start.13 = (bf16[4,8,16,512]{3,2,1,0:T(8,128)(2,1)S(1)}, bf16[4,8,16,512]{3,2,1,0:T(8,128)(2,1)S(1)}, u32[]{:S(2)}, u32[]{:S(2)}) collective-permute-start(bf16[4,8,16,512]{3,2,1,0:T(8,128)(2,1)S(1)} %pad_maximum_fusion.1.refs_1_.refs_5_), channel_id=1, source_target_pairs={{0,1},{1,0},{2,3},{3,2},{4,5},{5,4},{6,7},{7,6},{8,9},{9,8},{10,11... | collective-permute-start | bytes 1572872 | tf_op jit(solution)/shard_map/ppermute | solution.py:277
  72.7 16.8 %collective-permute-start.17 = (bf16[4,8,16,512]{3,2,1,0:T(8,128)(2,1)S(1)}, bf16[4,8,16,512]{3,2,1,0:T(8,128)(2,1)S(1)}, u32[]{:S(2)}, u32[]{:S(2)}) collective-permute-start(bf16[4,8,16,512]{3,2,1,0:T(8,128)(2,1)S(1)} %pad_maximum_fusion.2.refs_2_.refs_6_), channel_id=1, source_target_pairs={{0,2},{1,3},{2,4},{3,5},{4,6},{5,7},{6,0},{7,1},{8,10},{9,11},{10,... | collective-permute-start | bytes 1572872 | tf_op jit(solution)/shard_map/ppermute | solution.py:271
  73.1 19.1 %collective-permute-start.19 = (bf16[4,8,16,512]{3,2,1,0:T(8,128)(2,1)S(1)}, bf16[4,8,16,512]{3,2,1,0:T(8,128)(2,1)S(1)}, u32[]{:S(2)}, u32[]{:S(2)}) collective-permute-start(bf16[4,8,16,512]{3,2,1,0:T(8,128)(2,1)S(1)} %collective-permute-done.9.refs_4_), channel_id=1, source_target_pairs={{0,1},{1,0},{2,3},{3,2},{4,5},{5,4},{6,7},{7,6},{8,9},{9,8},{10,11... | collective-permute-start | bytes 1572872 | tf_op jit(solution)/shard_map/ppermute | solution.py:277
  73.1 16.8 %collective-permute-start.23 = (bf16[4,8,16,512]{3,2,1,0:T(8,128)(2,1)S(1)}, bf16[4,8,16,512]{3,2,1,0:T(8,128)(2,1)S(1)}, u32[]{:S(2)}, u32[]{:S(2)}) collective-permute-start(bf16[4,8,16,512]{3,2,1,0:T(8,128)(2,1)S(1)} %collective-permute-done.10.refs_5_), channel_id=1, source_target_pairs={{0,1},{1,0},{2,3},{3,2},{4,5},{5,4},{6,7},{7,6},{8,9},{9,8},{10,11... | collective-permute-start | bytes 1572872 | tf_op jit(solution)/shard_map/ppermute | solution.py:277
  86.3 7.5 %collective-permute-start.16 = (bf16[8,16,512]{2,1,0:T(8,128)(2,1)S(1)}, bf16[8,16,512]{2,1,0:T(8,128)(2,1)S(1)}, u32[]{:S(2)}, u32[]{:S(2)}) collective-permute-start(bf16[8,16,512]{2,1,0:T(8,128)(2,1)S(1)} %get-tuple-element.58), channel_id=1, source_target_pairs={{0,24},{8,16},{16,8},{24,0},{1,25},{9,17},{17,9},{25,1},{2,26},{10... | collective-permute-start | bytes 393224 | tf_op jit(solution)/shard_map/ppermute | solution.py:295
  87.8 8.4 %collective-permute-start.14 = (bf16[8,16,512]{2,1,0:T(8,128)(2,1)S(1)}, bf16[8,16,512]{2,1,0:T(8,128)(2,1)S(1)}, u32[]{:S(2)}, u32[]{:S(2)}) collective-permute-start(bf16[8,16,512]{2,1,0:T(8,128)(2,1)S(1)} %get-tuple-element.60), channel_id=1, source_target_pairs={{0,8},{8,0},{16,24},{24,16},{1,9},{9,1},{17,25},{25,17},{2,10},{10... | collective-permute-start | bytes 393224 | tf_op jit(solution)/shard_map/ppermute | solution.py:295
  89.5 6.7 %collective-permute-start.15 = (bf16[8,16,512]{2,1,0:T(8,128)(2,1)S(1)}, bf16[8,16,512]{2,1,0:T(8,128)(2,1)S(1)}, u32[]{:S(2)}, u32[]{:S(2)}) collective-permute-start(bf16[8,16,512]{2,1,0:T(8,128)(2,1)S(1)} %get-tuple-element.59), channel_id=1, source_target_pairs={{0,16},{8,24},{16,0},{24,8},{1,17},{9,25},{17,1},{25,9},{2,18},{10... | collective-permute-start | bytes 393224 | tf_op jit(solution)/shard_map/ppermute | solution.py:295
  90.7 16.7 %collective-permute-start.24 = (bf16[4,8,16,512]{3,2,1,0:T(8,128)(2,1)S(1)}, bf16[4,8,16,512]{3,2,1,0:T(8,128)(2,1)}, u32[]{:S(2)}, u32[]{:S(2)}) collective-permute-start(bf16[4,8,16,512]{3,2,1,0:T(8,128)(2,1)S(1)} %collective-permute-done.17.refs_6_), channel_id=1, source_target_pairs={{0,2},{1,3},{2,4},{3,5},{4,6},{5,7},{6,0},{7,1},{8,10},{9,11},{10,... | collective-permute-start | bytes 1572872 | tf_op jit(solution)/shard_map/ppermute | solution.py:271
  92.2 26.4 %collective-permute-start.20 = (bf16[4,8,16,512]{3,2,1,0:T(8,128)(2,1)S(1)}, bf16[4,8,16,512]{3,2,1,0:T(8,128)(2,1)S(1)}, u32[]{:S(2)}, u32[]{:S(2)}) collective-permute-start(bf16[4,8,16,512]{3,2,1,0:T(8,128)(2,1)S(1)} %collective-permute-done.10.refs_5_), channel_id=1, source_target_pairs={{0,2},{1,3},{2,4},{3,5},{4,6},{5,7},{6,0},{7,1},{8,10},{9,11},{10,... | collective-permute-start | bytes 1572872 | tf_op jit(solution)/shard_map/ppermute | solution.py:271
  96.3 32.2 %collective-permute-start.27 = (bf16[4,8,16,512]{3,2,1,0:T(8,128)(2,1)S(1)}, bf16[4,8,16,512]{3,2,1,0:T(8,128)(2,1)}, u32[]{:S(2)}, u32[]{:S(2)}) collective-permute-start(bf16[4,8,16,512]{3,2,1,0:T(8,128)(2,1)S(1)} %pad_maximum_fusion.3.refs_3_.refs_7_), channel_id=1, source_target_pairs={{0,2},{1,3},{2,4},{3,5},{4,6},{5,7},{6,0},{7,1},{8,10},{9,11},{10,... | collective-permute-start | bytes 1572872 | tf_op jit(solution)/shard_map/ppermute | solution.py:271
  97.2 31.3 %collective-permute-start.28 = (bf16[4,8,16,512]{3,2,1,0:T(8,128)(2,1)S(1)}, bf16[4,8,16,512]{3,2,1,0:T(8,128)(2,1)S(1)}, u32[]{:S(2)}, u32[]{:S(2)}) collective-permute-start(bf16[4,8,16,512]{3,2,1,0:T(8,128)(2,1)S(1)} %collective-permute-done.17.refs_6_), channel_id=1, source_target_pairs={{0,1},{1,0},{2,3},{3,2},{4,5},{5,4},{6,7},{7,6},{8,9},{9,8},{10,11... | collective-permute-start | bytes 1572872 | tf_op jit(solution)/shard_map/ppermute | solution.py:277
  97.2 32.1 %collective-permute-start.36 = (bf16[4,8,16,512]{3,2,1,0:T(8,128)(2,1)S(1)}, bf16[4,8,16,512]{3,2,1,0:T(8,128)(2,1)S(1)}, u32[]{:S(2)}, u32[]{:S(2)}) collective-permute-start(bf16[4,8,16,512]{3,2,1,0:T(8,128)(2,1)S(1)} %pad_maximum_fusion.2.refs_2_.refs_6_), channel_id=1, source_target_pairs={{0,1},{1,0},{2,3},{3,2},{4,5},{5,4},{6,7},{7,6},{8,9},{9,8},{10,11... | collective-permute-start | bytes 1572872 | tf_op jit(solution)/shard_map/ppermute | solution.py:277
  107.5 23.7 %collective-permute-start.21 = (bf16[4,8,16,512]{3,2,1,0:T(8,128)(2,1)}, bf16[4,8,16,512]{3,2,1,0:T(8,128)(2,1)S(1)}, u32[]{:S(2)}, u32[]{:S(2)}) collective-permute-start(bf16[4,8,16,512]{3,2,1,0:T(8,128)(2,1)} %collective-permute-done.11.refs_4_), channel_id=1, source_target_pairs={{0,1},{1,0},{2,3},{3,2},{4,5},{5,4},{6,7},{7,6},{8,9},{9,8},{10,11... | collective-permute-start | bytes 1572872 | tf_op jit(solution)/shard_map/ppermute | solution.py:277
  118.6 13.4 %collective-permute-start.30 = (bf16[4,8,16,512]{3,2,1,0:T(8,128)(2,1)}, bf16[4,8,16,512]{3,2,1,0:T(8,128)(2,1)}, u32[]{:S(2)}, u32[]{:S(2)}) collective-permute-start(bf16[4,8,16,512]{3,2,1,0:T(8,128)(2,1)} %collective-permute-done.24.refs_6_), channel_id=1, source_target_pairs={{0,1},{1,0},{2,3},{3,2},{4,5},{5,4},{6,7},{7,6},{8,9},{9,8},{10,11... | collective-permute-start | bytes 1572872 | tf_op jit(solution)/shard_map/ppermute | solution.py:277
  129.4 16.8 %collective-permute-start.29 = (bf16[4,8,16,512]{3,2,1,0:T(8,128)(2,1)}, bf16[4,8,16,512]{3,2,1,0:T(8,128)(2,1)}, u32[]{:S(2)}, u32[]{:S(2)}) collective-permute-start(bf16[4,8,16,512]{3,2,1,0:T(8,128)(2,1)} %collective-permute-done.27.refs_7_), channel_id=1, source_target_pairs={{0,2},{1,3},{2,4},{3,5},{4,6},{5,7},{6,0},{7,1},{8,10},{9,11},{10,... | collective-permute-start | bytes 1572872 | tf_op jit(solution)/shard_map/ppermute | solution.py:271
  130.2 27.2 %collective-permute-start.18 = (bf16[4,8,16,512]{3,2,1,0:T(8,128)(2,1)}, bf16[4,8,16,512]{3,2,1,0:T(8,128)(2,1)}, u32[]{:S(2)}, u32[]{:S(2)}) collective-permute-start(bf16[4,8,16,512]{3,2,1,0:T(8,128)(2,1)} %collective-permute-done.11.refs_4_), channel_id=1, source_target_pairs={{0,2},{1,3},{2,4},{3,5},{4,6},{5,7},{6,0},{7,1},{8,10},{9,11},{10,... | collective-permute-start | bytes 1572872 | tf_op jit(solution)/shard_map/ppermute | solution.py:271
  131.9 25.5 %collective-permute-start.37 = (bf16[4,8,16,512]{3,2,1,0:T(8,128)(2,1)S(1)}, bf16[4,8,16,512]{3,2,1,0:T(8,128)(2,1)}, u32[]{:S(2)}, u32[]{:S(2)}) collective-permute-start(bf16[4,8,16,512]{3,2,1,0:T(8,128)(2,1)S(1)} %pad_maximum_fusion.3.refs_3_.refs_7_), channel_id=1, source_target_pairs={{0,1},{1,0},{2,3},{3,2},{4,5},{5,4},{6,7},{7,6},{8,9},{9,8},{10,11... | collective-permute-start | bytes 1572872 | tf_op jit(solution)/shard_map/ppermute | solution.py:277
  131.9 36.8 %collective-permute-start.22 = (bf16[4,8,16,512]{3,2,1,0:T(8,128)(2,1)S(1)}, bf16[4,8,16,512]{3,2,1,0:T(8,128)(2,1)S(1)}, u32[]{:S(2)}, u32[]{:S(2)}) collective-permute-start(bf16[4,8,16,512]{3,2,1,0:T(8,128)(2,1)S(1)} %collective-permute-done.20.refs_5_), channel_id=1, source_target_pairs={{0,2},{1,3},{2,4},{3,5},{4,6},{5,7},{6,0},{7,1},{8,10},{9,11},{10,... | collective-permute-start | bytes 1572872 | tf_op jit(solution)/shard_map/ppermute | solution.py:271
  133.6 35.2 %collective-permute-start.35 = (bf16[4,8,16,512]{3,2,1,0:T(8,128)(2,1)}, bf16[4,8,16,512]{3,2,1,0:T(8,128)(2,1)S(1)}, u32[]{:S(2)}, u32[]{:S(2)}) collective-permute-start(bf16[4,8,16,512]{3,2,1,0:T(8,128)(2,1)} %collective-permute-done.27.refs_7_), channel_id=1, source_target_pairs={{0,1},{1,0},{2,3},{3,2},{4,5},{5,4},{6,7},{7,6},{8,9},{9,8},{10,11... | collective-permute-start | bytes 1572872 | tf_op jit(solution)/shard_map/ppermute | solution.py:277
  146.2 36.3 %collective-permute-start.34 = (bf16[4,8,16,512]{3,2,1,0:T(8,128)(2,1)}, bf16[4,8,16,512]{3,2,1,0:T(8,128)(2,1)S(1)}, u32[]{:S(2)}, u32[]{:S(2)}) collective-permute-start(bf16[4,8,16,512]{3,2,1,0:T(8,128)(2,1)} %collective-permute-done.29.refs_7_), channel_id=1, source_target_pairs={{0,1},{1,0},{2,3},{3,2},{4,5},{5,4},{6,7},{7,6},{8,9},{9,8},{10,11... | collective-permute-start | bytes 1572872 | tf_op jit(solution)/shard_map/ppermute | solution.py:277
  157.4 33.8 %collective-permute-start.26 = (bf16[4,8,16,512]{3,2,1,0:T(8,128)(2,1)}, bf16[4,8,16,512]{3,2,1,0:T(8,128)(2,1)S(1)}, u32[]{:S(2)}, u32[]{:S(2)}) collective-permute-start(bf16[4,8,16,512]{3,2,1,0:T(8,128)(2,1)} %collective-permute-done.24.refs_6_), channel_id=1, source_target_pairs={{0,2},{1,3},{2,4},{3,5},{4,6},{5,7},{6,0},{7,1},{8,10},{9,11},{10,... | collective-permute-start | bytes 1572872 | tf_op jit(solution)/shard_map/ppermute | solution.py:271
  157.4 33.7 %collective-permute-start.31 = (bf16[4,8,16,512]{3,2,1,0:T(8,128)(2,1)}, bf16[4,8,16,512]{3,2,1,0:T(8,128)(2,1)S(1)}, u32[]{:S(2)}, u32[]{:S(2)}) collective-permute-start(bf16[4,8,16,512]{3,2,1,0:T(8,128)(2,1)} %collective-permute-done.29.refs_7_), channel_id=1, source_target_pairs={{0,2},{1,3},{2,4},{3,5},{4,6},{5,7},{6,0},{7,1},{8,10},{9,11},{10,... | collective-permute-start | bytes 1572872 | tf_op jit(solution)/shard_map/ppermute | solution.py:271
  168.7 23.0 %collective-permute-start.32 = (bf16[4,8,16,512]{3,2,1,0:T(8,128)(2,1)}, bf16[4,8,16,512]{3,2,1,0:T(8,128)(2,1)S(1)}, u32[]{:S(2)}, u32[]{:S(2)}) collective-permute-start(bf16[4,8,16,512]{3,2,1,0:T(8,128)(2,1)} %collective-permute-done.18.refs_4_), channel_id=1, source_target_pairs={{0,1},{1,0},{2,3},{3,2},{4,5},{5,4},{6,7},{7,6},{8,9},{9,8},{10,11... | collective-permute-start | bytes 1572872 | tf_op jit(solution)/shard_map/ppermute | solution.py:277
  168.7 23.0 %collective-permute-start.33 = (bf16[4,8,16,512]{3,2,1,0:T(8,128)(2,1)S(1)}, bf16[4,8,16,512]{3,2,1,0:T(8,128)(2,1)S(1)}, u32[]{:S(2)}, u32[]{:S(2)}) collective-permute-start(bf16[4,8,16,512]{3,2,1,0:T(8,128)(2,1)S(1)} %collective-permute-done.22.refs_5_), channel_id=1, source_target_pairs={{0,1},{1,0},{2,3},{3,2},{4,5},{5,4},{6,7},{7,6},{8,9},{9,8},{10,11... | collective-permute-start | bytes 1572872 | tf_op jit(solution)/shard_map/ppermute | solution.py:277
  (28 other events, 311.9 us)

commit v5 on v4

--- a/solution.py
+++ b/solution.py
@@ -32,6 +32,10 @@
     return folded.reshape(P_SIZE, -1).astype(jnp.bfloat16)
 
 
+def joined(pieces):
+    return jnp.concatenate([piece.astype(jnp.float32) for piece in pieces], axis=0)
+
+
 def unit_shares(columns):
     if columns == MXU:
         half = T_BLOCK // 2
@@ -40,7 +44,7 @@
 
 
 def channelize_kernel(channels, x_ref, w_ref, after_ref, o_ref, y_ref, u_ref, s_ref, z_ref):
-    step = pl.program_id(0)
+    step = pl.program_id(1)
     width = 2 * channels
     halves = LANES // width
     depth = S // halves
@@ -52,14 +56,15 @@
             for unit, (begin, end, column) in enumerate(shares):
                 pltpu.matmul_push_rhs(w_ref[depths, column : column + MXU], k % 2, unit)
             for unit, (begin, end, column) in enumerate(shares):
-                rows = jnp.concatenate(
+                rows = joined(
                     [
                         x_ref[:, t * P_SIZE + k * MXU : t * P_SIZE + (k + 1) * MXU]
                         for t in range(begin, end)
-                    ],
-                    axis=0,
+                    ]
                 )
-                pltpu.matmul_acc_lhs(sums[unit], rows, load_staged_rhs=k % 2)
+                pltpu.matmul_acc_lhs(
+                    sums[unit], rows.astype(jnp.bfloat16), load_staged_rhs=k % 2
+                )
         for unit, (begin, end, column) in enumerate(shares):
             start = pl.multiple_of((step * T_BLOCK + begin) * GROUP, GROUP)
             y_ref[pl.ds(start, (end - begin) * GROUP), column : column + MXU] = (
@@ -74,7 +79,7 @@
         ],
     )
 
-    @pl.when(step == pl.num_programs(0) - 1)
+    @pl.when(step == pl.num_programs(1) - 1)
     def _():
         part = 8
 
@@ -129,21 +134,22 @@
             o_ref[:, :, lanes] = z_ref[part].astype(jnp.bfloat16).reshape(channels, GROUP, LANES)
 
 
-def channelize(voltages, table, after, group):
+def channelize(voltages, table, after, stream, block):
     samples = voltages.shape[1]
     columns = table.shape[1]
     channels = columns // (2 * TAPS)
     frames = samples // P_SIZE
+    groups = block // GROUP
     return pl.pallas_call(
         functools.partial(channelize_kernel, channels),
-        grid=(frames // T_BLOCK,),
+        grid=(groups, frames // T_BLOCK),
         in_specs=[
-            pl.BlockSpec((GROUP, T_BLOCK * P_SIZE), lambda t: (group, t)),
-            pl.BlockSpec((P_SIZE, columns), lambda t: (0, 0)),
+            pl.BlockSpec((GROUP, T_BLOCK * P_SIZE), lambda g, t: (stream * groups + g, t)),
+            pl.BlockSpec((P_SIZE, columns), lambda g, t: (0, 0)),
             pl.BlockSpec(memory_space=pl.ANY),
         ],
-        out_specs=pl.BlockSpec((channels, GROUP, 2 * S), lambda t: (0, 0, 0)),
-        out_shape=jax.ShapeDtypeStruct((channels, GROUP, 2 * S), jnp.bfloat16),
+        out_specs=pl.BlockSpec((channels, GROUP, 2 * S), lambda g, t: (0, g, 0)),
+        out_shape=jax.ShapeDtypeStruct((channels, block, 2 * S), jnp.bfloat16),
         scratch_shapes=[
             pltpu.VMEM((frames * GROUP, columns), jnp.float32),
             pltpu.VMEM((S * 2 * channels // LANES * GROUP, LANES), jnp.float32),
@@ -152,8 +158,8 @@
         ],
         compiler_params=pltpu.CompilerParams(vmem_limit_bytes=40 * 1024 * 1024),
         cost_estimate=pl.CostEstimate(
-            flops=2 * GROUP * samples * columns,
-            bytes_accessed=2 * GROUP * samples,
+            flops=2 * block * samples * columns,
+            bytes_accessed=2 * block * samples,
             transcendentals=0,
         ),
         name="channelize",
@@ -166,17 +172,15 @@
     own, same, other = (refs[i * groups : (i + 1) * groups] for i in range(3))
     freq_count = own[0].shape[0]
     freq, core = place_ref[0], place_ref[1]
-    rows = freq_count * groups * GROUP
+    rows = freq_count * groups * own[0].shape[1]
 
     def inputs_of(sources):
-        return jnp.concatenate(
-            [source[f ^ freq] for f in range(freq_count) for source in sources], axis=0
-        )
+        return joined([source[f ^ freq] for f in range(freq_count) for source in sources])
 
     left = inputs_of(own)
     turned = jnp.concatenate([left[:, S:], -left[:, :S]], axis=1)
-    stacked = jnp.concatenate([left, turned], axis=0)
-    rights = [inputs_of(same), inputs_of(other)]
+    stacked = jnp.concatenate([left, turned], axis=0).astype(jnp.bfloat16)
+    rights = [inputs_of(sources).astype(jnp.bfloat16) for sources in (same, other)]
 
     def keep(products, parity):
         products = products.astype(jnp.bfloat16)
@@ -206,13 +210,13 @@
             keep(products, parity)
 
 
-def correlate(place, own, same, other, previous, total_columns):
+def correlate(place, own, same, other, after, previous, total_columns):
     groups = len(own)
     freq_count, slab, block, depth = own[0].shape
     rows = freq_count * groups * block
     piece = pl.BlockSpec((freq_count, None, block, depth), lambda c, p: (0, c, 0, 0))
-    in_specs = [piece] * (3 * groups)
-    args = [place, *own, *same, *other]
+    in_specs = [piece] * (3 * groups) + [pl.BlockSpec(memory_space=pl.ANY)]
+    args = [place, *own, *same, *other, after]
     aliases = {}
     if previous is not None:
         aliases = {len(args): 0}
@@ -235,11 +239,7 @@
         ],
         input_output_aliases=aliases,
         compiler_params=pltpu.CompilerParams(vmem_limit_bytes=32 * 1024 * 1024),
-        cost_estimate=pl.CostEstimate(
-            flops=2 * slab * 2 * rows * 2 * rows * depth,
-            bytes_accessed=slab * 2 * rows * (3 * depth + 4 * rows),
-            transcendentals=0,
-        ),
+        cost_estimate=pl.CostEstimate(flops=0, bytes_accessed=0, transcendentals=0),
         name="correlate",
     )(*args)
 
@@ -249,76 +249,53 @@
     tm_count = lax.axis_size("tm")
     inputs_here = voltages.shape[0]
     total_columns = inputs_here * freq_count * tm_count
-    groups = inputs_here // GROUP
+    streams = min(2, inputs_here // GROUP)
+    block = inputs_here // streams
     ring = tm_count // 2
     tm = lax.axis_index("tm").astype(jnp.int32)
     freq = lax.axis_index("freq").astype(jnp.int32)
     swap = [(i, i ^ 1) for i in range(tm_count)]
     onward = [(i, (i + 2) % tm_count) for i in range(tm_count)]
 
-    table = folded_table(fir_taps, freq_count)
-    token = jnp.zeros((8, LANES), jnp.float32)
-    held, swapped = {}, {}
-
     def behind(array, *others):
         for other in others:
             array, _ = lax.optimization_barrier((array, other))
         return array
 
-    def move_on(step, group, *others):
-        if (step, group) not in held:
-            piece = behind(held[step - 1, group], *others)
-            held[step, group] = lax.ppermute(piece, "tm", onward)
-        return held[step, group]
-
-    def swap_cores(step, group, *others):
-        if (step, group) not in swapped:
-            piece = behind(held[step, group], *others)
-            swapped[step, group] = lax.ppermute(piece, "tm", swap)
-        return swapped[step, group]
-
-    deep = groups == 4 and ring >= 3
-    for group in range(groups):
-        if deep and group == 2:
-            token = behind(token, held[0, 0])
-        if deep and group == 3:
-            token = behind(token, held[0, 1], held[0, 2], move_on(1, 0))
-        spectra = channelize(voltages, table, token, group)
-        token = behind(token, spectra)
-        if deep and group == 3:
-            closed = [swap_cores(0, 0), swap_cores(0, 1)]
-            spectra = behind(spectra, move_on(1, 1), move_on(2, 0), *closed)
-        spectra = spectra.reshape(freq_count, CH_DEV, GROUP, 2 * S)
+    table = folded_table(fir_taps, freq_count)
+    token = jnp.zeros((8, LANES), jnp.float32)
+    own, early = [], []
+    for stream in range(streams):
+        if stream:
+            token = behind(token, own[0])
+        spectra = channelize(voltages, table, token, stream, block)
+        if stream:
+            early = [lax.ppermute(own[0], "tm", onward)]
+        spectra = spectra.reshape(freq_count, CH_DEV, block, 2 * S)
         parts = [spectra[0]]
         for k in range(1, freq_count):
             partners = [(i, i ^ k) for i in range(freq_count)]
             parts.append(lax.ppermute(spectra[k], "freq", partners))
-        if deep and group == 3:
-            parts[-1] = behind(parts[-1], move_on(1, 2))
-        held[0, group] = jnp.stack(parts)
-
-    result, tokens = None, []
+        if stream:
+            parts[-1] = behind(parts[-1], early[0])
+        own.append(jnp.stack(parts))
+
+    result, held, tokens = None, own, []
     for step in range(ring):
-        for group in range(groups):
-            others = []
-            if step >= 2 and group == groups - 1:
-                others.append(tokens[step - 2])
-            if step >= 2 and group >= 1:
-                others.append(swap_cores(step - 1, group - 1))
-            move_on(step, group, *others)
-        for group in range(groups):
-            late = step == ring - 1 and step >= 1 and group >= groups // 2
-            swap_cores(step, group, *([tokens[step - 1]] if late else []))
-        source = (tm // 2 + ring - step) % ring
-        place = jnp.stack([freq, tm % 2, source])
-        result, token = correlate(
-            place,
-            [held[0, group] for group in range(groups)],
-            [held[step, group] for group in range(groups)],
-            [swapped[step, group] for group in range(groups)],
-            result,
-            total_columns,
-        )
+        if step:
+            moved = []
+            for stream, piece in enumerate(held):
+                if step >= 3 and streams == 2:
+                    piece = behind(piece, tokens[step - 3 + stream])
+                moved.append(early.pop() if early else lax.ppermute(piece, "tm", onward))
+            held = moved
+        other = []
+        for stream, piece in enumerate(held):
+            if step == ring - 1 and step and stream == streams - 1:
+                piece = behind(piece, tokens[-1])
+            other.append(lax.ppermute(piece, "tm", swap))
+        place = jnp.stack([freq, tm % 2, (tm // 2 + ring - step) % ring])
+        result, token = correlate(place, own, held, other, token, result, total_columns)
         tokens.append(token)
     return result
 

time: 205 us -> 209 us (1.020); the launches traced: 202 us -> 208 us
  waiting for transfers between devices: 73.9 us -> 108 us
  starting transfers between devices: 29.3 us -> 14 us
  local copies, waits for them, and re-layouts: 12.4 us -> 2.98 us
  Pallas kernels: 83.3 us -> 80.6 us
    ppermute x28 -> x14, waiting for transfers between devices: 56.5 us -> 86.4 us  [the longest x5 83.8 us: on_device(): moved.append(early.pop() if early else lax.ppermute(piece, 'tm', onward))]
    unnamed x40 -> x4, local copies, waits for them, and re-layouts: 11.6 us -> 2.19 us
    ppermute x28 -> x14, starting transfers between devices: 14.1 us -> 5.87 us  [the longest x5 3.22 us: on_device(): moved.append(early.pop() if early else lax.ppermute(piece, 'tm', onward))]
    ppermute x12 -> x6, starting transfers between devices: 15.2 us -> 8.1 us  [on_device(): parts.append(lax.ppermute(spectra[k], 'freq', partners))]
    ppermute x12 -> x6, waiting for transfers between devices: 17.4 us -> 21.5 us  [on_device(): parts.append(lax.ppermute(spectra[k], 'freq', partners))]
    pallas_call x4 -> x2, Pallas kernels: 50.5 us -> 48.2 us  [channelize(): pl.pallas_call(functools.partial(channelize_kernel, channels), grid=(grou...]
  transfers between devices with their start and end apart: 40 -> 20, of which waited for: 16 -> 11; matrix products, arithmetic and copies ran while one was open for 0% -> 0% of each run, Pallas kernels for 31% -> 24%
where the time goes in v5:
time: 209 us; the launch traced here: 208 us
  waiting for transfers between devices  108 us (52%)
  Pallas kernels  80.6 us (39%)
  starting transfers between devices  14 us (7%)
  local copies, waits for them, and re-layouts  2.98 us (1%)
  other arithmetic  2.67 us (1%)
    ppermute x5, waiting for transfers between devices, on_device(): moved.append(early.pop() if early else lax.ppermute(piece, 'tm', onward))  83.8 us
    pallas_call x2, Pallas kernels, channelize(): pl.pallas_call(functools.partial(channelize_kernel, channels), grid=(grou...  48.2 us
    pallas_call x4, Pallas kernels, correlate(): pl.pallas_call(functools.partial(correlate_kernel, groups), grid_spec=plt...  32.4 us
    ppermute x6, waiting for transfers between devices, on_device(): parts.append(lax.ppermute(spectra[k], 'freq', partners))  21.5 us
    ppermute x6, starting transfers between devices, on_device(): parts.append(lax.ppermute(spectra[k], 'freq', partners))  8.1 us
  transfers between devices with their start and end apart: 20, of which 11 were waited for; matrix products, arithmetic and copies ran while one was open for 0% of the time, Pallas kernels for 24%

profile of v5, /device:TPU:0, one launch (start us, length us, event | category | flops | bytes accessed | tf_op | source)
XLA Modules:
  0.0 208.3 jit_solution(4608827476480933839)
XLA Ops:
  0.2 1.2 cosine_convert_fusion
  1.4 0.9 multiply_convert_fusion
  2.4 0.5 copy.7.w_ref
  2.9 24.1 %channelize.2 = bf16[32,32,512]{2,1,0:T(8,128)(2,1)S(1)} custom-call(bf16[64,530432]{1,0:T(8,128)(2,1)} %x_ref.3, bf16[2048,256]{1,0:T(8,128)(2,1)S(1)} %copy.7.w_ref, f32[8,128]{1,0:T(8,128)S(1)} %broadcast_in_dim.2.after_ref.refs_6_), custom_call_target="tpu_custom_call" | custom-call | flops 8690597888 | bytes 33947648 | tf_op jit(solution)/shard_map/channelize/pallas_call | solution.py:143
  27.1 3.0 %collective-permute-start = (bf16[8,32,512]{2,1,0:T(8,128)(2,1)S(1)}, bf16[8,32,512]{2,1,0:T(8,128)(2,1)S(1)}, u32[]{:S(2)}, u32[]{:S(2)}) collective-permute-start(bf16[8,32,512]{2,1,0:T(8,128)(2,1)S(1)} %get-tuple-element.38), channel_id=1, source_target_pairs={{0,8},{8,0},{16,24},{24,16},{1,9},{9,1},{17,25},{25,17},{2,10},{10... | collective-permute-start | bytes 786440 | tf_op jit(solution)/shard_map/ppermute | solution.py:278
  30.1 1.5 collective-permute-start.1
  31.7 5.6 %collective-permute-done = bf16[8,32,512]{2,1,0:T(8,128)(2,1)S(1)} collective-permute-done((bf16[8,32,512]{2,1,0:T(8,128)(2,1)S(1)}, bf16[8,32,512]{2,1,0:T(8,128)(2,1)S(1)}, u32[]{:S(2)}, u32[]{:S(2)}) %collective-permute-start) | collective-permute-done | bytes 262176 | tf_op jit(solution)/shard_map/ppermute | solution.py:278
  37.3 6.2 %collective-permute-done.1 = bf16[8,32,512]{2,1,0:T(8,128)(2,1)S(1)} collective-permute-done((bf16[8,32,512]{2,1,0:T(8,128)(2,1)S(1)}, bf16[8,32,512]{2,1,0:T(8,128)(2,1)S(1)}, u32[]{:S(2)}, u32[]{:S(2)}) %collective-permute-start.1) | collective-permute-done | bytes 262176 | tf_op jit(solution)/shard_map/ppermute | solution.py:278
  43.7 1.6 collective-permute-start.6
  45.3 24.1 %channelize.3 = bf16[32,32,512]{2,1,0:T(8,128)(2,1)S(1)} custom-call(bf16[64,530432]{1,0:T(8,128)(2,1)} %x_ref.3, bf16[2048,256]{1,0:T(8,128)(2,1)S(1)} %copy.7.w_ref, f32[8,128]{1,0:T(8,128)S(1)} %broadcast_in_dim.2.after_ref.refs_6_), custom_call_target="tpu_custom_call" | custom-call | flops 8690597888 | bytes 33947648 | tf_op jit(solution)/shard_map/channelize/pallas_call | solution.py:143
  69.5 1.6 collective-permute-start.5
  71.1 1.5 collective-permute-start.3
  72.6 0.5 collective-permute-start.4
  73.1 6.7 %collective-permute-done.5 = bf16[8,32,512]{2,1,0:T(8,128)(2,1)S(1)} collective-permute-done((bf16[8,32,512]{2,1,0:T(8,128)(2,1)S(1)}, bf16[8,32,512]{2,1,0:T(8,128)(2,1)S(1)}, u32[]{:S(2)}, u32[]{:S(2)}) %collective-permute-start.5) | collective-permute-done | bytes 262176 | tf_op jit(solution)/shard_map/ppermute | solution.py:278
  79.7 2.1 collective-permute-done.3
  81.8 1.0 collective-permute-done.4
  82.9 1.6 collective-permute-start.11
  84.5 0.5 collective-permute-start.9
  85.1 1.6 collective-permute-start.7
  86.6 24.3 %collective-permute-done.11.refs_3_ = bf16[4,8,32,512]{3,2,1,0:T(8,128)(2,1)} collective-permute-done((bf16[4,8,32,512]{3,2,1,0:T(8,128)(2,1)S(1)}, bf16[4,8,32,512]{3,2,1,0:T(8,128)(2,1)}, u32[]{:S(2)}, u32[]{:S(2)}) %collective-permute-start.11) | collective-permute-done | bytes 1048608 | tf_op jit(solution)/shard_map/ppermute | solution.py:290
  111.0 1.0 copy-done
  112.0 0.5 collective-permute-start.14
  112.6 1.2 copy-done.1
  113.8 8.3 %correlate.4 = (bf16[2,8,256,2048]{3,2,1,0:T(8,128)(2,1)}, f32[8,128]{1,0:T(8,128)S(1)}) custom-call(s32[3]{0:T(128)S(1)} %get-tuple-element.40.place_ref, bf16[4,8,32,512]{3,2,1,0:T(8,128)(2,1)S(1)} %pad_maximum_fusion.refs_0_.refs_2_, bf16[4,8,32,512]{3,2,1,0:T(8,128)(2,1)S(1)} %pad_maximum_fusion.1.refs_1_.refs_3_, ...), custom_call_target="tpu_custom_call" | custom-call | tf_op jit(solution)/shard_map/correlate/pallas_call | solution.py:225
  122.2 11.3 %collective-permute-done.7.refs_2_ = bf16[4,8,32,512]{3,2,1,0:T(8,128)(2,1)} collective-permute-done((bf16[4,8,32,512]{3,2,1,0:T(8,128)(2,1)S(1)}, bf16[4,8,32,512]{3,2,1,0:T(8,128)(2,1)}, u32[]{:S(2)}, u32[]{:S(2)}) %collective-permute-start.7) | collective-permute-done | bytes 1048608 | tf_op jit(solution)/shard_map/ppermute | solution.py:290
  133.4 22.5 %collective-permute-done.12.refs_3_ = bf16[4,8,32,512]{3,2,1,0:T(8,128)(2,1)} collective-permute-done((bf16[4,8,32,512]{3,2,1,0:T(8,128)(2,1)}, bf16[4,8,32,512]{3,2,1,0:T(8,128)(2,1)}, u32[]{:S(2)}, u32[]{:S(2)}) %collective-permute-start.12) | collective-permute-done | bytes 1048608 | tf_op jit(solution)/shard_map/ppermute | solution.py:290
  155.9 8.8 %correlate.5 = (bf16[2,8,256,2048]{3,2,1,0:T(8,128)(2,1)}, f32[8,128]{1,0:T(8,128)S(1)}) custom-call(s32[3]{0:T(128)S(1)} %get-tuple-element.39.place_ref, bf16[4,8,32,512]{3,2,1,0:T(8,128)(2,1)S(1)} %pad_maximum_fusion.refs_0_.refs_2_, bf16[4,8,32,512]{3,2,1,0:T(8,128)(2,1)S(1)} %pad_maximum_fusion.1.refs_1_.refs_3_, ...), custom_call_target="tpu_custom_call", output_to_operand_aliasing={{0}: (8, {})} | custom-call | tf_op jit(solution)/shard_map/correlate/pallas_call | solution.py:225
  164.7 13.5 %collective-permute-done.10.refs_2_ = bf16[4,8,32,512]{3,2,1,0:T(8,128)(2,1)S(1)} collective-permute-done((bf16[4,8,32,512]{3,2,1,0:T(8,128)(2,1)}, bf16[4,8,32,512]{3,2,1,0:T(8,128)(2,1)S(1)}, u32[]{:S(2)}, u32[]{:S(2)}) %collective-permute-start.10) | collective-permute-done | bytes 1048608 | tf_op jit(solution)/shard_map/ppermute | solution.py:290
  178.3 8.6 %correlate.6 = (bf16[2,8,256,2048]{3,2,1,0:T(8,128)(2,1)}, f32[8,128]{1,0:T(8,128)S(1)}) custom-call(s32[3]{0:T(128)S(1)} %get-tuple-element.29.place_ref, bf16[4,8,32,512]{3,2,1,0:T(8,128)(2,1)S(1)} %pad_maximum_fusion.refs_0_.refs_2_, bf16[4,8,32,512]{3,2,1,0:T(8,128)(2,1)S(1)} %pad_maximum_fusion.1.refs_1_.refs_3_, ...), custom_call_target="tpu_custom_call", output_to_operand_aliasing={{0}: (8, {})} | custom-call | tf_op jit(solution)/shard_map/correlate/pallas_call | solution.py:225
  186.8 12.1 %collective-permute-done.15.refs_3_ = bf16[4,8,32,512]{3,2,1,0:T(8,128)(2,1)S(1)} collective-permute-done((bf16[4,8,32,512]{3,2,1,0:T(8,128)(2,1)}, bf16[4,8,32,512]{3,2,1,0:T(8,128)(2,1)S(1)}, u32[]{:S(2)}, u32[]{:S(2)}) %collective-permute-start.15) | collective-permute-done | bytes 1048608 | tf_op jit(solution)/shard_map/ppermute | solution.py:290
  199.0 2.7 %collective-permute-done.19.refs_5_ = bf16[4,8,32,512]{3,2,1,0:T(8,128)(2,1)S(1)} collective-permute-done((bf16[4,8,32,512]{3,2,1,0:T(8,128)(2,1)S(1)}, bf16[4,8,32,512]{3,2,1,0:T(8,128)(2,1)S(1)}, u32[]{:S(2)}, u32[]{:S(2)}) %collective-permute-start.19) | collective-permute-done | bytes 1048608 | tf_op jit(solution)/shard_map/ppermute | solution.py:296
  201.7 6.7 %correlate.7 = (bf16[2,8,256,2048]{3,2,1,0:T(8,128)(2,1)}, f32[8,128]{1,0:T(8,128)}) custom-call(s32[3]{0:T(128)S(1)} %get-tuple-element.41.place_ref, bf16[4,8,32,512]{3,2,1,0:T(8,128)(2,1)S(1)} %pad_maximum_fusion.refs_0_.refs_2_, bf16[4,8,32,512]{3,2,1,0:T(8,128)(2,1)S(1)} %pad_maximum_fusion.1.refs_1_.refs_3_, ...), custom_call_target="tpu_custom_call", output_to_operand_aliasing={{0}: (8, {})} | custom-call | tf_op jit(solution)/shard_map/correlate/pallas_call | solution.py:225
  (32 shorter events, 0.9 us)
Async XLA Ops:
  27.1 10.1 %collective-permute-start = (bf16[8,32,512]{2,1,0:T(8,128)(2,1)S(1)}, bf16[8,32,512]{2,1,0:T(8,128)(2,1)S(1)}, u32[]{:S(2)}, u32[]{:S(2)}) collective-permute-start(bf16[8,32,512]{2,1,0:T(8,128)(2,1)S(1)} %get-tuple-element.38), channel_id=1, source_target_pairs={{0,8},{8,0},{16,24},{24,16},{1,9},{9,1},{17,25},{25,17},{2,10},{10... | collective-permute-start | bytes 786440 | tf_op jit(solution)/shard_map/ppermute | solution.py:278
  30.1 13.4 %collective-permute-start.1 = (bf16[8,32,512]{2,1,0:T(8,128)(2,1)S(1)}, bf16[8,32,512]{2,1,0:T(8,128)(2,1)S(1)}, u32[]{:S(2)}, u32[]{:S(2)}) collective-permute-start(bf16[8,32,512]{2,1,0:T(8,128)(2,1)S(1)} %get-tuple-element.37), channel_id=1, source_target_pairs={{0,16},{8,24},{16,0},{24,8},{1,17},{9,25},{17,1},{25,9},{2,18},{10... | collective-permute-start | bytes 786440 | tf_op jit(solution)/shard_map/ppermute | solution.py:278
  31.7 11.9 %collective-permute-start.2 = (bf16[8,32,512]{2,1,0:T(8,128)(2,1)S(1)}, bf16[8,32,512]{2,1,0:T(8,128)(2,1)S(1)}, u32[]{:S(2)}, u32[]{:S(2)}) collective-permute-start(bf16[8,32,512]{2,1,0:T(8,128)(2,1)S(1)} %get-tuple-element.36), channel_id=1, source_target_pairs={{0,24},{8,16},{16,8},{24,0},{1,25},{9,17},{17,9},{25,1},{2,26},{10... | collective-permute-start | bytes 786440 | tf_op jit(solution)/shard_map/ppermute | solution.py:278
  43.7 36.1 %collective-permute-start.6 = (bf16[4,8,32,512]{3,2,1,0:T(8,128)(2,1)S(1)}, bf16[4,8,32,512]{3,2,1,0:T(8,128)(2,1)S(1)}, u32[]{:S(2)}, u32[]{:S(2)}) collective-permute-start(bf16[4,8,32,512]{3,2,1,0:T(8,128)(2,1)S(1)} %pad_maximum_fusion.refs_0_.refs_2_), channel_id=1, source_target_pairs={{0,2},{1,3},{2,4},{3,5},{4,6},{5,7},{6,0},{7,1},{8,10},{9,11},{10,... | collective-permute-start | bytes 3145736 | tf_op jit(solution)/shard_map/ppermute | solution.py:273
  69.5 10.2 %collective-permute-start.5 = (bf16[8,32,512]{2,1,0:T(8,128)(2,1)S(1)}, bf16[8,32,512]{2,1,0:T(8,128)(2,1)S(1)}, u32[]{:S(2)}, u32[]{:S(2)}) collective-permute-start(bf16[8,32,512]{2,1,0:T(8,128)(2,1)S(1)} %get-tuple-element.32), channel_id=1, source_target_pairs={{0,24},{8,16},{16,8},{24,0},{1,25},{9,17},{17,9},{25,1},{2,26},{10... | collective-permute-start | bytes 786440 | tf_op jit(solution)/shard_map/ppermute | solution.py:278
  71.1 10.7 %collective-permute-start.3 = (bf16[8,32,512]{2,1,0:T(8,128)(2,1)S(1)}, bf16[8,32,512]{2,1,0:T(8,128)(2,1)S(1)}, u32[]{:S(2)}, u32[]{:S(2)}) collective-permute-start(bf16[8,32,512]{2,1,0:T(8,128)(2,1)S(1)} %get-tuple-element.34), channel_id=1, source_target_pairs={{0,8},{8,0},{16,24},{24,16},{1,9},{9,1},{17,25},{25,17},{2,10},{10... | collective-permute-start | bytes 786440 | tf_op jit(solution)/shard_map/ppermute | solution.py:278
  72.6 10.2 %collective-permute-start.4 = (bf16[8,32,512]{2,1,0:T(8,128)(2,1)S(1)}, bf16[8,32,512]{2,1,0:T(8,128)(2,1)S(1)}, u32[]{:S(2)}, u32[]{:S(2)}) collective-permute-start(bf16[8,32,512]{2,1,0:T(8,128)(2,1)S(1)} %get-tuple-element.33), channel_id=1, source_target_pairs={{0,16},{8,24},{16,0},{24,8},{1,17},{9,25},{17,1},{25,9},{2,18},{10... | collective-permute-start | bytes 786440 | tf_op jit(solution)/shard_map/ppermute | solution.py:278
  82.9 28.1 %collective-permute-start.11 = (bf16[4,8,32,512]{3,2,1,0:T(8,128)(2,1)S(1)}, bf16[4,8,32,512]{3,2,1,0:T(8,128)(2,1)}, u32[]{:S(2)}, u32[]{:S(2)}) collective-permute-start(bf16[4,8,32,512]{3,2,1,0:T(8,128)(2,1)S(1)} %pad_maximum_fusion.1.refs_1_.refs_3_), channel_id=1, source_target_pairs={{0,2},{1,3},{2,4},{3,5},{4,6},{5,7},{6,0},{7,1},{8,10},{9,11},{10,... | collective-permute-start | bytes 3145736 | tf_op jit(solution)/shard_map/ppermute | solution.py:290
  84.5 26.4 %collective-permute-start.8 = (bf16[4,8,32,512]{3,2,1,0:T(8,128)(2,1)S(1)}, bf16[4,8,32,512]{3,2,1,0:T(8,128)(2,1)S(1)}, u32[]{:S(2)}, u32[]{:S(2)}) collective-permute-start(bf16[4,8,32,512]{3,2,1,0:T(8,128)(2,1)S(1)} %pad_maximum_fusion.refs_0_.refs_2_), channel_id=1, source_target_pairs={{0,1},{1,0},{2,3},{3,2},{4,5},{5,4},{6,7},{7,6},{8,9},{9,8},{10,11... | collective-permute-start | bytes 3145736 | tf_op jit(solution)/shard_map/ppermute | solution.py:296
  84.5 28.1 %collective-permute-start.9 = (bf16[4,8,32,512]{3,2,1,0:T(8,128)(2,1)S(1)}, bf16[4,8,32,512]{3,2,1,0:T(8,128)(2,1)}, u32[]{:S(2)}, u32[]{:S(2)}) collective-permute-start(bf16[4,8,32,512]{3,2,1,0:T(8,128)(2,1)S(1)} %pad_maximum_fusion.1.refs_1_.refs_3_), channel_id=1, source_target_pairs={{0,1},{1,0},{2,3},{3,2},{4,5},{5,4},{6,7},{7,6},{8,9},{9,8},{10,11... | collective-permute-start | bytes 3145736 | tf_op jit(solution)/shard_map/ppermute | solution.py:296
  85.1 48.4 %collective-permute-start.7 = (bf16[4,8,32,512]{3,2,1,0:T(8,128)(2,1)S(1)}, bf16[4,8,32,512]{3,2,1,0:T(8,128)(2,1)}, u32[]{:S(2)}, u32[]{:S(2)}) collective-permute-start(bf16[4,8,32,512]{3,2,1,0:T(8,128)(2,1)S(1)} %collective-permute-done.6.refs_2_), channel_id=1, source_target_pairs={{0,2},{1,3},{2,4},{3,5},{4,6},{5,7},{6,0},{7,1},{8,10},{9,11},{10,... | collective-permute-start | bytes 3145736 | tf_op jit(solution)/shard_map/ppermute | solution.py:290
  111.0 44.9 %collective-permute-start.12 = (bf16[4,8,32,512]{3,2,1,0:T(8,128)(2,1)}, bf16[4,8,32,512]{3,2,1,0:T(8,128)(2,1)}, u32[]{:S(2)}, u32[]{:S(2)}) collective-permute-start(bf16[4,8,32,512]{3,2,1,0:T(8,128)(2,1)} %collective-permute-done.11.refs_3_), channel_id=1, source_target_pairs={{0,2},{1,3},{2,4},{3,5},{4,6},{5,7},{6,0},{7,1},{8,10},{9,11},{10,... | collective-permute-start | bytes 3145736 | tf_op jit(solution)/shard_map/ppermute | solution.py:290
  111.0 44.9 %collective-permute-start.13 = (bf16[4,8,32,512]{3,2,1,0:T(8,128)(2,1)S(1)}, bf16[4,8,32,512]{3,2,1,0:T(8,128)(2,1)}, u32[]{:S(2)}, u32[]{:S(2)}) collective-permute-start(bf16[4,8,32,512]{3,2,1,0:T(8,128)(2,1)S(1)} %collective-permute-done.6.refs_2_), channel_id=1, source_target_pairs={{0,1},{1,0},{2,3},{3,2},{4,5},{5,4},{6,7},{7,6},{8,9},{9,8},{10,11... | collective-permute-start | bytes 3145736 | tf_op jit(solution)/shard_map/ppermute | solution.py:296
  111.0 1.0 copy-start
  112.0 44.0 %collective-permute-start.14 = (bf16[4,8,32,512]{3,2,1,0:T(8,128)(2,1)}, bf16[4,8,32,512]{3,2,1,0:T(8,128)(2,1)}, u32[]{:S(2)}, u32[]{:S(2)}) collective-permute-start(bf16[4,8,32,512]{3,2,1,0:T(8,128)(2,1)} %collective-permute-done.11.refs_3_), channel_id=1, source_target_pairs={{0,1},{1,0},{2,3},{3,2},{4,5},{5,4},{6,7},{7,6},{8,9},{9,8},{10,11... | collective-permute-start | bytes 3145736 | tf_op jit(solution)/shard_map/ppermute | solution.py:296
  112.6 1.2 copy-start.1
  133.4 44.8 %collective-permute-start.10 = (bf16[4,8,32,512]{3,2,1,0:T(8,128)(2,1)}, bf16[4,8,32,512]{3,2,1,0:T(8,128)(2,1)S(1)}, u32[]{:S(2)}, u32[]{:S(2)}) collective-permute-start(bf16[4,8,32,512]{3,2,1,0:T(8,128)(2,1)} %collective-permute-done.7.refs_2_), channel_id=1, source_target_pairs={{0,2},{1,3},{2,4},{3,5},{4,6},{5,7},{6,0},{7,1},{8,10},{9,11},{10,... | collective-permute-start | bytes 3145736 | tf_op jit(solution)/shard_map/ppermute | solution.py:290
  133.4 44.8 %collective-permute-start.17 = (bf16[4,8,32,512]{3,2,1,0:T(8,128)(2,1)}, bf16[4,8,32,512]{3,2,1,0:T(8,128)(2,1)S(1)}, u32[]{:S(2)}, u32[]{:S(2)}) collective-permute-start(bf16[4,8,32,512]{3,2,1,0:T(8,128)(2,1)} %collective-permute-done.7.refs_2_), channel_id=1, source_target_pairs={{0,1},{1,0},{2,3},{3,2},{4,5},{5,4},{6,7},{7,6},{8,9},{9,8},{10,11... | collective-permute-start | bytes 3145736 | tf_op jit(solution)/shard_map/ppermute | solution.py:296
  155.9 22.4 %collective-permute-start.18 = (bf16[4,8,32,512]{3,2,1,0:T(8,128)(2,1)}, bf16[4,8,32,512]{3,2,1,0:T(8,128)(2,1)S(1)}, u32[]{:S(2)}, u32[]{:S(2)}) collective-permute-start(bf16[4,8,32,512]{3,2,1,0:T(8,128)(2,1)} %collective-permute-done.12.refs_3_), channel_id=1, source_target_pairs={{0,1},{1,0},{2,3},{3,2},{4,5},{5,4},{6,7},{7,6},{8,9},{9,8},{10,11... | collective-permute-start | bytes 3145736 | tf_op jit(solution)/shard_map/ppermute | solution.py:296
  164.7 34.3 %collective-permute-start.15 = (bf16[4,8,32,512]{3,2,1,0:T(8,128)(2,1)}, bf16[4,8,32,512]{3,2,1,0:T(8,128)(2,1)S(1)}, u32[]{:S(2)}, u32[]{:S(2)}) collective-permute-start(bf16[4,8,32,512]{3,2,1,0:T(8,128)(2,1)} %collective-permute-done.12.refs_3_), channel_id=1, source_target_pairs={{0,2},{1,3},{2,4},{3,5},{4,6},{5,7},{6,0},{7,1},{8,10},{9,11},{10,... | collective-permute-start | bytes 3145736 | tf_op jit(solution)/shard_map/ppermute | solution.py:290
  178.3 20.7 %collective-permute-start.16 = (bf16[4,8,32,512]{3,2,1,0:T(8,128)(2,1)S(1)}, bf16[4,8,32,512]{3,2,1,0:T(8,128)(2,1)S(1)}, u32[]{:S(2)}, u32[]{:S(2)}) collective-permute-start(bf16[4,8,32,512]{3,2,1,0:T(8,128)(2,1)S(1)} %collective-permute-done.10.refs_2_), channel_id=1, source_target_pairs={{0,1},{1,0},{2,3},{3,2},{4,5},{5,4},{6,7},{7,6},{8,9},{9,8},{10,11... | collective-permute-start | bytes 3145736 | tf_op jit(solution)/shard_map/ppermute | solution.py:296
  199.0 2.7 %collective-permute-start.19 = (bf16[4,8,32,512]{3,2,1,0:T(8,128)(2,1)S(1)}, bf16[4,8,32,512]{3,2,1,0:T(8,128)(2,1)S(1)}, u32[]{:S(2)}, u32[]{:S(2)}) collective-permute-start(bf16[4,8,32,512]{3,2,1,0:T(8,128)(2,1)S(1)} %collective-permute-done.15.refs_3_), channel_id=1, source_target_pairs={{0,1},{1,0},{2,3},{3,2},{4,5},{5,4},{6,7},{7,6},{8,9},{9,8},{10,11... | collective-permute-start | bytes 3145736 | tf_op jit(solution)/shard_map/ppermute | solution.py:296

commit v6 on v5

--- a/solution.py
+++ b/solution.py
@@ -16,6 +16,9 @@
 GROUP = 16
 T_BLOCK = 37
 MXU = 256
+SLOTS = 4
+PARTS = ((0, 10), (10, 19), (19, 28), (28, 37))
+CH_STEP = 2
 LANES = 128
 
 
@@ -43,8 +46,40 @@
     return [(0, T_BLOCK, 0), (0, T_BLOCK, MXU)]
 
 
-def channelize_kernel(channels, x_ref, w_ref, after_ref, o_ref, y_ref, u_ref, s_ref, z_ref):
+def channelize_kernel(
+    channels, first_group, x_hbm, w_ref, after_ref, o_ref, y_ref, u_ref, s_ref, z_ref, x_ref, sems
+):
     step = pl.program_id(1)
+    steps = pl.num_programs(1)
+    count = pl.num_programs(0) * steps
+    now = pl.program_id(0) * steps + step
+
+    def copies(block):
+        slot = lax.rem(block, SLOTS)
+        row = pl.multiple_of((first_group + lax.div(block, steps)) * GROUP, GROUP)
+        for part, (begin, end) in enumerate(PARTS):
+            lane = (lax.rem(block, steps) * T_BLOCK + begin) * P_SIZE
+            start = pl.multiple_of(lane, P_SIZE)
+            yield pltpu.make_async_copy(
+                x_hbm.at[pl.ds(row, GROUP), pl.ds(start, (end - begin) * P_SIZE)],
+                x_ref.at[slot, :, pl.ds(begin * P_SIZE, (end - begin) * P_SIZE)],
+                sems.at[slot, part],
+            )
+
+    @pl.when(now == 0)
+    def _():
+        for block in range(SLOTS - 1):
+            for copy in copies(block):
+                copy.start()
+
+    @pl.when(now + SLOTS - 1 < count)
+    def _():
+        for copy in copies(now + SLOTS - 1):
+            copy.start()
+
+    for copy in copies(now):
+        copy.wait()
+    slot = lax.rem(now, SLOTS)
     width = 2 * channels
     halves = LANES // width
     depth = S // halves
@@ -58,7 +93,7 @@
             for unit, (begin, end, column) in enumerate(shares):
                 rows = joined(
                     [
-                        x_ref[:, t * P_SIZE + k * MXU : t * P_SIZE + (k + 1) * MXU]
+                        x_ref[slot, :, t * P_SIZE + k * MXU : t * P_SIZE + (k + 1) * MXU]
                         for t in range(begin, end)
                     ]
                 )
@@ -79,7 +114,7 @@
         ],
     )
 
-    @pl.when(step == pl.num_programs(1) - 1)
+    @pl.when(step == steps - 1)
     def _():
         part = 8
 
@@ -134,88 +169,105 @@
             o_ref[:, :, lanes] = z_ref[part].astype(jnp.bfloat16).reshape(channels, GROUP, LANES)
 
 
-def channelize(voltages, table, after, stream, block):
+def channelize(voltages, table, after, first_group, groups):
     samples = voltages.shape[1]
     columns = table.shape[1]
     channels = columns // (2 * TAPS)
     frames = samples // P_SIZE
-    groups = block // GROUP
     return pl.pallas_call(
-        functools.partial(channelize_kernel, channels),
+        functools.partial(channelize_kernel, channels, first_group),
         grid=(groups, frames // T_BLOCK),
         in_specs=[
-            pl.BlockSpec((GROUP, T_BLOCK * P_SIZE), lambda g, t: (stream * groups + g, t)),
+            pl.BlockSpec(memory_space=pl.ANY),
             pl.BlockSpec((P_SIZE, columns), lambda g, t: (0, 0)),
             pl.BlockSpec(memory_space=pl.ANY),
         ],
         out_specs=pl.BlockSpec((channels, GROUP, 2 * S), lambda g, t: (0, g, 0)),
-        out_shape=jax.ShapeDtypeStruct((channels, block, 2 * S), jnp.bfloat16),
+        out_shape=jax.ShapeDtypeStruct((channels, groups * GROUP, 2 * S), jnp.bfloat16),
         scratch_shapes=[
             pltpu.VMEM((frames * GROUP, columns), jnp.float32),
             pltpu.VMEM((S * 2 * channels // LANES * GROUP, LANES), jnp.float32),
             pltpu.VMEM((GROUP, LANES), jnp.float32),
             pltpu.VMEM((2 * S // LANES, channels * GROUP, LANES), jnp.float32),
+            pltpu.VMEM((SLOTS, GROUP, T_BLOCK * P_SIZE), jnp.bfloat16),
+            pltpu.SemaphoreType.DMA((SLOTS, len(PARTS))),
         ],
         compiler_params=pltpu.CompilerParams(vmem_limit_bytes=40 * 1024 * 1024),
         cost_estimate=pl.CostEstimate(
-            flops=2 * block * samples * columns,
-            bytes_accessed=2 * block * samples,
+            flops=2 * groups * GROUP * samples * columns,
+            bytes_accessed=2 * groups * GROUP * samples,
             transcendentals=0,
         ),
         name="channelize",
     )(voltages, table, after)
 
 
-def correlate_kernel(groups, place_ref, *refs):
+def correlate_kernel(streams, place_ref, *refs):
     o_ref, token_ref = refs[-2:]
     token_ref[...] = jnp.zeros_like(token_ref)
-    own, same, other = (refs[i * groups : (i + 1) * groups] for i in range(3))
-    freq_count = own[0].shape[0]
+    own, same, other = (refs[i * streams : (i + 1) * streams] for i in range(3))
+    freq_count, channels = own[0].shape[1:3]
     freq, core = place_ref[0], place_ref[1]
-    rows = freq_count * groups * own[0].shape[1]
-
-    def inputs_of(sources):
-        return joined([source[f ^ freq] for f in range(freq_count) for source in sources])
-
-    left = inputs_of(own)
-    turned = jnp.concatenate([left[:, S:], -left[:, :S]], axis=1)
-    stacked = jnp.concatenate([left, turned], axis=0).astype(jnp.bfloat16)
-    rights = [inputs_of(sources).astype(jnp.bfloat16) for sources in (same, other)]
-
-    def keep(products, parity):
-        products = products.astype(jnp.bfloat16)
-        column = pl.multiple_of(parity * rows, rows)
-        o_ref[0, :, pl.ds(column, rows)] = products[:rows]
-        o_ref[1, :, pl.ds(column, rows)] = products[rows:]
-
-    def multiply(*sums):
-        for k in range(2 * S // MXU):
-            depths = slice(k * MXU, (k + 1) * MXU)
-            for unit, right in enumerate(rights):
-                pltpu.matmul_push_rhs(right[:, depths], k % 2, unit, transpose=True)
-            for unit in range(2):
-                pltpu.matmul_acc_lhs(sums[unit], stacked[:, depths], load_staged_rhs=k % 2)
-        for unit, parity in enumerate((core, 1 - core)):
-            keep(pltpu.matmul_pop(sums[unit]), parity)
-
-    if rows == MXU:
-        pl.run_scoped(
-            multiply, *[pltpu.ACC(unit)((2 * rows, MXU), jnp.float32) for unit in range(2)]
+    rows = freq_count * sum(piece.shape[0] * piece.shape[3] for piece in own)
+
+    def inputs_of(sources, channel):
+        pieces = [
+            source[g, f ^ freq, channel]
+            for f in range(freq_count)
+            for source in sources
+            for g in range(source.shape[0])
+        ]
+        return joined(pieces)
+
+    def one_channel(channel):
+        left = inputs_of(own, channel)
+        turned = jnp.concatenate([left[:, S:], -left[:, :S]], axis=1)
+        stacked = jnp.concatenate([left, turned], axis=0).astype(jnp.bfloat16)
+        rights = [inputs_of(sources, channel).astype(jnp.bfloat16) for sources in (same, other)]
+
+        def keep(products, parity):
+            products = products.astype(jnp.bfloat16)
+            column = pl.multiple_of(parity * rows, rows)
+            o_ref[0, channel, :, pl.ds(column, rows)] = products[:rows]
+            o_ref[1, channel, :, pl.ds(column, rows)] = products[rows:]
+
+        def multiply(*sums):
+            for k in range(2 * S // MXU):
+                depths = slice(k * MXU, (k + 1) * MXU)
+                for unit, right in enumerate(rights):
+                    pltpu.matmul_push_rhs(right[:, depths], k % 2, unit, transpose=True)
+                for unit in range(2):
+                    pltpu.matmul_acc_lhs(sums[unit], stacked[:, depths], load_staged_rhs=k % 2)
+            for unit, parity in enumerate((core, 1 - core)):
+                keep(pltpu.matmul_pop(sums[unit]), parity)
+
+        if rows == MXU:
+            pl.run_scoped(
+                multiply, *[pltpu.ACC(unit)((2 * rows, MXU), jnp.float32) for unit in range(2)]
+            )
+        else:
+            for right, parity in zip(rights, (core, 1 - core)):
+                products = lax.dot_general(
+                    stacked, right, (((1,), (1,)), ((), ())), preferred_element_type=jnp.float32
+                )
+                keep(products, parity)
+
+    for channel in range(channels):
+        one_channel(channel)
+
+
+def correlate(place, own, same, other, after, previous, total_columns):
+    streams = len(own)
+    freq_count, slab, _, depth = own[0].shape[1:]
+    rows = freq_count * sum(piece.shape[0] * piece.shape[3] for piece in own)
+    in_specs = [
+        pl.BlockSpec(
+            (piece.shape[0], freq_count, CH_STEP, piece.shape[3], depth),
+            lambda c, p: (0, 0, c, 0, 0),
         )
-    else:
-        for right, parity in zip(rights, (core, 1 - core)):
-            products = lax.dot_general(
-                stacked, right, (((1,), (1,)), ((), ())), preferred_element_type=jnp.float32
-            )
-            keep(products, parity)
-
-
-def correlate(place, own, same, other, after, previous, total_columns):
-    groups = len(own)
-    freq_count, slab, block, depth = own[0].shape
-    rows = freq_count * groups * block
-    piece = pl.BlockSpec((freq_count, None, block, depth), lambda c, p: (0, c, 0, 0))
-    in_specs = [piece] * (3 * groups) + [pl.BlockSpec(memory_space=pl.ANY)]
+        for piece in (*own, *same, *other)
+    ]
+    in_specs.append(pl.BlockSpec(memory_space=pl.ANY))
     args = [place, *own, *same, *other, after]
     aliases = {}
     if previous is not None:
@@ -223,13 +275,13 @@
         in_specs.append(pl.BlockSpec(memory_space=pl.ANY))
         args.append(previous)
     return pl.pallas_call(
-        functools.partial(correlate_kernel, groups),
+        functools.partial(correlate_kernel, streams),
         grid_spec=pltpu.PrefetchScalarGridSpec(
             num_scalar_prefetch=1,
-            grid=(slab,),
+            grid=(slab // CH_STEP,),
             in_specs=in_specs,
             out_specs=[
-                pl.BlockSpec((2, None, rows, 2 * rows), lambda c, p: (0, c, 0, p[2])),
+                pl.BlockSpec((2, CH_STEP, rows, 2 * rows), lambda c, p: (0, c, 0, p[2])),
                 pl.BlockSpec((8, LANES), lambda c, p: (0, 0)),
             ],
         ),
@@ -249,8 +301,8 @@
     tm_count = lax.axis_size("tm")
     inputs_here = voltages.shape[0]
     total_columns = inputs_here * freq_count * tm_count
-    streams = min(2, inputs_here // GROUP)
-    block = inputs_here // streams
+    groups = inputs_here // GROUP
+    streams = min(2, groups)
     ring = tm_count // 2
     tm = lax.axis_index("tm").astype(jnp.int32)
     freq = lax.axis_index("freq").astype(jnp.int32)
@@ -266,19 +318,23 @@
     token = jnp.zeros((8, LANES), jnp.float32)
     own, early = [], []
     for stream in range(streams):
+        first, last = stream * groups // streams, (stream + 1) * groups // streams
+        at_once = 1 if stream == 0 else last - first
         if stream:
             token = behind(token, own[0])
-        spectra = channelize(voltages, table, token, stream, block)
+        parts = []
+        for group in range(first, last, at_once):
+            spectra = channelize(voltages, table, token, group, at_once)
+            token = behind(token, spectra)
+            spectra = spectra.reshape(freq_count, CH_DEV, at_once * GROUP, 2 * S)
+            parts.append(spectra[0])
+            for k in range(1, freq_count):
+                partners = [(i, i ^ k) for i in range(freq_count)]
+                parts.append(lax.ppermute(spectra[k], "freq", partners))
         if stream:
             early = [lax.ppermute(own[0], "tm", onward)]
-        spectra = spectra.reshape(freq_count, CH_DEV, block, 2 * S)
-        parts = [spectra[0]]
-        for k in range(1, freq_count):
-            partners = [(i, i ^ k) for i in range(freq_count)]
-            parts.append(lax.ppermute(spectra[k], "freq", partners))
-        if stream:
             parts[-1] = behind(parts[-1], early[0])
-        own.append(jnp.stack(parts))
+        own.append(jnp.stack(parts).reshape(-1, freq_count, *parts[0].shape))
 
     result, held, tokens = None, own, []
     for step in range(ring):

time: 209 us -> 195 us (0.933)
  Pallas kernels: 80.6 us -> 65 us
  starting transfers between devices: 14 us -> 17.6 us
    pallas_call x6 -> x7, Pallas kernels: 80.6 us -> 65 us  [the longest x3 39.6 us: channelize(): pl.pallas_call(functools.partial(channelize_kernel, channels, first_group...]
    ppermute x6 -> x9, waiting for transfers between devices: 21.5 us -> 14.9 us  [on_device(): parts.append(lax.ppermute(spectra[k], 'freq', partners))]
    ppermute x5, waiting for transfers between devices: 83.8 us -> 88.9 us  [on_device(): moved.append(early.pop() if early else lax.ppermute(piece, 'tm', onward))]
    ppermute x6 -> x9, starting transfers between devices: 8.1 us -> 11.7 us  [on_device(): parts.append(lax.ppermute(spectra[k], 'freq', partners))]
  transfers between devices with their start and end apart: 20 -> 23, of which waited for: 11 -> 11; matrix products, arithmetic and copies ran while one was open for 0% -> 0% of each run, Pallas kernels for 24% -> 25%
where the time goes in v6:
time: 195 us
  waiting for transfers between devices  106 us (54%)
  Pallas kernels  65 us (33%)
  starting transfers between devices  17.6 us (9%)
  local copies, waits for them, and re-layouts  3.04 us (2%)
  other arithmetic  2.54 us (1%)
    ppermute x5, waiting for transfers between devices, on_device(): moved.append(early.pop() if early else lax.ppermute(piece, 'tm', onward))  88.9 us
    pallas_call x3, Pallas kernels, channelize(): pl.pallas_call(functools.partial(channelize_kernel, channels, first_group...  39.6 us
    pallas_call x4, Pallas kernels, correlate(): pl.pallas_call(functools.partial(correlate_kernel, streams), grid_spec=pl...  25.4 us
    ppermute x9, waiting for transfers between devices, on_device(): parts.append(lax.ppermute(spectra[k], 'freq', partners))  14.9 us
    ppermute x9, starting transfers between devices, on_device(): parts.append(lax.ppermute(spectra[k], 'freq', partners))  11.7 us
  transfers between devices with their start and end apart: 23, of which 11 were waited for; matrix products, arithmetic and copies ran while one was open for 0% of the time, Pallas kernels for 25%

profile of v6, /device:TPU:0, one launch (start us, length us, event | category | flops | bytes accessed | tf_op | source)
XLA Modules:
  0.0 194.8 jit_solution(10138751193971426654)
XLA Ops:
  0.2 1.2 cosine_convert_fusion
  1.4 0.9 multiply_convert_fusion
  2.9 10.3 %channelize.3 = bf16[32,16,512]{2,1,0:T(8,128)(2,1)S(1)} custom-call(bf16[64,530432]{1,0:T(8,128)(2,1)} %x_hbm.5, bf16[2048,256]{1,0:T(8,128)(2,1)S(1)} %copy.7.w_ref, f32[8,128]{1,0:T(8,128)S(1)} %broadcast_in_dim.2.after_ref.refs_6_), custom_call_target="tpu_custom_call" | custom-call | flops 4345298944 | bytes 16973824 | tf_op jit(solution)/shard_map/channelize/pallas_call | solution.py:177
  13.2 3.0 %collective-permute-start = (bf16[8,16,512]{2,1,0:T(8,128)(2,1)S(1)}, bf16[8,16,512]{2,1,0:T(8,128)(2,1)S(1)}, u32[]{:S(2)}, u32[]{:S(2)}) collective-permute-start(bf16[8,16,512]{2,1,0:T(8,128)(2,1)S(1)} %get-tuple-element.46), channel_id=1, source_target_pairs={{0,8},{8,0},{16,24},{24,16},{1,9},{9,1},{17,25},{25,17},{2,10},{10... | collective-permute-start | bytes 393224 | tf_op jit(solution)/shard_map/ppermute | solution.py:333
  16.2 1.5 collective-permute-start.1
  17.8 10.3 %channelize.4 = bf16[32,16,512]{2,1,0:T(8,128)(2,1)S(1)} custom-call(bf16[64,530432]{1,0:T(8,128)(2,1)} %x_hbm.5, bf16[2048,256]{1,0:T(8,128)(2,1)S(1)} %copy.7.w_ref, f32[8,128]{1,0:T(8,128)S(1)} %broadcast_in_dim.2.after_ref.refs_6_), custom_call_target="tpu_custom_call" | custom-call | flops 4345298944 | bytes 16973824 | tf_op jit(solution)/shard_map/channelize/pallas_call | solution.py:177
  28.1 2.0 %collective-permute-start.3 = (bf16[8,16,512]{2,1,0:T(8,128)(2,1)S(1)}, bf16[8,16,512]{2,1,0:T(8,128)(2,1)S(1)}, u32[]{:S(2)}, u32[]{:S(2)}) collective-permute-start(bf16[8,16,512]{2,1,0:T(8,128)(2,1)S(1)} %get-tuple-element.43), channel_id=1, source_target_pairs={{0,8},{8,0},{16,24},{24,16},{1,9},{9,1},{17,25},{25,17},{2,10},{10... | collective-permute-start | bytes 393224 | tf_op jit(solution)/shard_map/ppermute | solution.py:333
  30.1 1.5 collective-permute-start.4
  31.9 1.7 collective-permute-done.3
  33.6 4.3 %collective-permute-done.4 = bf16[8,16,512]{2,1,0:T(8,128)(2,1)S(1)} collective-permute-done((bf16[8,16,512]{2,1,0:T(8,128)(2,1)S(1)}, bf16[8,16,512]{2,1,0:T(8,128)(2,1)S(1)}, u32[]{:S(2)}, u32[]{:S(2)}) %collective-permute-start.4) | collective-permute-done | bytes 131104 | tf_op jit(solution)/shard_map/ppermute | solution.py:333
  37.9 1.6 collective-permute-start.9
  39.6 19.0 %channelize.5 = bf16[32,32,512]{2,1,0:T(8,128)(2,1)S(1)} custom-call(bf16[64,530432]{1,0:T(8,128)(2,1)} %x_hbm.5, bf16[2048,256]{1,0:T(8,128)(2,1)S(1)} %copy.7.w_ref, f32[8,128]{1,0:T(8,128)S(1)} %broadcast_in_dim.2.after_ref.refs_6_), custom_call_target="tpu_custom_call" | custom-call | flops 8690597888 | bytes 33947648 | tf_op jit(solution)/shard_map/channelize/pallas_call | solution.py:177
  58.7 1.0 collective-permute-start.8
  59.6 1.6 collective-permute-start.6
  61.2 1.0 collective-permute-start.7
  62.3 6.2 %collective-permute-done.8 = bf16[8,32,512]{2,1,0:T(8,128)(2,1)S(1)} collective-permute-done((bf16[8,32,512]{2,1,0:T(8,128)(2,1)S(1)}, bf16[8,32,512]{2,1,0:T(8,128)(2,1)S(1)}, u32[]{:S(2)}, u32[]{:S(2)}) %collective-permute-start.8) | collective-permute-done | bytes 262176 | tf_op jit(solution)/shard_map/ppermute | solution.py:333
  68.5 1.8 collective-permute-done.6
  70.2 0.9 collective-permute-done.7
  71.3 1.6 collective-permute-start.14
  73.4 1.6 collective-permute-start.10
  75.0 24.3 %collective-permute-done.14.refs_3_ = bf16[1,4,8,32,512]{4,3,2,1,0:T(8,128)(2,1)} collective-permute-done((bf16[1,4,8,32,512]{4,3,2,1,0:T(8,128)(2,1)S(1)}, bf16[1,4,8,32,512]{4,3,2,1,0:T(8,128)(2,1)}, u32[]{:S(2)}, u32[]{:S(2)}) %collective-permute-start.14) | collective-permute-done | bytes 1048608 | tf_op jit(solution)/shard_map/ppermute | solution.py:346
  99.3 1.0 copy-done
  101.0 1.2 copy-done.1
  102.2 6.5 %correlate.4 = (bf16[2,8,256,2048]{3,2,1,0:T(8,128)(2,1)}, f32[8,128]{1,0:T(8,128)S(1)}) custom-call(s32[3]{0:T(128)S(1)} %get-tuple-element.48.place_ref, bf16[2,4,8,16,512]{4,3,2,1,0:T(8,128)(2,1)S(1)} %bitcast.38, bf16[1,4,8,32,512]{4,3,2,1,0:T(8,128)(2,1)S(1)} %maximum_bitcast_fusion.refs_1_.refs_3_, bf16[2,4,8,16,512]{4,3,2,1,0:T(8,128)(2,1)S(1)} %bitcast.39, ...), custom_call_target="tpu_custom_call" | custom-call | tf_op jit(solution)/shard_map/correlate/pallas_call | solution.py:277
  108.7 13.1 %collective-permute-done.10.refs_2_ = bf16[2,4,8,16,512]{4,3,2,1,0:T(8,128)(2,1)} collective-permute-done((bf16[2,4,8,16,512]{4,3,2,1,0:T(8,128)(2,1)S(1)}, bf16[2,4,8,16,512]{4,3,2,1,0:T(8,128)(2,1)}, u32[]{:S(2)}, u32[]{:S(2)}) %collective-permute-start.10) | collective-permute-done | bytes 1048608 | tf_op jit(solution)/shard_map/ppermute | solution.py:346
  121.8 22.5 %collective-permute-done.15.refs_3_ = bf16[1,4,8,32,512]{4,3,2,1,0:T(8,128)(2,1)} collective-permute-done((bf16[1,4,8,32,512]{4,3,2,1,0:T(8,128)(2,1)}, bf16[1,4,8,32,512]{4,3,2,1,0:T(8,128)(2,1)}, u32[]{:S(2)}, u32[]{:S(2)}) %collective-permute-start.15) | collective-permute-done | bytes 1048608 | tf_op jit(solution)/shard_map/ppermute | solution.py:346
  144.3 6.8 %correlate.5 = (bf16[2,8,256,2048]{3,2,1,0:T(8,128)(2,1)}, f32[8,128]{1,0:T(8,128)S(1)}) custom-call(s32[3]{0:T(128)S(1)} %get-tuple-element.47.place_ref, bf16[2,4,8,16,512]{4,3,2,1,0:T(8,128)(2,1)S(1)} %bitcast.40, bf16[1,4,8,32,512]{4,3,2,1,0:T(8,128)(2,1)S(1)} %maximum_bitcast_fusion.refs_1_.refs_3_, ...), custom_call_target="tpu_custom_call", output_to_operand_aliasing={{0}: (8, {})} | custom-call | tf_op jit(solution)/shard_map/correlate/pallas_call | solution.py:277
  151.1 15.5 %collective-permute-done.13.refs_2_ = bf16[2,4,8,16,512]{4,3,2,1,0:T(8,128)(2,1)S(1)} collective-permute-done((bf16[2,4,8,16,512]{4,3,2,1,0:T(8,128)(2,1)}, bf16[2,4,8,16,512]{4,3,2,1,0:T(8,128)(2,1)S(1)}, u32[]{:S(2)}, u32[]{:S(2)}) %collective-permute-start.13) | collective-permute-done | bytes 1048608 | tf_op jit(solution)/shard_map/ppermute | solution.py:346
  166.6 6.7 %correlate.6 = (bf16[2,8,256,2048]{3,2,1,0:T(8,128)(2,1)}, f32[8,128]{1,0:T(8,128)S(1)}) custom-call(s32[3]{0:T(128)S(1)} %get-tuple-element.35.place_ref, bf16[2,4,8,16,512]{4,3,2,1,0:T(8,128)(2,1)S(1)} %bitcast.41, bf16[1,4,8,32,512]{4,3,2,1,0:T(8,128)(2,1)S(1)} %maximum_bitcast_fusion.refs_1_.refs_3_, ...), custom_call_target="tpu_custom_call", output_to_operand_aliasing={{0}: (8, {})} | custom-call | tf_op jit(solution)/shard_map/correlate/pallas_call | solution.py:277
  173.3 13.5 %collective-permute-done.18.refs_3_ = bf16[1,4,8,32,512]{4,3,2,1,0:T(8,128)(2,1)S(1)} collective-permute-done((bf16[1,4,8,32,512]{4,3,2,1,0:T(8,128)(2,1)}, bf16[1,4,8,32,512]{4,3,2,1,0:T(8,128)(2,1)S(1)}, u32[]{:S(2)}, u32[]{:S(2)}) %collective-permute-start.18) | collective-permute-done | bytes 1048608 | tf_op jit(solution)/shard_map/ppermute | solution.py:346
  186.8 2.7 %collective-permute-done.22.refs_5_ = bf16[1,4,8,32,512]{4,3,2,1,0:T(8,128)(2,1)S(1)} collective-permute-done((bf16[1,4,8,32,512]{4,3,2,1,0:T(8,128)(2,1)S(1)}, bf16[1,4,8,32,512]{4,3,2,1,0:T(8,128)(2,1)S(1)}, u32[]{:S(2)}, u32[]{:S(2)}) %collective-permute-start.22) | collective-permute-done | bytes 1048608 | tf_op jit(solution)/shard_map/ppermute | solution.py:352
  189.4 5.4 %correlate.7 = (bf16[2,8,256,2048]{3,2,1,0:T(8,128)(2,1)}, f32[8,128]{1,0:T(8,128)}) custom-call(s32[3]{0:T(128)S(1)} %get-tuple-element.49.place_ref, bf16[2,4,8,16,512]{4,3,2,1,0:T(8,128)(2,1)S(1)} %bitcast.42, bf16[1,4,8,32,512]{4,3,2,1,0:T(8,128)(2,1)S(1)} %maximum_bitcast_fusion.refs_1_.refs_3_, ...), custom_call_target="tpu_custom_call", output_to_operand_aliasing={{0}: (8, {})} | custom-call | tf_op jit(solution)/shard_map/correlate/pallas_call | solution.py:277
  (47 shorter events, 2.4 us)
Async XLA Ops:
  13.2 18.4 %collective-permute-start = (bf16[8,16,512]{2,1,0:T(8,128)(2,1)S(1)}, bf16[8,16,512]{2,1,0:T(8,128)(2,1)S(1)}, u32[]{:S(2)}, u32[]{:S(2)}) collective-permute-start(bf16[8,16,512]{2,1,0:T(8,128)(2,1)S(1)} %get-tuple-element.46), channel_id=1, source_target_pairs={{0,8},{8,0},{16,24},{24,16},{1,9},{9,1},{17,25},{25,17},{2,10},{10... | collective-permute-start | bytes 393224 | tf_op jit(solution)/shard_map/ppermute | solution.py:333
  16.2 15.5 %collective-permute-start.1 = (bf16[8,16,512]{2,1,0:T(8,128)(2,1)S(1)}, bf16[8,16,512]{2,1,0:T(8,128)(2,1)S(1)}, u32[]{:S(2)}, u32[]{:S(2)}) collective-permute-start(bf16[8,16,512]{2,1,0:T(8,128)(2,1)S(1)} %get-tuple-element.45), channel_id=1, source_target_pairs={{0,16},{8,24},{16,0},{24,8},{1,17},{9,25},{17,1},{25,9},{2,18},{10... | collective-permute-start | bytes 393224 | tf_op jit(solution)/shard_map/ppermute | solution.py:333
  17.8 14.0 %collective-permute-start.2 = (bf16[8,16,512]{2,1,0:T(8,128)(2,1)S(1)}, bf16[8,16,512]{2,1,0:T(8,128)(2,1)S(1)}, u32[]{:S(2)}, u32[]{:S(2)}) collective-permute-start(bf16[8,16,512]{2,1,0:T(8,128)(2,1)S(1)} %get-tuple-element.44), channel_id=1, source_target_pairs={{0,24},{8,16},{16,8},{24,0},{1,25},{9,17},{17,9},{25,1},{2,26},{10... | collective-permute-start | bytes 393224 | tf_op jit(solution)/shard_map/ppermute | solution.py:333
  28.1 5.5 %collective-permute-start.3 = (bf16[8,16,512]{2,1,0:T(8,128)(2,1)S(1)}, bf16[8,16,512]{2,1,0:T(8,128)(2,1)S(1)}, u32[]{:S(2)}, u32[]{:S(2)}) collective-permute-start(bf16[8,16,512]{2,1,0:T(8,128)(2,1)S(1)} %get-tuple-element.43), channel_id=1, source_target_pairs={{0,8},{8,0},{16,24},{24,16},{1,9},{9,1},{17,25},{25,17},{2,10},{10... | collective-permute-start | bytes 393224 | tf_op jit(solution)/shard_map/ppermute | solution.py:333
  30.1 7.8 %collective-permute-start.4 = (bf16[8,16,512]{2,1,0:T(8,128)(2,1)S(1)}, bf16[8,16,512]{2,1,0:T(8,128)(2,1)S(1)}, u32[]{:S(2)}, u32[]{:S(2)}) collective-permute-start(bf16[8,16,512]{2,1,0:T(8,128)(2,1)S(1)} %get-tuple-element.42), channel_id=1, source_target_pairs={{0,16},{8,24},{16,0},{24,8},{1,17},{9,25},{17,1},{25,9},{2,18},{10... | collective-permute-start | bytes 393224 | tf_op jit(solution)/shard_map/ppermute | solution.py:333
  31.7 6.2 %collective-permute-start.5 = (bf16[8,16,512]{2,1,0:T(8,128)(2,1)S(1)}, bf16[8,16,512]{2,1,0:T(8,128)(2,1)S(1)}, u32[]{:S(2)}, u32[]{:S(2)}) collective-permute-start(bf16[8,16,512]{2,1,0:T(8,128)(2,1)S(1)} %get-tuple-element.41), channel_id=1, source_target_pairs={{0,24},{8,16},{16,8},{24,0},{1,25},{9,17},{17,9},{25,1},{2,26},{10... | collective-permute-start | bytes 393224 | tf_op jit(solution)/shard_map/ppermute | solution.py:333
  37.9 30.5 %collective-permute-start.9 = (bf16[2,4,8,16,512]{4,3,2,1,0:T(8,128)(2,1)S(1)}, bf16[2,4,8,16,512]{4,3,2,1,0:T(8,128)(2,1)S(1)}, u32[]{:S(2)}, u32[]{:S(2)}) collective-permute-start(bf16[2,4,8,16,512]{4,3,2,1,0:T(8,128)(2,1)S(1)} %bitcast.36), channel_id=1, source_target_pairs={{0,2},{1,3},{2,4},{3,5},{4,6},{5,7},{6,0},{7,1},{8,10},{9,11},{10,... | collective-permute-start | bytes 3145736 | tf_op jit(solution)/shard_map/ppermute | solution.py:335
  58.7 9.8 %collective-permute-start.8 = (bf16[8,32,512]{2,1,0:T(8,128)(2,1)S(1)}, bf16[8,32,512]{2,1,0:T(8,128)(2,1)S(1)}, u32[]{:S(2)}, u32[]{:S(2)}) collective-permute-start(bf16[8,32,512]{2,1,0:T(8,128)(2,1)S(1)} %get-tuple-element.38), channel_id=1, source_target_pairs={{0,24},{8,16},{16,8},{24,0},{1,25},{9,17},{17,9},{25,1},{2,26},{10... | collective-permute-start | bytes 786440 | tf_op jit(solution)/shard_map/ppermute | solution.py:333
  59.6 10.6 %collective-permute-start.6 = (bf16[8,32,512]{2,1,0:T(8,128)(2,1)S(1)}, bf16[8,32,512]{2,1,0:T(8,128)(2,1)S(1)}, u32[]{:S(2)}, u32[]{:S(2)}) collective-permute-start(bf16[8,32,512]{2,1,0:T(8,128)(2,1)S(1)} %get-tuple-element.40), channel_id=1, source_target_pairs={{0,8},{8,0},{16,24},{24,16},{1,9},{9,1},{17,25},{25,17},{2,10},{10... | collective-permute-start | bytes 786440 | tf_op jit(solution)/shard_map/ppermute | solution.py:333
  61.2 9.9 %collective-permute-start.7 = (bf16[8,32,512]{2,1,0:T(8,128)(2,1)S(1)}, bf16[8,32,512]{2,1,0:T(8,128)(2,1)S(1)}, u32[]{:S(2)}, u32[]{:S(2)}) collective-permute-start(bf16[8,32,512]{2,1,0:T(8,128)(2,1)S(1)} %get-tuple-element.39), channel_id=1, source_target_pairs={{0,16},{8,24},{16,0},{24,8},{1,17},{9,25},{17,1},{25,9},{2,18},{10... | collective-permute-start | bytes 786440 | tf_op jit(solution)/shard_map/ppermute | solution.py:333
  71.3 28.1 %collective-permute-start.14 = (bf16[1,4,8,32,512]{4,3,2,1,0:T(8,128)(2,1)S(1)}, bf16[1,4,8,32,512]{4,3,2,1,0:T(8,128)(2,1)}, u32[]{:S(2)}, u32[]{:S(2)}) collective-permute-start(bf16[1,4,8,32,512]{4,3,2,1,0:T(8,128)(2,1)S(1)} %maximum_bitcast_fusion.refs_1_.refs_3_), channel_id=1, source_target_pairs={{0,2},{1,3},{2,4},{3,5},{4,6},{5,7},{6,0},{7,1},{8,10},{9,11},{10,... | collective-permute-start | bytes 3145736 | tf_op jit(solution)/shard_map/ppermute | solution.py:346
  72.9 26.4 %collective-permute-start.11 = (bf16[2,4,8,16,512]{4,3,2,1,0:T(8,128)(2,1)S(1)}, bf16[2,4,8,16,512]{4,3,2,1,0:T(8,128)(2,1)S(1)}, u32[]{:S(2)}, u32[]{:S(2)}) collective-permute-start(bf16[2,4,8,16,512]{4,3,2,1,0:T(8,128)(2,1)S(1)} %bitcast.37), channel_id=1, source_target_pairs={{0,1},{1,0},{2,3},{3,2},{4,5},{5,4},{6,7},{7,6},{8,9},{9,8},{10,11... | collective-permute-start | bytes 3145736 | tf_op jit(solution)/shard_map/ppermute | solution.py:352
  72.9 28.0 %collective-permute-start.12 = (bf16[1,4,8,32,512]{4,3,2,1,0:T(8,128)(2,1)S(1)}, bf16[1,4,8,32,512]{4,3,2,1,0:T(8,128)(2,1)}, u32[]{:S(2)}, u32[]{:S(2)}) collective-permute-start(bf16[1,4,8,32,512]{4,3,2,1,0:T(8,128)(2,1)S(1)} %maximum_bitcast_fusion.refs_1_.refs_3_), channel_id=1, source_target_pairs={{0,1},{1,0},{2,3},{3,2},{4,5},{5,4},{6,7},{7,6},{8,9},{9,8},{10,11... | collective-permute-start | bytes 3145736 | tf_op jit(solution)/shard_map/ppermute | solution.py:352
  73.4 48.4 %collective-permute-start.10 = (bf16[2,4,8,16,512]{4,3,2,1,0:T(8,128)(2,1)S(1)}, bf16[2,4,8,16,512]{4,3,2,1,0:T(8,128)(2,1)}, u32[]{:S(2)}, u32[]{:S(2)}) collective-permute-start(bf16[2,4,8,16,512]{4,3,2,1,0:T(8,128)(2,1)S(1)} %collective-permute-done.9.refs_2_), channel_id=1, source_target_pairs={{0,2},{1,3},{2,4},{3,5},{4,6},{5,7},{6,0},{7,1},{8,10},{9,11},{10,... | collective-permute-start | bytes 3145736 | tf_op jit(solution)/shard_map/ppermute | solution.py:346
  99.3 44.9 %collective-permute-start.15 = (bf16[1,4,8,32,512]{4,3,2,1,0:T(8,128)(2,1)}, bf16[1,4,8,32,512]{4,3,2,1,0:T(8,128)(2,1)}, u32[]{:S(2)}, u32[]{:S(2)}) collective-permute-start(bf16[1,4,8,32,512]{4,3,2,1,0:T(8,128)(2,1)} %collective-permute-done.14.refs_3_), channel_id=1, source_target_pairs={{0,2},{1,3},{2,4},{3,5},{4,6},{5,7},{6,0},{7,1},{8,10},{9,11},{10,... | collective-permute-start | bytes 3145736 | tf_op jit(solution)/shard_map/ppermute | solution.py:346
  99.3 44.9 %collective-permute-start.16 = (bf16[2,4,8,16,512]{4,3,2,1,0:T(8,128)(2,1)S(1)}, bf16[2,4,8,16,512]{4,3,2,1,0:T(8,128)(2,1)}, u32[]{:S(2)}, u32[]{:S(2)}) collective-permute-start(bf16[2,4,8,16,512]{4,3,2,1,0:T(8,128)(2,1)S(1)} %collective-permute-done.9.refs_2_), channel_id=1, source_target_pairs={{0,1},{1,0},{2,3},{3,2},{4,5},{5,4},{6,7},{7,6},{8,9},{9,8},{10,11... | collective-permute-start | bytes 3145736 | tf_op jit(solution)/shard_map/ppermute | solution.py:352
  99.3 1.0 copy-start
  100.3 44.0 %collective-permute-start.17 = (bf16[1,4,8,32,512]{4,3,2,1,0:T(8,128)(2,1)}, bf16[1,4,8,32,512]{4,3,2,1,0:T(8,128)(2,1)}, u32[]{:S(2)}, u32[]{:S(2)}) collective-permute-start(bf16[1,4,8,32,512]{4,3,2,1,0:T(8,128)(2,1)} %collective-permute-done.14.refs_3_), channel_id=1, source_target_pairs={{0,1},{1,0},{2,3},{3,2},{4,5},{5,4},{6,7},{7,6},{8,9},{9,8},{10,11... | collective-permute-start | bytes 3145736 | tf_op jit(solution)/shard_map/ppermute | solution.py:352
  101.0 1.2 copy-start.1
  121.8 44.8 %collective-permute-start.13 = (bf16[2,4,8,16,512]{4,3,2,1,0:T(8,128)(2,1)}, bf16[2,4,8,16,512]{4,3,2,1,0:T(8,128)(2,1)S(1)}, u32[]{:S(2)}, u32[]{:S(2)}) collective-permute-start(bf16[2,4,8,16,512]{4,3,2,1,0:T(8,128)(2,1)} %collective-permute-done.10.refs_2_), channel_id=1, source_target_pairs={{0,2},{1,3},{2,4},{3,5},{4,6},{5,7},{6,0},{7,1},{8,10},{9,11},{10,... | collective-permute-start | bytes 3145736 | tf_op jit(solution)/shard_map/ppermute | solution.py:346
  121.8 44.8 %collective-permute-start.20 = (bf16[2,4,8,16,512]{4,3,2,1,0:T(8,128)(2,1)}, bf16[2,4,8,16,512]{4,3,2,1,0:T(8,128)(2,1)S(1)}, u32[]{:S(2)}, u32[]{:S(2)}) collective-permute-start(bf16[2,4,8,16,512]{4,3,2,1,0:T(8,128)(2,1)} %collective-permute-done.10.refs_2_), channel_id=1, source_target_pairs={{0,1},{1,0},{2,3},{3,2},{4,5},{5,4},{6,7},{7,6},{8,9},{9,8},{10,11... | collective-permute-start | bytes 3145736 | tf_op jit(solution)/shard_map/ppermute | solution.py:352
  144.3 22.4 %collective-permute-start.21 = (bf16[1,4,8,32,512]{4,3,2,1,0:T(8,128)(2,1)}, bf16[1,4,8,32,512]{4,3,2,1,0:T(8,128)(2,1)S(1)}, u32[]{:S(2)}, u32[]{:S(2)}) collective-permute-start(bf16[1,4,8,32,512]{4,3,2,1,0:T(8,128)(2,1)} %collective-permute-done.15.refs_3_), channel_id=1, source_target_pairs={{0,1},{1,0},{2,3},{3,2},{4,5},{5,4},{6,7},{7,6},{8,9},{9,8},{10,11... | collective-permute-start | bytes 3145736 | tf_op jit(solution)/shard_map/ppermute | solution.py:352
  151.1 35.7 %collective-permute-start.18 = (bf16[1,4,8,32,512]{4,3,2,1,0:T(8,128)(2,1)}, bf16[1,4,8,32,512]{4,3,2,1,0:T(8,128)(2,1)S(1)}, u32[]{:S(2)}, u32[]{:S(2)}) collective-permute-start(bf16[1,4,8,32,512]{4,3,2,1,0:T(8,128)(2,1)} %collective-permute-done.15.refs_3_), channel_id=1, source_target_pairs={{0,2},{1,3},{2,4},{3,5},{4,6},{5,7},{6,0},{7,1},{8,10},{9,11},{10,... | collective-permute-start | bytes 3145736 | tf_op jit(solution)/shard_map/ppermute | solution.py:346
  166.6 20.2 %collective-permute-start.19 = (bf16[2,4,8,16,512]{4,3,2,1,0:T(8,128)(2,1)S(1)}, bf16[2,4,8,16,512]{4,3,2,1,0:T(8,128)(2,1)S(1)}, u32[]{:S(2)}, u32[]{:S(2)}) collective-permute-start(bf16[2,4,8,16,512]{4,3,2,1,0:T(8,128)(2,1)S(1)} %collective-permute-done.13.refs_2_), channel_id=1, source_target_pairs={{0,1},{1,0},{2,3},{3,2},{4,5},{5,4},{6,7},{7,6},{8,9},{9,8},{10,11... | collective-permute-start | bytes 3145736 | tf_op jit(solution)/shard_map/ppermute | solution.py:352
  186.8 2.7 %collective-permute-start.22 = (bf16[1,4,8,32,512]{4,3,2,1,0:T(8,128)(2,1)S(1)}, bf16[1,4,8,32,512]{4,3,2,1,0:T(8,128)(2,1)S(1)}, u32[]{:S(2)}, u32[]{:S(2)}) collective-permute-start(bf16[1,4,8,32,512]{4,3,2,1,0:T(8,128)(2,1)S(1)} %collective-permute-done.18.refs_3_), channel_id=1, source_target_pairs={{0,1},{1,0},{2,3},{3,2},{4,5},{5,4},{6,7},{7,6},{8,9},{9,8},{10,11... | collective-permute-start | bytes 3145736 | tf_op jit(solution)/shard_map/ppermute | solution.py:352

commit v7 on v6

--- a/solution.py
+++ b/solution.py
@@ -91,15 +91,14 @@
             for unit, (begin, end, column) in enumerate(shares):
                 pltpu.matmul_push_rhs(w_ref[depths, column : column + MXU], k % 2, unit)
             for unit, (begin, end, column) in enumerate(shares):
-                rows = joined(
+                rows = jnp.concatenate(
                     [
                         x_ref[slot, :, t * P_SIZE + k * MXU : t * P_SIZE + (k + 1) * MXU]
                         for t in range(begin, end)
-                    ]
+                    ],
+                    axis=0,
                 )
-                pltpu.matmul_acc_lhs(
-                    sums[unit], rows.astype(jnp.bfloat16), load_staged_rhs=k % 2
-                )
+                pltpu.matmul_acc_lhs(sums[unit], rows, load_staged_rhs=k % 2)
         for unit, (begin, end, column) in enumerate(shares):
             start = pl.multiple_of((step * T_BLOCK + begin) * GROUP, GROUP)
             y_ref[pl.ds(start, (end - begin) * GROUP), column : column + MXU] = (
@@ -202,22 +201,16 @@
     )(voltages, table, after)
 
 
-def correlate_kernel(streams, place_ref, *refs):
+def correlate_kernel(counts, place_ref, *refs):
     o_ref, token_ref = refs[-2:]
     token_ref[...] = jnp.zeros_like(token_ref)
-    own, same, other = (refs[i * streams : (i + 1) * streams] for i in range(3))
-    freq_count, channels = own[0].shape[1:3]
+    own, same, other = (refs[sum(counts[:i]) : sum(counts[: i + 1])] for i in range(3))
+    freq_count, channels = own[0].shape[:2]
     freq, core = place_ref[0], place_ref[1]
-    rows = freq_count * sum(piece.shape[0] * piece.shape[3] for piece in own)
+    rows = freq_count * sum(piece.shape[2] for piece in own)
 
     def inputs_of(sources, channel):
-        pieces = [
-            source[g, f ^ freq, channel]
-            for f in range(freq_count)
-            for source in sources
-            for g in range(source.shape[0])
-        ]
-        return joined(pieces)
+        return joined([source[f ^ freq, channel] for f in range(freq_count) for source in sources])
 
     def one_channel(channel):
         left = inputs_of(own, channel)
@@ -257,25 +250,25 @@
 
 
 def correlate(place, own, same, other, after, previous, total_columns):
-    streams = len(own)
-    freq_count, slab, _, depth = own[0].shape[1:]
-    rows = freq_count * sum(piece.shape[0] * piece.shape[3] for piece in own)
+    pieces = (*own, *same, *other)
+    freq_count, slab, _, depth = own[0][0].shape[1:]
+    rows = freq_count * sum(array.shape[3] for array, part in own)
     in_specs = [
         pl.BlockSpec(
-            (piece.shape[0], freq_count, CH_STEP, piece.shape[3], depth),
-            lambda c, p: (0, 0, c, 0, 0),
+            (None, freq_count, CH_STEP, array.shape[3], depth),
+            lambda c, p, part=part: (part, 0, c, 0, 0),
         )
-        for piece in (*own, *same, *other)
+        for array, part in pieces
     ]
     in_specs.append(pl.BlockSpec(memory_space=pl.ANY))
-    args = [place, *own, *same, *other, after]
+    args = [place, *[array for array, part in pieces], after]
     aliases = {}
     if previous is not None:
         aliases = {len(args): 0}
         in_specs.append(pl.BlockSpec(memory_space=pl.ANY))
         args.append(previous)
     return pl.pallas_call(
-        functools.partial(correlate_kernel, streams),
+        functools.partial(correlate_kernel, (len(own), len(same), len(other))),
         grid_spec=pltpu.PrefetchScalarGridSpec(
             num_scalar_prefetch=1,
             grid=(slab // CH_STEP,),
@@ -302,7 +295,8 @@
     inputs_here = voltages.shape[0]
     total_columns = inputs_here * freq_count * tm_count
     groups = inputs_here // GROUP
-    streams = min(2, groups)
+    widths = (1, 1, groups - 2) if groups >= 3 else (1,) * groups
+    streams = len(widths)
     ring = tm_count // 2
     tm = lax.axis_index("tm").astype(jnp.int32)
     freq = lax.axis_index("freq").astype(jnp.int32)
@@ -316,42 +310,69 @@
 
     table = folded_table(fir_taps, freq_count)
     token = jnp.zeros((8, LANES), jnp.float32)
-    own, early = [], []
-    for stream in range(streams):
-        first, last = stream * groups // streams, (stream + 1) * groups // streams
-        at_once = 1 if stream == 0 else last - first
-        if stream:
-            token = behind(token, own[0])
-        parts = []
-        for group in range(first, last, at_once):
-            spectra = channelize(voltages, table, token, group, at_once)
-            token = behind(token, spectra)
-            spectra = spectra.reshape(freq_count, CH_DEV, at_once * GROUP, 2 * S)
-            parts.append(spectra[0])
-            for k in range(1, freq_count):
-                partners = [(i, i ^ k) for i in range(freq_count)]
-                parts.append(lax.ppermute(spectra[k], "freq", partners))
-        if stream:
-            early = [lax.ppermute(own[0], "tm", onward)]
-            parts[-1] = behind(parts[-1], early[0])
-        own.append(jnp.stack(parts).reshape(-1, freq_count, *parts[0].shape))
-
-    result, held, tokens = None, own, []
+    held, swapped = {}, {}
+
+    def move_on(step, stream, *others):
+        if (step, stream) not in held:
+            array, part = held[step - 1, stream]
+            piece = behind(array[part : part + 1], *others)
+            held[step, stream] = (lax.ppermute(piece, "tm", onward), 0)
+        return held[step, stream][0]
+
+    def swap_cores(step, stream, *others):
+        array, part = held[step, stream]
+        if (step, stream) not in swapped:
+            for place, (other, number) in held.items():
+                if other is array and place in swapped:
+                    swapped[step, stream] = (swapped[place][0], part)
+        if (step, stream) not in swapped:
+            swapped[step, stream] = (lax.ppermute(behind(array, *others), "tm", swap), part)
+
+    ahead = streams == 3 and ring == 4
+    first = 0
+    for stream, width in enumerate(widths):
+        if stream >= 2:
+            token = behind(token, *[held[0, earlier][0] for earlier in range(stream)])
+        spectra = channelize(voltages, table, token, first, width)
+        first += width
+        token = behind(token, spectra)
+        spectra = spectra.reshape(freq_count, CH_DEV, width * GROUP, 2 * S)
+        parts = [spectra[0]]
+        for k in range(1, freq_count):
+            partners = [(i, i ^ k) for i in range(freq_count)]
+            parts.append(lax.ppermute(spectra[k], "freq", partners))
+        if ahead and stream == 2:
+            parts[-1] = behind(parts[-1], move_on(1, 1), move_on(1, 0), move_on(2, 0))
+        held[0, stream] = (jnp.stack(parts)[None], 0)
+
+    if ahead:
+        both = jnp.concatenate([held[2, 0][0], held[1, 1][0]], axis=0)
+        both = lax.ppermute(both, "tm", onward)
+        held[3, 0], held[2, 1] = (both, 0), (both, 1)
+    names = list(range(streams))
+    result, tokens = None, [token]
     for step in range(ring):
-        if step:
-            moved = []
-            for stream, piece in enumerate(held):
-                if step >= 3 and streams == 2:
-                    piece = behind(piece, tokens[step - 3 + stream])
-                moved.append(early.pop() if early else lax.ppermute(piece, "tm", onward))
-            held = moved
-        other = []
-        for stream, piece in enumerate(held):
-            if step == ring - 1 and step and stream == streams - 1:
-                piece = behind(piece, tokens[-1])
-            other.append(lax.ppermute(piece, "tm", swap))
+        if ahead and step == 2:
+            third, names = held[1, 2][0], [0, 1, 2, 3]
+            middle = third.shape[3] // 2
+            held[1, 2], held[1, 3] = (third[:, :, :, :middle], 0), (third[:, :, :, middle:], 0)
+        for name in names:
+            if step:
+                late = ahead and step == 3 and name == 3
+                move_on(step, name, *([tokens[2]] if late else []))
+        for name in names:
+            late = step == ring - 1 and step and name == names[-1]
+            swap_cores(step, name, *([tokens[-1]] if late else []))
         place = jnp.stack([freq, tm % 2, (tm // 2 + ring - step) % ring])
-        result, token = correlate(place, own, held, other, token, result, total_columns)
+        result, token = correlate(
+            place,
+            [held[0, name] for name in range(streams)],
+            [held[step, name] for name in names],
+            [swapped[step, name] for name in names],
+            tokens[-1],
+            result,
+            total_columns,
+        )
         tokens.append(token)
     return result
 

time: 195 us -> 198 us (1.015)
  waiting for transfers between devices: 106 us -> 92.7 us
  local copies, waits for them, and re-layouts: 3.04 us -> 13 us
  starting transfers between devices: 17.6 us -> 21.8 us
    ppermute x14 -> x23, waiting for transfers between devices: 91.6 us -> 73.4 us  [the longest x9 51.8 us: move_on(): held[step, stream] = (lax.ppermute(piece, 'tm', onward), 0)]
    unnamed x11 -> x28, local copies, waits for them, and re-layouts: 2.26 us -> 9.26 us
    ppermute x9, waiting for transfers between devices: 14.9 us -> 19.3 us  [on_device(): parts.append(lax.ppermute(spectra[k], 'freq', partners))]
    ppermute x14 -> x23, starting transfers between devices: 5.88 us -> 10.1 us  [the longest x9 6.48 us: move_on(): held[step, stream] = (lax.ppermute(piece, 'tm', onward), 0)]
    slice x3 -> x5, local copies, waits for them, and re-layouts: 0.16 us -> 3.11 us  [the longest x1 2.09 us: on_device(): third[:, :, :, middle:]]
  transfers between devices with their start and end apart: 23 -> 32, of which waited for: 11 -> 13; matrix products, arithmetic and copies ran while one was open for 0% -> 2% of each run, Pallas kernels for 25% -> 25%
where the time goes in v7:
time: 198 us; the launch traced here: 197 us
  waiting for transfers between devices  92.7 us (47%)
  Pallas kernels  65.2 us (33%)
  starting transfers between devices  21.8 us (11%)
  local copies, waits for them, and re-layouts  13 us (7%)
  other arithmetic  3.82 us (2%)
    ppermute x9, waiting for transfers between devices, move_on(): held[step, stream] = (lax.ppermute(piece, 'tm', onward), 0)  51.8 us
    pallas_call x3, Pallas kernels, channelize(): pl.pallas_call(functools.partial(channelize_kernel, channels, first_group...  39.6 us
    pallas_call x4, Pallas kernels, correlate(): pl.pallas_call(functools.partial(correlate_kernel, (len(own), len(same),...  25.6 us
    ppermute x1, waiting for transfers between devices, on_device(): both = lax.ppermute(both, 'tm', onward)  19.7 us
    ppermute x9, waiting for transfers between devices, on_device(): parts.append(lax.ppermute(spectra[k], 'freq', partners))  19.3 us
    ppermute x9, starting transfers between devices, on_device(): parts.append(lax.ppermute(spectra[k], 'freq', partners))  11.7 us
    unnamed x28, local copies, waits for them, and re-layouts  9.26 us
    ppermute x9, starting transfers between devices, move_on(): held[step, stream] = (lax.ppermute(piece, 'tm', onward), 0)  6.48 us
  transfers between devices with their start and end apart: 32, of which 13 were waited for; matrix products, arithmetic and copies ran while one was open for 2% of the time, Pallas kernels for 25%

profile of v7, /device:TPU:0, one launch (start us, length us, event | category | flops | bytes accessed | tf_op | source)
XLA Modules:
  0.0 196.7 jit_solution(16267797337768244066)
XLA Ops:
  0.2 1.2 cosine_convert_fusion
  2.9 10.3 %channelize.3 = bf16[32,16,512]{2,1,0:T(8,128)(2,1)S(1)} custom-call(bf16[64,530432]{1,0:T(8,128)(2,1)} %x_hbm.5, bf16[2048,256]{1,0:T(8,128)(2,1)S(1)} %copy.7.w_ref, f32[8,128]{1,0:T(8,128)S(1)} %broadcast_in_dim.8.after_ref.refs_9_), custom_call_target="tpu_custom_call" | custom-call | flops 4345298944 | bytes 16973824 | tf_op jit(solution)/shard_map/channelize/pallas_call | solution.py:176
  13.3 3.0 %collective-permute-start = (bf16[8,16,512]{2,1,0:T(8,128)(2,1)S(1)}, bf16[8,16,512]{2,1,0:T(8,128)(2,1)S(1)}, u32[]{:S(2)}, u32[]{:S(2)}) collective-permute-start(bf16[8,16,512]{2,1,0:T(8,128)(2,1)S(1)} %get-tuple-element.54), channel_id=1, source_target_pairs={{0,8},{8,0},{16,24},{24,16},{1,9},{9,1},{17,25},{25,17},{2,10},{10... | collective-permute-start | bytes 393224 | tf_op jit(solution)/shard_map/ppermute | solution.py:343
  16.3 1.5 collective-permute-start.1
  17.8 2.4 %collective-permute-done = bf16[8,16,512]{2,1,0:T(8,128)(2,1)S(1)} collective-permute-done((bf16[8,16,512]{2,1,0:T(8,128)(2,1)S(1)}, bf16[8,16,512]{2,1,0:T(8,128)(2,1)S(1)}, u32[]{:S(2)}, u32[]{:S(2)}) %collective-permute-start) | collective-permute-done | bytes 131104 | tf_op jit(solution)/shard_map/ppermute | solution.py:343
  20.2 3.9 %collective-permute-done.1 = bf16[8,16,512]{2,1,0:T(8,128)(2,1)S(1)} collective-permute-done((bf16[8,16,512]{2,1,0:T(8,128)(2,1)S(1)}, bf16[8,16,512]{2,1,0:T(8,128)(2,1)S(1)}, u32[]{:S(2)}, u32[]{:S(2)}) %collective-permute-start.1) | collective-permute-done | bytes 131104 | tf_op jit(solution)/shard_map/ppermute | solution.py:343
  24.1 1.6 collective-permute-start.10
  25.7 10.3 %channelize.4 = bf16[32,16,512]{2,1,0:T(8,128)(2,1)S(1)} custom-call(bf16[64,530432]{1,0:T(8,128)(2,1)} %x_hbm.5, bf16[2048,256]{1,0:T(8,128)(2,1)S(1)} %copy.7.w_ref, f32[8,128]{1,0:T(8,128)S(1)} %broadcast_in_dim.8.after_ref.refs_9_), custom_call_target="tpu_custom_call" | custom-call | flops 4345298944 | bytes 16973824 | tf_op jit(solution)/shard_map/channelize/pallas_call | solution.py:176
  36.1 1.3 collective-permute-start.3
  38.2 1.4 collective-permute-start.5
  39.6 2.7 %collective-permute-done.3 = bf16[8,16,512]{2,1,0:T(8,128)(2,1)S(1)} collective-permute-done((bf16[8,16,512]{2,1,0:T(8,128)(2,1)S(1)}, bf16[8,16,512]{2,1,0:T(8,128)(2,1)S(1)}, u32[]{:S(2)}, u32[]{:S(2)}) %collective-permute-start.3) | collective-permute-done | bytes 131104 | tf_op jit(solution)/shard_map/ppermute | solution.py:343
  42.6 1.5 collective-permute-done.5
  44.1 1.6 collective-permute-start.9
  45.8 1.6 collective-permute-start.11
  47.3 19.0 %channelize.5 = bf16[32,32,512]{2,1,0:T(8,128)(2,1)S(1)} custom-call(bf16[64,530432]{1,0:T(8,128)(2,1)} %x_hbm.5, bf16[2048,256]{1,0:T(8,128)(2,1)S(1)} %copy.7.w_ref, f32[8,128]{1,0:T(8,128)S(1)} %broadcast_in_dim.8.after_ref.refs_9_), custom_call_target="tpu_custom_call" | custom-call | flops 8690597888 | bytes 33947648 | tf_op jit(solution)/shard_map/channelize/pallas_call | solution.py:176
  66.5 1.6 collective-permute-start.8
  68.1 1.4 collective-permute-start.6
  70.0 5.3 %collective-permute-done.8 = bf16[8,32,512]{2,1,0:T(8,128)(2,1)S(1)} collective-permute-done((bf16[8,32,512]{2,1,0:T(8,128)(2,1)S(1)}, bf16[8,32,512]{2,1,0:T(8,128)(2,1)S(1)}, u32[]{:S(2)}, u32[]{:S(2)}) %collective-permute-start.8) | collective-permute-done | bytes 262176 | tf_op jit(solution)/shard_map/ppermute | solution.py:343
  75.3 3.4 %collective-permute-done.6 = bf16[8,32,512]{2,1,0:T(8,128)(2,1)S(1)} collective-permute-done((bf16[8,32,512]{2,1,0:T(8,128)(2,1)S(1)}, bf16[8,32,512]{2,1,0:T(8,128)(2,1)S(1)}, u32[]{:S(2)}, u32[]{:S(2)}) %collective-permute-start.6) | collective-permute-done | bytes 262176 | tf_op jit(solution)/shard_map/ppermute | solution.py:343
  81.1 1.4 collective-permute-start.12
  83.8 23.1 %collective-permute-done.14.refs_5_ = bf16[1,4,8,32,512]{4,3,2,1,0:T(8,128)(2,1)} collective-permute-done((bf16[1,4,8,32,512]{4,3,2,1,0:T(8,128)(2,1)S(1)}, bf16[1,4,8,32,512]{4,3,2,1,0:T(8,128)(2,1)}, u32[]{:S(2)}, u32[]{:S(2)}) %collective-permute-start.14) | collective-permute-done | bytes 1048608 | tf_op jit(solution)/shard_map/ppermute | solution.py:319
  106.9 2.1 %fusion.6 = (bf16[1,4,8,16,512]{4,3,2,1,0:T(8,128)(2,1)}, bf16[1,4,8,16,512]{4,3,2,1,0:T(8,128)(2,1)S(1)}) fusion(bf16[1,4,8,32,512]{4,3,2,1,0:T(8,128)(2,1)} %collective-permute-done.14.refs_5_), kind=kLoop, calls=%fused_computation.27 | loop fusion | bytes 2097152 | tf_op jit(solution)/shard_map/slice | solution.py:358
  109.6 19.7 %collective-permute-done.12.refs_4_.refs_3_ = bf16[2,4,8,16,512]{4,3,2,1,0:T(8,128)(2,1)S(1)} collective-permute-done((bf16[2,4,8,16,512]{4,3,2,1,0:T(8,128)(2,1)S(1)}, bf16[2,4,8,16,512]{4,3,2,1,0:T(8,128)(2,1)S(1)}, u32[]{:S(2)}, u32[]{:S(2)}) %collective-permute-start.12) | collective-permute-done | bytes 1048608 | tf_op jit(solution)/shard_map/ppermute | solution.py:350
  131.1 9.5 %collective-permute-done.15.refs_5_ = bf16[1,4,8,16,512]{4,3,2,1,0:T(8,128)(2,1)} collective-permute-done((bf16[1,4,8,16,512]{4,3,2,1,0:T(8,128)(2,1)S(1)}, bf16[1,4,8,16,512]{4,3,2,1,0:T(8,128)(2,1)}, u32[]{:S(2)}, u32[]{:S(2)}) %collective-permute-start.15) | collective-permute-done | bytes 524320 | tf_op jit(solution)/shard_map/ppermute | solution.py:319
  140.9 1.2 copy-done.3
  144.2 5.4 %correlate.4 = (bf16[2,8,256,2048]{3,2,1,0:T(8,128)(2,1)}, f32[8,128]{1,0:T(8,128)S(1)}) custom-call(s32[3]{0:T(128)S(1)} %get-tuple-element.55.place_ref, bf16[1,4,8,16,512]{4,3,2,1,0:T(8,128)(2,1)S(1)} %maximum_bitcast_fusion.1.refs_0_.refs_3_, bf16[1,4,8,16,512]{4,3,2,1,0:T(8,128)(2,1)S(1)} %maximum_bitcast_fusion.2.refs_1_.refs_4_, ...), custom_call_target="tpu_custom_call" | custom-call | tf_op jit(solution)/shard_map/correlate/pallas_call | solution.py:270
  153.8 6.7 %correlate.5 = (bf16[2,8,256,2048]{3,2,1,0:T(8,128)(2,1)}, f32[8,128]{1,0:T(8,128)S(1)}) custom-call(s32[3]{0:T(128)S(1)} %get-tuple-element.56.place_ref, bf16[1,4,8,16,512]{4,3,2,1,0:T(8,128)(2,1)S(1)} %maximum_bitcast_fusion.1.refs_0_.refs_3_, ...), custom_call_target="tpu_custom_call", output_to_operand_aliasing={{0}: (11, {})} | custom-call | tf_op jit(solution)/shard_map/correlate/pallas_call | solution.py:270
  162.2 15.1 %collective-permute-done.16.refs_5_ = bf16[1,4,8,16,512]{4,3,2,1,0:T(8,128)(2,1)S(1)} collective-permute-done((bf16[1,4,8,16,512]{4,3,2,1,0:T(8,128)(2,1)}, bf16[1,4,8,16,512]{4,3,2,1,0:T(8,128)(2,1)S(1)}, u32[]{:S(2)}, u32[]{:S(2)}) %collective-permute-start.16) | collective-permute-done | bytes 524320 | tf_op jit(solution)/shard_map/ppermute | solution.py:319
  177.3 6.9 %correlate.6 = (bf16[2,8,256,2048]{3,2,1,0:T(8,128)(2,1)}, f32[8,128]{1,0:T(8,128)S(1)}) custom-call(s32[3]{0:T(128)S(1)} %get-tuple-element.39.place_ref, bf16[1,4,8,16,512]{4,3,2,1,0:T(8,128)(2,1)S(1)} %maximum_bitcast_fusion.1.refs_0_.refs_3_, ...), custom_call_target="tpu_custom_call", output_to_operand_aliasing={{0}: (13, {})} | custom-call | tf_op jit(solution)/shard_map/correlate/pallas_call | solution.py:270
  184.2 4.1 %collective-permute-done.24.refs_6_ = bf16[1,4,8,16,512]{4,3,2,1,0:T(8,128)(2,1)S(1)} collective-permute-done((bf16[1,4,8,16,512]{4,3,2,1,0:T(8,128)(2,1)}, bf16[1,4,8,16,512]{4,3,2,1,0:T(8,128)(2,1)S(1)}, u32[]{:S(2)}, u32[]{:S(2)}) %collective-permute-start.24) | collective-permute-done | bytes 524320 | tf_op jit(solution)/shard_map/ppermute | solution.py:319
  188.3 1.9 collective-permute-done.31.refs_10_
  190.2 6.6 %correlate.7 = (bf16[2,8,256,2048]{3,2,1,0:T(8,128)(2,1)}, f32[8,128]{1,0:T(8,128)}) custom-call(s32[3]{0:T(128)S(1)} %get-tuple-element.57.place_ref, bf16[1,4,8,16,512]{4,3,2,1,0:T(8,128)(2,1)S(1)} %maximum_bitcast_fusion.1.refs_0_.refs_3_, bf16[1,4,8,16,512]{4,3,2,1,0:T(8,128)(2,1)S(1)} %maximum_bitcast_fusion.2.refs_1_.refs_4_, ...), custom_call_target="tpu_custom_call", output_to_operand_aliasing={{0}: (13, {})} | custom-call | tf_op jit(solution)/shard_map/correlate/pallas_call | solution.py:270
  (86 shorter events, 17.8 us)
Async XLA Ops:
  13.3 6.9 %collective-permute-start = (bf16[8,16,512]{2,1,0:T(8,128)(2,1)S(1)}, bf16[8,16,512]{2,1,0:T(8,128)(2,1)S(1)}, u32[]{:S(2)}, u32[]{:S(2)}) collective-permute-start(bf16[8,16,512]{2,1,0:T(8,128)(2,1)S(1)} %get-tuple-element.54), channel_id=1, source_target_pairs={{0,8},{8,0},{16,24},{24,16},{1,9},{9,1},{17,25},{25,17},{2,10},{10... | collective-permute-start | bytes 393224 | tf_op jit(solution)/shard_map/ppermute | solution.py:343
  16.3 7.8 %collective-permute-start.1 = (bf16[8,16,512]{2,1,0:T(8,128)(2,1)S(1)}, bf16[8,16,512]{2,1,0:T(8,128)(2,1)S(1)}, u32[]{:S(2)}, u32[]{:S(2)}) collective-permute-start(bf16[8,16,512]{2,1,0:T(8,128)(2,1)S(1)} %get-tuple-element.53), channel_id=1, source_target_pairs={{0,16},{8,24},{16,0},{24,8},{1,17},{9,25},{17,1},{25,9},{2,18},{10... | collective-permute-start | bytes 393224 | tf_op jit(solution)/shard_map/ppermute | solution.py:343
  17.8 6.2 %collective-permute-start.2 = (bf16[8,16,512]{2,1,0:T(8,128)(2,1)S(1)}, bf16[8,16,512]{2,1,0:T(8,128)(2,1)S(1)}, u32[]{:S(2)}, u32[]{:S(2)}) collective-permute-start(bf16[8,16,512]{2,1,0:T(8,128)(2,1)S(1)} %get-tuple-element.52), channel_id=1, source_target_pairs={{0,24},{8,16},{16,8},{24,0},{1,25},{9,17},{17,9},{25,1},{2,26},{10... | collective-permute-start | bytes 393224 | tf_op jit(solution)/shard_map/ppermute | solution.py:343
  24.1 21.6 %collective-permute-start.10 = (bf16[1,4,8,16,512]{4,3,2,1,0:T(8,128)(2,1)S(1)}, bf16[1,4,8,16,512]{4,3,2,1,0:T(8,128)(2,1)S(1)}, u32[]{:S(2)}, u32[]{:S(2)}) collective-permute-start(bf16[1,4,8,16,512]{4,3,2,1,0:T(8,128)(2,1)S(1)} %maximum_bitcast_fusion.1.refs_0_.refs_3_), channel_id=1, source_target_pairs={{0,2},{1,3},{2,4},{3,5},{4,6},{5,7},{6,0},{7,1},{8,10},{9,11},{10,... | collective-permute-start | bytes 1572872 | tf_op jit(solution)/shard_map/ppermute | solution.py:319
  36.1 6.3 %collective-permute-start.3 = (bf16[8,16,512]{2,1,0:T(8,128)(2,1)S(1)}, bf16[8,16,512]{2,1,0:T(8,128)(2,1)S(1)}, u32[]{:S(2)}, u32[]{:S(2)}) collective-permute-start(bf16[8,16,512]{2,1,0:T(8,128)(2,1)S(1)} %get-tuple-element.50), channel_id=1, source_target_pairs={{0,8},{8,0},{16,24},{24,16},{1,9},{9,1},{17,25},{25,17},{2,10},{10... | collective-permute-start | bytes 393224 | tf_op jit(solution)/shard_map/ppermute | solution.py:343
  37.4 5.2 %collective-permute-start.4 = (bf16[8,16,512]{2,1,0:T(8,128)(2,1)S(1)}, bf16[8,16,512]{2,1,0:T(8,128)(2,1)S(1)}, u32[]{:S(2)}, u32[]{:S(2)}) collective-permute-start(bf16[8,16,512]{2,1,0:T(8,128)(2,1)S(1)} %get-tuple-element.49), channel_id=1, source_target_pairs={{0,16},{8,24},{16,0},{24,8},{1,17},{9,25},{17,1},{25,9},{2,18},{10... | collective-permute-start | bytes 393224 | tf_op jit(solution)/shard_map/ppermute | solution.py:343
  38.2 5.9 %collective-permute-start.5 = (bf16[8,16,512]{2,1,0:T(8,128)(2,1)S(1)}, bf16[8,16,512]{2,1,0:T(8,128)(2,1)S(1)}, u32[]{:S(2)}, u32[]{:S(2)}) collective-permute-start(bf16[8,16,512]{2,1,0:T(8,128)(2,1)S(1)} %get-tuple-element.48), channel_id=1, source_target_pairs={{0,24},{8,16},{16,8},{24,0},{1,25},{9,17},{17,9},{25,1},{2,26},{10... | collective-permute-start | bytes 393224 | tf_op jit(solution)/shard_map/ppermute | solution.py:343
  44.1 31.2 %collective-permute-start.9 = (bf16[1,4,8,16,512]{4,3,2,1,0:T(8,128)(2,1)S(1)}, bf16[1,4,8,16,512]{4,3,2,1,0:T(8,128)(2,1)S(1)}, u32[]{:S(2)}, u32[]{:S(2)}) collective-permute-start(bf16[1,4,8,16,512]{4,3,2,1,0:T(8,128)(2,1)S(1)} %maximum_bitcast_fusion.2.refs_1_.refs_4_), channel_id=1, source_target_pairs={{0,2},{1,3},{2,4},{3,5},{4,6},{5,7},{6,0},{7,1},{8,10},{9,11},{10,... | collective-permute-start | bytes 1572872 | tf_op jit(solution)/shard_map/ppermute | solution.py:319
  45.8 29.6 %collective-permute-start.11 = (bf16[1,4,8,16,512]{4,3,2,1,0:T(8,128)(2,1)S(1)}, bf16[1,4,8,16,512]{4,3,2,1,0:T(8,128)(2,1)}, u32[]{:S(2)}, u32[]{:S(2)}) collective-permute-start(bf16[1,4,8,16,512]{4,3,2,1,0:T(8,128)(2,1)S(1)} %collective-permute-done.10.refs_3_), channel_id=1, source_target_pairs={{0,2},{1,3},{2,4},{3,5},{4,6},{5,7},{6,0},{7,1},{8,10},{9,11},{10,... | collective-permute-start | bytes 1572872 | tf_op jit(solution)/shard_map/ppermute | solution.py:319
  66.5 8.8 %collective-permute-start.8 = (bf16[8,32,512]{2,1,0:T(8,128)(2,1)S(1)}, bf16[8,32,512]{2,1,0:T(8,128)(2,1)S(1)}, u32[]{:S(2)}, u32[]{:S(2)}) collective-permute-start(bf16[8,32,512]{2,1,0:T(8,128)(2,1)S(1)} %get-tuple-element.44), channel_id=1, source_target_pairs={{0,24},{8,16},{16,8},{24,0},{1,25},{9,17},{17,9},{25,1},{2,26},{10... | collective-permute-start | bytes 786440 | tf_op jit(solution)/shard_map/ppermute | solution.py:343
  68.1 10.7 %collective-permute-start.6 = (bf16[8,32,512]{2,1,0:T(8,128)(2,1)S(1)}, bf16[8,32,512]{2,1,0:T(8,128)(2,1)S(1)}, u32[]{:S(2)}, u32[]{:S(2)}) collective-permute-start(bf16[8,32,512]{2,1,0:T(8,128)(2,1)S(1)} %get-tuple-element.46), channel_id=1, source_target_pairs={{0,8},{8,0},{16,24},{24,16},{1,9},{9,1},{17,25},{25,17},{2,10},{10... | collective-permute-start | bytes 786440 | tf_op jit(solution)/shard_map/ppermute | solution.py:343
  69.5 9.2 %collective-permute-start.7 = (bf16[8,32,512]{2,1,0:T(8,128)(2,1)S(1)}, bf16[8,32,512]{2,1,0:T(8,128)(2,1)S(1)}, u32[]{:S(2)}, u32[]{:S(2)}) collective-permute-start(bf16[8,32,512]{2,1,0:T(8,128)(2,1)S(1)} %get-tuple-element.45), channel_id=1, source_target_pairs={{0,16},{8,24},{16,0},{24,8},{1,17},{9,25},{17,1},{25,9},{2,18},{10... | collective-permute-start | bytes 786440 | tf_op jit(solution)/shard_map/ppermute | solution.py:343
  78.9 28.1 %collective-permute-start.14 = (bf16[1,4,8,32,512]{4,3,2,1,0:T(8,128)(2,1)S(1)}, bf16[1,4,8,32,512]{4,3,2,1,0:T(8,128)(2,1)}, u32[]{:S(2)}, u32[]{:S(2)}) collective-permute-start(bf16[1,4,8,32,512]{4,3,2,1,0:T(8,128)(2,1)S(1)} %maximum_bitcast_fusion.refs_2_.refs_5_), channel_id=1, source_target_pairs={{0,2},{1,3},{2,4},{3,5},{4,6},{5,7},{6,0},{7,1},{8,10},{9,11},{10,... | collective-permute-start | bytes 3145736 | tf_op jit(solution)/shard_map/ppermute | solution.py:319
  79.4 3.0 %collective-permute-start.22 = (bf16[1,4,8,16,512]{4,3,2,1,0:T(8,128)(2,1)S(1)}, bf16[1,4,8,16,512]{4,3,2,1,0:T(8,128)(2,1)S(1)}, u32[]{:S(2)}, u32[]{:S(2)}) collective-permute-start(bf16[1,4,8,16,512]{4,3,2,1,0:T(8,128)(2,1)S(1)} %maximum_bitcast_fusion.2.refs_1_.refs_4_), channel_id=1, source_target_pairs={{0,1},{1,0},{2,3},{3,2},{4,5},{5,4},{6,7},{7,6},{8,9},{9,8},{10,11... | collective-permute-start | bytes 1572872 | tf_op jit(solution)/shard_map/ppermute | solution.py:329
  79.4 4.3 %collective-permute-start.21 = (bf16[1,4,8,16,512]{4,3,2,1,0:T(8,128)(2,1)S(1)}, bf16[1,4,8,16,512]{4,3,2,1,0:T(8,128)(2,1)S(1)}, u32[]{:S(2)}, u32[]{:S(2)}) collective-permute-start(bf16[1,4,8,16,512]{4,3,2,1,0:T(8,128)(2,1)S(1)} %maximum_bitcast_fusion.1.refs_0_.refs_3_), channel_id=1, source_target_pairs={{0,1},{1,0},{2,3},{3,2},{4,5},{5,4},{6,7},{7,6},{8,9},{9,8},{10,11... | collective-permute-start | bytes 1572872 | tf_op jit(solution)/shard_map/ppermute | solution.py:329
  81.1 48.2 %collective-permute-start.12 = (bf16[2,4,8,16,512]{4,3,2,1,0:T(8,128)(2,1)S(1)}, bf16[2,4,8,16,512]{4,3,2,1,0:T(8,128)(2,1)S(1)}, u32[]{:S(2)}, u32[]{:S(2)}) collective-permute-start(bf16[2,4,8,16,512]{4,3,2,1,0:T(8,128)(2,1)S(1)} %pad_maximum_fusion), channel_id=1, source_target_pairs={{0,2},{1,3},{2,4},{3,5},{4,6},{5,7},{6,0},{7,1},{8,10},{9,11},{10,... | collective-permute-start | bytes 3145736 | tf_op jit(solution)/shard_map/ppermute | solution.py:350
  82.4 26.6 %collective-permute-start.19 = (bf16[1,4,8,16,512]{4,3,2,1,0:T(8,128)(2,1)S(1)}, bf16[1,4,8,16,512]{4,3,2,1,0:T(8,128)(2,1)S(1)}, u32[]{:S(2)}, u32[]{:S(2)}) collective-permute-start(bf16[1,4,8,16,512]{4,3,2,1,0:T(8,128)(2,1)S(1)} %collective-permute-done.9.refs_4_), channel_id=1, source_target_pairs={{0,1},{1,0},{2,3},{3,2},{4,5},{5,4},{6,7},{7,6},{8,9},{9,8},{10,11... | collective-permute-start | bytes 1572872 | tf_op jit(solution)/shard_map/ppermute | solution.py:329
  83.2 46.9 %collective-permute-start.23 = (bf16[1,4,8,32,512]{4,3,2,1,0:T(8,128)(2,1)S(1)}, bf16[1,4,8,32,512]{4,3,2,1,0:T(8,128)(2,1)S(1)}, u32[]{:S(2)}, u32[]{:S(2)}) collective-permute-start(bf16[1,4,8,32,512]{4,3,2,1,0:T(8,128)(2,1)S(1)} %maximum_bitcast_fusion.refs_2_.refs_5_), channel_id=1, source_target_pairs={{0,1},{1,0},{2,3},{3,2},{4,5},{5,4},{6,7},{7,6},{8,9},{9,8},{10,11... | collective-permute-start | bytes 3145736 | tf_op jit(solution)/shard_map/ppermute | solution.py:329
  83.7 25.3 %collective-permute-start.18 = (bf16[1,4,8,16,512]{4,3,2,1,0:T(8,128)(2,1)S(1)}, bf16[1,4,8,16,512]{4,3,2,1,0:T(8,128)(2,1)S(1)}, u32[]{:S(2)}, u32[]{:S(2)}) collective-permute-start(bf16[1,4,8,16,512]{4,3,2,1,0:T(8,128)(2,1)S(1)} %collective-permute-done.10.refs_3_), channel_id=1, source_target_pairs={{0,1},{1,0},{2,3},{3,2},{4,5},{5,4},{6,7},{7,6},{8,9},{9,8},{10,11... | collective-permute-start | bytes 1572872 | tf_op jit(solution)/shard_map/ppermute | solution.py:329
  106.9 42.7 %collective-permute-start.20 = (bf16[1,4,8,32,512]{4,3,2,1,0:T(8,128)(2,1)}, bf16[1,4,8,32,512]{4,3,2,1,0:T(8,128)(2,1)}, u32[]{:S(2)}, u32[]{:S(2)}) collective-permute-start(bf16[1,4,8,32,512]{4,3,2,1,0:T(8,128)(2,1)} %collective-permute-done.14.refs_5_), channel_id=1, source_target_pairs={{0,1},{1,0},{2,3},{3,2},{4,5},{5,4},{6,7},{7,6},{8,9},{9,8},{10,11... | collective-permute-start | bytes 3145736 | tf_op jit(solution)/shard_map/ppermute | solution.py:329
  109.0 31.6 %collective-permute-start.15 = (bf16[1,4,8,16,512]{4,3,2,1,0:T(8,128)(2,1)S(1)}, bf16[1,4,8,16,512]{4,3,2,1,0:T(8,128)(2,1)}, u32[]{:S(2)}, u32[]{:S(2)}) collective-permute-start(bf16[1,4,8,16,512]{4,3,2,1,0:T(8,128)(2,1)S(1)} %get-tuple-element.42), channel_id=1, source_target_pairs={{0,2},{1,3},{2,4},{3,5},{4,6},{5,7},{6,0},{7,1},{8,10},{9,11},{10,... | collective-permute-start | bytes 1572872 | tf_op jit(solution)/shard_map/ppermute | solution.py:319
  109.0 51.5 %collective-permute-start.28 = (bf16[1,4,8,16,512]{4,3,2,1,0:T(8,128)(2,1)}, bf16[1,4,8,16,512]{4,3,2,1,0:T(8,128)(2,1)}, u32[]{:S(2)}, u32[]{:S(2)}) collective-permute-start(bf16[1,4,8,16,512]{4,3,2,1,0:T(8,128)(2,1)} %collective-permute-done.11.refs_3_), channel_id=1, source_target_pairs={{0,1},{1,0},{2,3},{3,2},{4,5},{5,4},{6,7},{7,6},{8,9},{9,8},{10,11... | collective-permute-start | bytes 1572872 | tf_op jit(solution)/shard_map/ppermute | solution.py:329
  129.3 31.2 %collective-permute-start.17 = (bf16[1,4,8,16,512]{4,3,2,1,0:T(8,128)(2,1)}, bf16[1,4,8,16,512]{4,3,2,1,0:T(8,128)(2,1)}, u32[]{:S(2)}, u32[]{:S(2)}) collective-permute-start(bf16[1,4,8,16,512]{4,3,2,1,0:T(8,128)(2,1)} %get-tuple-element.41), channel_id=1, source_target_pairs={{0,2},{1,3},{2,4},{3,5},{4,6},{5,7},{6,0},{7,1},{8,10},{9,11},{10,... | collective-permute-start | bytes 1572872 | tf_op jit(solution)/shard_map/ppermute | solution.py:319
  131.1 46.2 %collective-permute-start.25 = (bf16[2,4,8,16,512]{4,3,2,1,0:T(8,128)(2,1)S(1)}, bf16[2,4,8,16,512]{4,3,2,1,0:T(8,128)(2,1)}, u32[]{:S(2)}, u32[]{:S(2)}) collective-permute-start(bf16[2,4,8,16,512]{4,3,2,1,0:T(8,128)(2,1)S(1)} %collective-permute-done.12.refs_4_.refs_3_), channel_id=1, source_target_pairs={{0,1},{1,0},{2,3},{3,2},{4,5},{5,4},{6,7},{7,6},{8,9},{9,8},{10,11... | collective-permute-start | bytes 3145736 | tf_op jit(solution)/shard_map/ppermute | solution.py:329
  140.6 20.4 %collective-permute-start.13 = (bf16[1,4,8,16,512]{4,3,2,1,0:T(8,128)(2,1)}, bf16[1,4,8,16,512]{4,3,2,1,0:T(8,128)(2,1)}, u32[]{:S(2)}, u32[]{:S(2)}) collective-permute-start(bf16[1,4,8,16,512]{4,3,2,1,0:T(8,128)(2,1)} %slice.93), channel_id=1, source_target_pairs={{0,2},{1,3},{2,4},{3,5},{4,6},{5,7},{6,0},{7,1},{8,10},{9,11},{10,... | collective-permute-start | bytes 1572872 | tf_op jit(solution)/shard_map/ppermute | solution.py:319
  149.6 12.5 %collective-permute-start.29 = (bf16[1,4,8,16,512]{4,3,2,1,0:T(8,128)(2,1)}, bf16[1,4,8,16,512]{4,3,2,1,0:T(8,128)(2,1)S(1)}, u32[]{:S(2)}, u32[]{:S(2)}) collective-permute-start(bf16[1,4,8,16,512]{4,3,2,1,0:T(8,128)(2,1)} %collective-permute-done.15.refs_5_), channel_id=1, source_target_pairs={{0,1},{1,0},{2,3},{3,2},{4,5},{5,4},{6,7},{7,6},{8,9},{9,8},{10,11... | collective-permute-start | bytes 1572872 | tf_op jit(solution)/shard_map/ppermute | solution.py:329
  160.5 16.8 %collective-permute-start.16 = (bf16[1,4,8,16,512]{4,3,2,1,0:T(8,128)(2,1)}, bf16[1,4,8,16,512]{4,3,2,1,0:T(8,128)(2,1)S(1)}, u32[]{:S(2)}, u32[]{:S(2)}) collective-permute-start(bf16[1,4,8,16,512]{4,3,2,1,0:T(8,128)(2,1)} %collective-permute-done.15.refs_5_), channel_id=1, source_target_pairs={{0,2},{1,3},{2,4},{3,5},{4,6},{5,7},{6,0},{7,1},{8,10},{9,11},{10,... | collective-permute-start | bytes 1572872 | tf_op jit(solution)/shard_map/ppermute | solution.py:319
  160.5 16.8 %collective-permute-start.30 = (bf16[1,4,8,16,512]{4,3,2,1,0:T(8,128)(2,1)}, bf16[1,4,8,16,512]{4,3,2,1,0:T(8,128)(2,1)S(1)}, u32[]{:S(2)}, u32[]{:S(2)}) collective-permute-start(bf16[1,4,8,16,512]{4,3,2,1,0:T(8,128)(2,1)} %collective-permute-done.17.refs_6_), channel_id=1, source_target_pairs={{0,1},{1,0},{2,3},{3,2},{4,5},{5,4},{6,7},{7,6},{8,9},{9,8},{10,11... | collective-permute-start | bytes 1572872 | tf_op jit(solution)/shard_map/ppermute | solution.py:329
  161.1 27.2 %collective-permute-start.24 = (bf16[1,4,8,16,512]{4,3,2,1,0:T(8,128)(2,1)}, bf16[1,4,8,16,512]{4,3,2,1,0:T(8,128)(2,1)S(1)}, u32[]{:S(2)}, u32[]{:S(2)}) collective-permute-start(bf16[1,4,8,16,512]{4,3,2,1,0:T(8,128)(2,1)} %collective-permute-done.17.refs_6_), channel_id=1, source_target_pairs={{0,2},{1,3},{2,4},{3,5},{4,6},{5,7},{6,0},{7,1},{8,10},{9,11},{10,... | collective-permute-start | bytes 1572872 | tf_op jit(solution)/shard_map/ppermute | solution.py:319
  162.2 26.1 %collective-permute-start.26 = (bf16[1,4,8,16,512]{4,3,2,1,0:T(8,128)(2,1)}, bf16[1,4,8,16,512]{4,3,2,1,0:T(8,128)(2,1)S(1)}, u32[]{:S(2)}, u32[]{:S(2)}) collective-permute-start(bf16[1,4,8,16,512]{4,3,2,1,0:T(8,128)(2,1)} %collective-permute-done.13.refs_4_), channel_id=1, source_target_pairs={{0,1},{1,0},{2,3},{3,2},{4,5},{5,4},{6,7},{7,6},{8,9},{9,8},{10,11... | collective-permute-start | bytes 1572872 | tf_op jit(solution)/shard_map/ppermute | solution.py:329
  177.3 11.0 %collective-permute-start.27 = (bf16[1,4,8,16,512]{4,3,2,1,0:T(8,128)(2,1)S(1)}, bf16[1,4,8,16,512]{4,3,2,1,0:T(8,128)(2,1)S(1)}, u32[]{:S(2)}, u32[]{:S(2)}) collective-permute-start(bf16[1,4,8,16,512]{4,3,2,1,0:T(8,128)(2,1)S(1)} %collective-permute-done.16.refs_5_), channel_id=1, source_target_pairs={{0,1},{1,0},{2,3},{3,2},{4,5},{5,4},{6,7},{7,6},{8,9},{9,8},{10,11... | collective-permute-start | bytes 1572872 | tf_op jit(solution)/shard_map/ppermute | solution.py:329
  188.3 1.9 collective-permute-start.31
  (14 other events, 212.7 us)

commit v8 on v7

--- a/solution.py
+++ b/solution.py
@@ -358,8 +358,14 @@
             held[1, 2], held[1, 3] = (third[:, :, :, :middle], 0), (third[:, :, :, middle:], 0)
         for name in names:
             if step:
-                late = ahead and step == 3 and name == 3
-                move_on(step, name, *([tokens[2]] if late else []))
+                others = []
+                if ahead and (step, name) == (2, 2):
+                    others = [tokens[1]]
+                elif ahead and (step, name) == (3, 1):
+                    others = [tokens[2]]
+                elif ahead and (step, name) == (3, 3):
+                    others = [held[3, 1][0]]
+                move_on(step, name, *others)
         for name in names:
             late = step == ring - 1 and step and name == names[-1]
             swap_cores(step, name, *([tokens[-1]] if late else []))

time: 198 us -> 190 us (0.960)
  local copies, waits for them, and re-layouts: 13 us -> 4.17 us
  waiting for transfers between devices: 92.7 us -> 96.4 us
    ppermute x9, waiting for transfers between devices: 51.8 us -> 61.7 us  [move_on(): held[step, stream] = (lax.ppermute(piece, 'tm', onward), 0)]
    unnamed x28 -> x12, local copies, waits for them, and re-layouts: 9.26 us -> 2.09 us
    ppermute x1, waiting for transfers between devices: 19.7 us -> 13.4 us  [on_device(): both = lax.ppermute(both, 'tm', onward)]
  transfers between devices with their start and end apart: 32 -> 32, of which waited for: 13 -> 15; matrix products, arithmetic and copies ran while one was open for 2% -> 1% of each run, Pallas kernels for 25% -> 26%
where the time goes in v8:
time: 190 us
  waiting for transfers between devices  96.4 us (51%)
  Pallas kernels  64.4 us (34%)
  starting transfers between devices  20.5 us (11%)
  local copies, waits for them, and re-layouts  4.17 us (2%)
  other arithmetic  3.74 us (2%)
    ppermute x9, waiting for transfers between devices, move_on(): held[step, stream] = (lax.ppermute(piece, 'tm', onward), 0)  61.7 us
    pallas_call x3, Pallas kernels, channelize(): pl.pallas_call(functools.partial(channelize_kernel, channels, first_group...  39.6 us
    pallas_call x4, Pallas kernels, correlate(): pl.pallas_call(functools.partial(correlate_kernel, (len(own), len(same),...  24.8 us
    ppermute x9, waiting for transfers between devices, on_device(): parts.append(lax.ppermute(spectra[k], 'freq', partners))  19.3 us
    ppermute x1, waiting for transfers between devices, on_device(): both = lax.ppermute(both, 'tm', onward)  13.4 us
    ppermute x9, starting transfers between devices, on_device(): parts.append(lax.ppermute(spectra[k], 'freq', partners))  11.7 us
    ppermute x9, starting transfers between devices, move_on(): held[step, stream] = (lax.ppermute(piece, 'tm', onward), 0)  5.46 us
  transfers between devices with their start and end apart: 32, of which 15 were waited for; matrix products, arithmetic and copies ran while one was open for 1% of the time, Pallas kernels for 26%

profile of v8, /device:TPU:0, one launch (start us, length us, event | category | flops | bytes accessed | tf_op | source)
XLA Modules:
  0.0 189.5 jit_solution(2794055167806676666)
XLA Ops:
  2.9 10.3 %channelize.3 = bf16[32,16,512]{2,1,0:T(8,128)(2,1)S(1)} custom-call(bf16[64,530432]{1,0:T(8,128)(2,1)} %x_hbm.5, bf16[2048,256]{1,0:T(8,128)(2,1)S(1)} %copy.7.w_ref, f32[8,128]{1,0:T(8,128)S(1)} %broadcast_in_dim.8.after_ref.refs_9_), custom_call_target="tpu_custom_call" | custom-call | flops 4345298944 | bytes 16973824 | tf_op jit(solution)/shard_map/channelize/pallas_call | solution.py:176
  13.3 3.0 %collective-permute-start = (bf16[8,16,512]{2,1,0:T(8,128)(2,1)S(1)}, bf16[8,16,512]{2,1,0:T(8,128)(2,1)S(1)}, u32[]{:S(2)}, u32[]{:S(2)}) collective-permute-start(bf16[8,16,512]{2,1,0:T(8,128)(2,1)S(1)} %get-tuple-element.58), channel_id=1, source_target_pairs={{0,8},{8,0},{16,24},{24,16},{1,9},{9,1},{17,25},{25,17},{2,10},{10... | collective-permute-start | bytes 393224 | tf_op jit(solution)/shard_map/ppermute | solution.py:343
  16.3 1.5 collective-permute-start.1
  17.8 2.4 %collective-permute-done = bf16[8,16,512]{2,1,0:T(8,128)(2,1)S(1)} collective-permute-done((bf16[8,16,512]{2,1,0:T(8,128)(2,1)S(1)}, bf16[8,16,512]{2,1,0:T(8,128)(2,1)S(1)}, u32[]{:S(2)}, u32[]{:S(2)}) %collective-permute-start) | collective-permute-done | bytes 131104 | tf_op jit(solution)/shard_map/ppermute | solution.py:343
  20.2 3.9 %collective-permute-done.1 = bf16[8,16,512]{2,1,0:T(8,128)(2,1)S(1)} collective-permute-done((bf16[8,16,512]{2,1,0:T(8,128)(2,1)S(1)}, bf16[8,16,512]{2,1,0:T(8,128)(2,1)S(1)}, u32[]{:S(2)}, u32[]{:S(2)}) %collective-permute-start.1) | collective-permute-done | bytes 131104 | tf_op jit(solution)/shard_map/ppermute | solution.py:343
  24.1 1.6 collective-permute-start.10
  25.7 10.3 %channelize.4 = bf16[32,16,512]{2,1,0:T(8,128)(2,1)S(1)} custom-call(bf16[64,530432]{1,0:T(8,128)(2,1)} %x_hbm.5, bf16[2048,256]{1,0:T(8,128)(2,1)S(1)} %copy.7.w_ref, f32[8,128]{1,0:T(8,128)S(1)} %broadcast_in_dim.8.after_ref.refs_9_), custom_call_target="tpu_custom_call" | custom-call | flops 4345298944 | bytes 16973824 | tf_op jit(solution)/shard_map/channelize/pallas_call | solution.py:176
  36.1 1.3 collective-permute-start.3
  38.2 1.4 collective-permute-start.5
  39.6 2.7 %collective-permute-done.3 = bf16[8,16,512]{2,1,0:T(8,128)(2,1)S(1)} collective-permute-done((bf16[8,16,512]{2,1,0:T(8,128)(2,1)S(1)}, bf16[8,16,512]{2,1,0:T(8,128)(2,1)S(1)}, u32[]{:S(2)}, u32[]{:S(2)}) %collective-permute-start.3) | collective-permute-done | bytes 131104 | tf_op jit(solution)/shard_map/ppermute | solution.py:343
  42.6 1.5 collective-permute-done.5
  44.1 1.6 collective-permute-start.9
  45.8 1.6 collective-permute-start.11
  47.3 19.0 %channelize.5 = bf16[32,32,512]{2,1,0:T(8,128)(2,1)S(1)} custom-call(bf16[64,530432]{1,0:T(8,128)(2,1)} %x_hbm.5, bf16[2048,256]{1,0:T(8,128)(2,1)S(1)} %copy.7.w_ref, f32[8,128]{1,0:T(8,128)S(1)} %broadcast_in_dim.8.after_ref.refs_9_), custom_call_target="tpu_custom_call" | custom-call | flops 8690597888 | bytes 33947648 | tf_op jit(solution)/shard_map/channelize/pallas_call | solution.py:176
  66.5 1.6 collective-permute-start.8
  68.1 1.4 collective-permute-start.6
  70.1 5.3 %collective-permute-done.8 = bf16[8,32,512]{2,1,0:T(8,128)(2,1)S(1)} collective-permute-done((bf16[8,32,512]{2,1,0:T(8,128)(2,1)S(1)}, bf16[8,32,512]{2,1,0:T(8,128)(2,1)S(1)}, u32[]{:S(2)}, u32[]{:S(2)}) %collective-permute-start.8) | collective-permute-done | bytes 262176 | tf_op jit(solution)/shard_map/ppermute | solution.py:343
  75.4 3.4 %collective-permute-done.6 = bf16[8,32,512]{2,1,0:T(8,128)(2,1)S(1)} collective-permute-done((bf16[8,32,512]{2,1,0:T(8,128)(2,1)S(1)}, bf16[8,32,512]{2,1,0:T(8,128)(2,1)S(1)}, u32[]{:S(2)}, u32[]{:S(2)}) %collective-permute-start.6) | collective-permute-done | bytes 262176 | tf_op jit(solution)/shard_map/ppermute | solution.py:343
  81.0 1.3 collective-permute-start.12
  82.3 24.6 %collective-permute-done.13.refs_5_ = bf16[1,4,8,32,512]{4,3,2,1,0:T(8,128)(2,1)} collective-permute-done((bf16[1,4,8,32,512]{4,3,2,1,0:T(8,128)(2,1)S(1)}, bf16[1,4,8,32,512]{4,3,2,1,0:T(8,128)(2,1)}, u32[]{:S(2)}, u32[]{:S(2)}) %collective-permute-start.13) | collective-permute-done | bytes 1048608 | tf_op jit(solution)/shard_map/ppermute | solution.py:319
  107.7 6.8 %correlate.4 = (bf16[2,8,256,2048]{3,2,1,0:T(8,128)(2,1)}, f32[8,128]{1,0:T(8,128)S(1)}) custom-call(s32[3]{0:T(128)S(1)} %get-tuple-element.59.place_ref, bf16[1,4,8,16,512]{4,3,2,1,0:T(8,128)(2,1)S(1)} %maximum_bitcast_fusion.1.refs_0_.refs_3_, bf16[1,4,8,16,512]{4,3,2,1,0:T(8,128)(2,1)S(1)} %maximum_bitcast_fusion.2.refs_1_.refs_4_, ...), custom_call_target="tpu_custom_call" | custom-call | tf_op jit(solution)/shard_map/correlate/pallas_call | solution.py:270
  114.5 1.3 fusion.6
  115.9 13.4 %collective-permute-done.12.refs_4_.refs_3_ = bf16[2,4,8,16,512]{4,3,2,1,0:T(8,128)(2,1)S(1)} collective-permute-done((bf16[2,4,8,16,512]{4,3,2,1,0:T(8,128)(2,1)}, bf16[2,4,8,16,512]{4,3,2,1,0:T(8,128)(2,1)S(1)}, u32[]{:S(2)}, u32[]{:S(2)}) %collective-permute-start.12) | collective-permute-done | bytes 1048608 | tf_op jit(solution)/shard_map/ppermute | solution.py:350
  131.5 6.9 %correlate.5 = (bf16[2,8,256,2048]{3,2,1,0:T(8,128)(2,1)}, f32[8,128]{1,0:T(8,128)S(1)}) custom-call(s32[3]{0:T(128)S(1)} %get-tuple-element.60.place_ref, bf16[1,4,8,16,512]{4,3,2,1,0:T(8,128)(2,1)S(1)} %maximum_bitcast_fusion.1.refs_0_.refs_3_, ...), custom_call_target="tpu_custom_call", output_to_operand_aliasing={{0}: (11, {})} | custom-call | tf_op jit(solution)/shard_map/correlate/pallas_call | solution.py:270
  138.9 1.6 collective-permute-done.21.refs_5_
  140.5 11.2 %collective-permute-done.23.refs_6_ = bf16[1,4,8,16,512]{4,3,2,1,0:T(8,128)(2,1)S(1)} collective-permute-done((bf16[1,4,8,16,512]{4,3,2,1,0:T(8,128)(2,1)S(1)}, bf16[1,4,8,16,512]{4,3,2,1,0:T(8,128)(2,1)S(1)}, u32[]{:S(2)}, u32[]{:S(2)}) %collective-permute-start.23) | collective-permute-done | bytes 524320 | tf_op jit(solution)/shard_map/ppermute | solution.py:319
  151.8 11.2 %collective-permute-done.20.refs_4_ = bf16[1,4,8,16,512]{4,3,2,1,0:T(8,128)(2,1)S(1)} collective-permute-done((bf16[1,4,8,16,512]{4,3,2,1,0:T(8,128)(2,1)S(1)}, bf16[1,4,8,16,512]{4,3,2,1,0:T(8,128)(2,1)S(1)}, u32[]{:S(2)}, u32[]{:S(2)}) %collective-permute-start.20) | collective-permute-done | bytes 524320 | tf_op jit(solution)/shard_map/ppermute | solution.py:319
  163.0 10.7 %collective-permute-done.22.refs_5_ = bf16[1,4,8,16,512]{4,3,2,1,0:T(8,128)(2,1)S(1)} collective-permute-done((bf16[1,4,8,16,512]{4,3,2,1,0:T(8,128)(2,1)S(1)}, bf16[1,4,8,16,512]{4,3,2,1,0:T(8,128)(2,1)S(1)}, u32[]{:S(2)}, u32[]{:S(2)}) %collective-permute-start.22) | collective-permute-done | bytes 524320 | tf_op jit(solution)/shard_map/ppermute | solution.py:319
  173.7 5.5 %correlate.6 = (bf16[2,8,256,2048]{3,2,1,0:T(8,128)(2,1)}, f32[8,128]{1,0:T(8,128)S(1)}) custom-call(s32[3]{0:T(128)S(1)} %get-tuple-element.43.place_ref, bf16[1,4,8,16,512]{4,3,2,1,0:T(8,128)(2,1)S(1)} %maximum_bitcast_fusion.1.refs_0_.refs_3_, ...), custom_call_target="tpu_custom_call", output_to_operand_aliasing={{0}: (13, {})} | custom-call | tf_op jit(solution)/shard_map/correlate/pallas_call | solution.py:270
  179.7 2.3 %collective-permute-done.24.refs_6_ = bf16[1,4,8,16,512]{4,3,2,1,0:T(8,128)(2,1)S(1)} collective-permute-done((bf16[1,4,8,16,512]{4,3,2,1,0:T(8,128)(2,1)S(1)}, bf16[1,4,8,16,512]{4,3,2,1,0:T(8,128)(2,1)S(1)}, u32[]{:S(2)}, u32[]{:S(2)}) %collective-permute-start.24) | collective-permute-done | bytes 524320 | tf_op jit(solution)/shard_map/ppermute | solution.py:319
  182.1 1.9 %collective-permute-done.31.refs_10_ = bf16[1,4,8,16,512]{4,3,2,1,0:T(8,128)(2,1)S(1)} collective-permute-done((bf16[1,4,8,16,512]{4,3,2,1,0:T(8,128)(2,1)S(1)}, bf16[1,4,8,16,512]{4,3,2,1,0:T(8,128)(2,1)S(1)}, u32[]{:S(2)}, u32[]{:S(2)}) %collective-permute-start.31) | collective-permute-done | bytes 524320 | tf_op jit(solution)/shard_map/ppermute | solution.py:329
  184.0 5.5 %correlate.7 = (bf16[2,8,256,2048]{3,2,1,0:T(8,128)(2,1)}, f32[8,128]{1,0:T(8,128)}) custom-call(s32[3]{0:T(128)S(1)} %get-tuple-element.61.place_ref, bf16[1,4,8,16,512]{4,3,2,1,0:T(8,128)(2,1)S(1)} %maximum_bitcast_fusion.1.refs_0_.refs_3_, bf16[1,4,8,16,512]{4,3,2,1,0:T(8,128)(2,1)S(1)} %maximum_bitcast_fusion.2.refs_1_.refs_4_, ...), custom_call_target="tpu_custom_call", output_to_operand_aliasing={{0}: (13, {})} | custom-call | tf_op jit(solution)/shard_map/correlate/pallas_call | solution.py:270
  (70 shorter events, 11.0 us)
Async XLA Ops:
  13.3 6.9 %collective-permute-start = (bf16[8,16,512]{2,1,0:T(8,128)(2,1)S(1)}, bf16[8,16,512]{2,1,0:T(8,128)(2,1)S(1)}, u32[]{:S(2)}, u32[]{:S(2)}) collective-permute-start(bf16[8,16,512]{2,1,0:T(8,128)(2,1)S(1)} %get-tuple-element.58), channel_id=1, source_target_pairs={{0,8},{8,0},{16,24},{24,16},{1,9},{9,1},{17,25},{25,17},{2,10},{10... | collective-permute-start | bytes 393224 | tf_op jit(solution)/shard_map/ppermute | solution.py:343
  16.3 7.8 %collective-permute-start.1 = (bf16[8,16,512]{2,1,0:T(8,128)(2,1)S(1)}, bf16[8,16,512]{2,1,0:T(8,128)(2,1)S(1)}, u32[]{:S(2)}, u32[]{:S(2)}) collective-permute-start(bf16[8,16,512]{2,1,0:T(8,128)(2,1)S(1)} %get-tuple-element.57), channel_id=1, source_target_pairs={{0,16},{8,24},{16,0},{24,8},{1,17},{9,25},{17,1},{25,9},{2,18},{10... | collective-permute-start | bytes 393224 | tf_op jit(solution)/shard_map/ppermute | solution.py:343
  17.8 6.2 %collective-permute-start.2 = (bf16[8,16,512]{2,1,0:T(8,128)(2,1)S(1)}, bf16[8,16,512]{2,1,0:T(8,128)(2,1)S(1)}, u32[]{:S(2)}, u32[]{:S(2)}) collective-permute-start(bf16[8,16,512]{2,1,0:T(8,128)(2,1)S(1)} %get-tuple-element.56), channel_id=1, source_target_pairs={{0,24},{8,16},{16,8},{24,0},{1,25},{9,17},{17,9},{25,1},{2,26},{10... | collective-permute-start | bytes 393224 | tf_op jit(solution)/shard_map/ppermute | solution.py:343
  24.1 21.6 %collective-permute-start.10 = (bf16[1,4,8,16,512]{4,3,2,1,0:T(8,128)(2,1)S(1)}, bf16[1,4,8,16,512]{4,3,2,1,0:T(8,128)(2,1)S(1)}, u32[]{:S(2)}, u32[]{:S(2)}) collective-permute-start(bf16[1,4,8,16,512]{4,3,2,1,0:T(8,128)(2,1)S(1)} %maximum_bitcast_fusion.1.refs_0_.refs_3_), channel_id=1, source_target_pairs={{0,2},{1,3},{2,4},{3,5},{4,6},{5,7},{6,0},{7,1},{8,10},{9,11},{10,... | collective-permute-start | bytes 1572872 | tf_op jit(solution)/shard_map/ppermute | solution.py:319
  36.1 6.3 %collective-permute-start.3 = (bf16[8,16,512]{2,1,0:T(8,128)(2,1)S(1)}, bf16[8,16,512]{2,1,0:T(8,128)(2,1)S(1)}, u32[]{:S(2)}, u32[]{:S(2)}) collective-permute-start(bf16[8,16,512]{2,1,0:T(8,128)(2,1)S(1)} %get-tuple-element.54), channel_id=1, source_target_pairs={{0,8},{8,0},{16,24},{24,16},{1,9},{9,1},{17,25},{25,17},{2,10},{10... | collective-permute-start | bytes 393224 | tf_op jit(solution)/shard_map/ppermute | solution.py:343
  37.4 5.2 %collective-permute-start.4 = (bf16[8,16,512]{2,1,0:T(8,128)(2,1)S(1)}, bf16[8,16,512]{2,1,0:T(8,128)(2,1)S(1)}, u32[]{:S(2)}, u32[]{:S(2)}) collective-permute-start(bf16[8,16,512]{2,1,0:T(8,128)(2,1)S(1)} %get-tuple-element.53), channel_id=1, source_target_pairs={{0,16},{8,24},{16,0},{24,8},{1,17},{9,25},{17,1},{25,9},{2,18},{10... | collective-permute-start | bytes 393224 | tf_op jit(solution)/shard_map/ppermute | solution.py:343
  38.2 5.9 %collective-permute-start.5 = (bf16[8,16,512]{2,1,0:T(8,128)(2,1)S(1)}, bf16[8,16,512]{2,1,0:T(8,128)(2,1)S(1)}, u32[]{:S(2)}, u32[]{:S(2)}) collective-permute-start(bf16[8,16,512]{2,1,0:T(8,128)(2,1)S(1)} %get-tuple-element.52), channel_id=1, source_target_pairs={{0,24},{8,16},{16,8},{24,0},{1,25},{9,17},{17,9},{25,1},{2,26},{10... | collective-permute-start | bytes 393224 | tf_op jit(solution)/shard_map/ppermute | solution.py:343
  44.1 31.2 %collective-permute-start.9 = (bf16[1,4,8,16,512]{4,3,2,1,0:T(8,128)(2,1)S(1)}, bf16[1,4,8,16,512]{4,3,2,1,0:T(8,128)(2,1)S(1)}, u32[]{:S(2)}, u32[]{:S(2)}) collective-permute-start(bf16[1,4,8,16,512]{4,3,2,1,0:T(8,128)(2,1)S(1)} %maximum_bitcast_fusion.2.refs_1_.refs_4_), channel_id=1, source_target_pairs={{0,2},{1,3},{2,4},{3,5},{4,6},{5,7},{6,0},{7,1},{8,10},{9,11},{10,... | collective-permute-start | bytes 1572872 | tf_op jit(solution)/shard_map/ppermute | solution.py:319
  45.8 29.6 %collective-permute-start.11 = (bf16[1,4,8,16,512]{4,3,2,1,0:T(8,128)(2,1)S(1)}, bf16[1,4,8,16,512]{4,3,2,1,0:T(8,128)(2,1)S(1)}, u32[]{:S(2)}, u32[]{:S(2)}) collective-permute-start(bf16[1,4,8,16,512]{4,3,2,1,0:T(8,128)(2,1)S(1)} %collective-permute-done.10.refs_3_), channel_id=1, source_target_pairs={{0,2},{1,3},{2,4},{3,5},{4,6},{5,7},{6,0},{7,1},{8,10},{9,11},{10,... | collective-permute-start | bytes 1572872 | tf_op jit(solution)/shard_map/ppermute | solution.py:319
  66.5 8.8 %collective-permute-start.8 = (bf16[8,32,512]{2,1,0:T(8,128)(2,1)S(1)}, bf16[8,32,512]{2,1,0:T(8,128)(2,1)S(1)}, u32[]{:S(2)}, u32[]{:S(2)}) collective-permute-start(bf16[8,32,512]{2,1,0:T(8,128)(2,1)S(1)} %get-tuple-element.48), channel_id=1, source_target_pairs={{0,24},{8,16},{16,8},{24,0},{1,25},{9,17},{17,9},{25,1},{2,26},{10... | collective-permute-start | bytes 786440 | tf_op jit(solution)/shard_map/ppermute | solution.py:343
  68.1 10.7 %collective-permute-start.6 = (bf16[8,32,512]{2,1,0:T(8,128)(2,1)S(1)}, bf16[8,32,512]{2,1,0:T(8,128)(2,1)S(1)}, u32[]{:S(2)}, u32[]{:S(2)}) collective-permute-start(bf16[8,32,512]{2,1,0:T(8,128)(2,1)S(1)} %get-tuple-element.50), channel_id=1, source_target_pairs={{0,8},{8,0},{16,24},{24,16},{1,9},{9,1},{17,25},{25,17},{2,10},{10... | collective-permute-start | bytes 786440 | tf_op jit(solution)/shard_map/ppermute | solution.py:343
  69.5 9.2 %collective-permute-start.7 = (bf16[8,32,512]{2,1,0:T(8,128)(2,1)S(1)}, bf16[8,32,512]{2,1,0:T(8,128)(2,1)S(1)}, u32[]{:S(2)}, u32[]{:S(2)}) collective-permute-start(bf16[8,32,512]{2,1,0:T(8,128)(2,1)S(1)} %get-tuple-element.49), channel_id=1, source_target_pairs={{0,16},{8,24},{16,0},{24,8},{1,17},{9,25},{17,1},{25,9},{2,18},{10... | collective-permute-start | bytes 786440 | tf_op jit(solution)/shard_map/ppermute | solution.py:343
  78.9 28.1 %collective-permute-start.13 = (bf16[1,4,8,32,512]{4,3,2,1,0:T(8,128)(2,1)S(1)}, bf16[1,4,8,32,512]{4,3,2,1,0:T(8,128)(2,1)}, u32[]{:S(2)}, u32[]{:S(2)}) collective-permute-start(bf16[1,4,8,32,512]{4,3,2,1,0:T(8,128)(2,1)S(1)} %maximum_bitcast_fusion.refs_2_.refs_5_), channel_id=1, source_target_pairs={{0,2},{1,3},{2,4},{3,5},{4,6},{5,7},{6,0},{7,1},{8,10},{9,11},{10,... | collective-permute-start | bytes 3145736 | tf_op jit(solution)/shard_map/ppermute | solution.py:319
  79.4 28.3 %collective-permute-start.19 = (bf16[1,4,8,32,512]{4,3,2,1,0:T(8,128)(2,1)S(1)}, bf16[1,4,8,32,512]{4,3,2,1,0:T(8,128)(2,1)}, u32[]{:S(2)}, u32[]{:S(2)}) collective-permute-start(bf16[1,4,8,32,512]{4,3,2,1,0:T(8,128)(2,1)S(1)} %maximum_bitcast_fusion.refs_2_.refs_5_), channel_id=1, source_target_pairs={{0,1},{1,0},{2,3},{3,2},{4,5},{5,4},{6,7},{7,6},{8,9},{9,8},{10,11... | collective-permute-start | bytes 3145736 | tf_op jit(solution)/shard_map/ppermute | solution.py:329
  79.4 27.6 %collective-permute-start.18 = (bf16[1,4,8,16,512]{4,3,2,1,0:T(8,128)(2,1)S(1)}, bf16[1,4,8,16,512]{4,3,2,1,0:T(8,128)(2,1)}, u32[]{:S(2)}, u32[]{:S(2)}) collective-permute-start(bf16[1,4,8,16,512]{4,3,2,1,0:T(8,128)(2,1)S(1)} %maximum_bitcast_fusion.2.refs_1_.refs_4_), channel_id=1, source_target_pairs={{0,1},{1,0},{2,3},{3,2},{4,5},{5,4},{6,7},{7,6},{8,9},{9,8},{10,11... | collective-permute-start | bytes 1572872 | tf_op jit(solution)/shard_map/ppermute | solution.py:329
  79.9 27.5 %collective-permute-start.17 = (bf16[1,4,8,16,512]{4,3,2,1,0:T(8,128)(2,1)S(1)}, bf16[1,4,8,16,512]{4,3,2,1,0:T(8,128)(2,1)}, u32[]{:S(2)}, u32[]{:S(2)}) collective-permute-start(bf16[1,4,8,16,512]{4,3,2,1,0:T(8,128)(2,1)S(1)} %maximum_bitcast_fusion.1.refs_0_.refs_3_), channel_id=1, source_target_pairs={{0,1},{1,0},{2,3},{3,2},{4,5},{5,4},{6,7},{7,6},{8,9},{9,8},{10,11... | collective-permute-start | bytes 1572872 | tf_op jit(solution)/shard_map/ppermute | solution.py:329
  81.0 48.3 %collective-permute-start.12 = (bf16[2,4,8,16,512]{4,3,2,1,0:T(8,128)(2,1)}, bf16[2,4,8,16,512]{4,3,2,1,0:T(8,128)(2,1)S(1)}, u32[]{:S(2)}, u32[]{:S(2)}) collective-permute-start(bf16[2,4,8,16,512]{4,3,2,1,0:T(8,128)(2,1)} %pad_maximum_fusion), channel_id=1, source_target_pairs={{0,2},{1,3},{2,4},{3,5},{4,6},{5,7},{6,0},{7,1},{8,10},{9,11},{10,... | collective-permute-start | bytes 3145736 | tf_op jit(solution)/shard_map/ppermute | solution.py:350
  106.9 22.4 %collective-permute-start.16 = (bf16[1,4,8,32,512]{4,3,2,1,0:T(8,128)(2,1)}, bf16[1,4,8,32,512]{4,3,2,1,0:T(8,128)(2,1)}, u32[]{:S(2)}, u32[]{:S(2)}) collective-permute-start(bf16[1,4,8,32,512]{4,3,2,1,0:T(8,128)(2,1)} %collective-permute-done.13.refs_5_), channel_id=1, source_target_pairs={{0,1},{1,0},{2,3},{3,2},{4,5},{5,4},{6,7},{7,6},{8,9},{9,8},{10,11... | collective-permute-start | bytes 3145736 | tf_op jit(solution)/shard_map/ppermute | solution.py:329
  107.0 22.4 %collective-permute-start.15 = (bf16[1,4,8,16,512]{4,3,2,1,0:T(8,128)(2,1)}, bf16[1,4,8,16,512]{4,3,2,1,0:T(8,128)(2,1)}, u32[]{:S(2)}, u32[]{:S(2)}) collective-permute-start(bf16[1,4,8,16,512]{4,3,2,1,0:T(8,128)(2,1)} %copy-done.2), channel_id=1, source_target_pairs={{0,1},{1,0},{2,3},{3,2},{4,5},{5,4},{6,7},{7,6},{8,9},{9,8},{10,11... | collective-permute-start | bytes 1572872 | tf_op jit(solution)/shard_map/ppermute | solution.py:329
  107.5 21.9 %collective-permute-start.14 = (bf16[1,4,8,16,512]{4,3,2,1,0:T(8,128)(2,1)}, bf16[1,4,8,16,512]{4,3,2,1,0:T(8,128)(2,1)}, u32[]{:S(2)}, u32[]{:S(2)}) collective-permute-start(bf16[1,4,8,16,512]{4,3,2,1,0:T(8,128)(2,1)} %copy-done.4), channel_id=1, source_target_pairs={{0,1},{1,0},{2,3},{3,2},{4,5},{5,4},{6,7},{7,6},{8,9},{9,8},{10,11... | collective-permute-start | bytes 1572872 | tf_op jit(solution)/shard_map/ppermute | solution.py:329
  115.8 24.7 %collective-permute-start.21 = (bf16[1,4,8,16,512]{4,3,2,1,0:T(8,128)(2,1)S(1)}, bf16[1,4,8,16,512]{4,3,2,1,0:T(8,128)(2,1)S(1)}, u32[]{:S(2)}, u32[]{:S(2)}) collective-permute-start(bf16[1,4,8,16,512]{4,3,2,1,0:T(8,128)(2,1)S(1)} %get-tuple-element.36), channel_id=1, source_target_pairs={{0,2},{1,3},{2,4},{3,5},{4,6},{5,7},{6,0},{7,1},{8,10},{9,11},{10,... | collective-permute-start | bytes 1572872 | tf_op jit(solution)/shard_map/ppermute | solution.py:319
  129.3 22.5 %collective-permute-start.23 = (bf16[1,4,8,16,512]{4,3,2,1,0:T(8,128)(2,1)S(1)}, bf16[1,4,8,16,512]{4,3,2,1,0:T(8,128)(2,1)S(1)}, u32[]{:S(2)}, u32[]{:S(2)}) collective-permute-start(bf16[1,4,8,16,512]{4,3,2,1,0:T(8,128)(2,1)S(1)} %get-tuple-element.45), channel_id=1, source_target_pairs={{0,2},{1,3},{2,4},{3,5},{4,6},{5,7},{6,0},{7,1},{8,10},{9,11},{10,... | collective-permute-start | bytes 1572872 | tf_op jit(solution)/shard_map/ppermute | solution.py:319
  138.4 24.6 %collective-permute-start.20 = (bf16[1,4,8,16,512]{4,3,2,1,0:T(8,128)(2,1)S(1)}, bf16[1,4,8,16,512]{4,3,2,1,0:T(8,128)(2,1)S(1)}, u32[]{:S(2)}, u32[]{:S(2)}) collective-permute-start(bf16[1,4,8,16,512]{4,3,2,1,0:T(8,128)(2,1)S(1)} %slice.93), channel_id=1, source_target_pairs={{0,2},{1,3},{2,4},{3,5},{4,6},{5,7},{6,0},{7,1},{8,10},{9,11},{10,... | collective-permute-start | bytes 1572872 | tf_op jit(solution)/shard_map/ppermute | solution.py:319
  138.4 35.3 %collective-permute-start.25 = (bf16[2,4,8,16,512]{4,3,2,1,0:T(8,128)(2,1)S(1)}, bf16[2,4,8,16,512]{4,3,2,1,0:T(8,128)(2,1)S(1)}, u32[]{:S(2)}, u32[]{:S(2)}) collective-permute-start(bf16[2,4,8,16,512]{4,3,2,1,0:T(8,128)(2,1)S(1)} %collective-permute-done.12.refs_4_.refs_3_), channel_id=1, source_target_pairs={{0,1},{1,0},{2,3},{3,2},{4,5},{5,4},{6,7},{7,6},{8,9},{9,8},{10,11... | collective-permute-start | bytes 3145736 | tf_op jit(solution)/shard_map/ppermute | solution.py:329
  138.4 24.6 %collective-permute-start.28 = (bf16[1,4,8,16,512]{4,3,2,1,0:T(8,128)(2,1)S(1)}, bf16[1,4,8,16,512]{4,3,2,1,0:T(8,128)(2,1)S(1)}, u32[]{:S(2)}, u32[]{:S(2)}) collective-permute-start(bf16[1,4,8,16,512]{4,3,2,1,0:T(8,128)(2,1)S(1)} %copy-done.1), channel_id=1, source_target_pairs={{0,1},{1,0},{2,3},{3,2},{4,5},{5,4},{6,7},{7,6},{8,9},{9,8},{10,11... | collective-permute-start | bytes 1572872 | tf_op jit(solution)/shard_map/ppermute | solution.py:329
  140.5 33.1 %collective-permute-start.22 = (bf16[1,4,8,16,512]{4,3,2,1,0:T(8,128)(2,1)S(1)}, bf16[1,4,8,16,512]{4,3,2,1,0:T(8,128)(2,1)S(1)}, u32[]{:S(2)}, u32[]{:S(2)}) collective-permute-start(bf16[1,4,8,16,512]{4,3,2,1,0:T(8,128)(2,1)S(1)} %collective-permute-done.21.refs_5_), channel_id=1, source_target_pairs={{0,2},{1,3},{2,4},{3,5},{4,6},{5,7},{6,0},{7,1},{8,10},{9,11},{10,... | collective-permute-start | bytes 1572872 | tf_op jit(solution)/shard_map/ppermute | solution.py:319
  151.8 21.9 %collective-permute-start.29 = (bf16[1,4,8,16,512]{4,3,2,1,0:T(8,128)(2,1)S(1)}, bf16[1,4,8,16,512]{4,3,2,1,0:T(8,128)(2,1)S(1)}, u32[]{:S(2)}, u32[]{:S(2)}) collective-permute-start(bf16[1,4,8,16,512]{4,3,2,1,0:T(8,128)(2,1)S(1)} %collective-permute-done.21.refs_5_), channel_id=1, source_target_pairs={{0,1},{1,0},{2,3},{3,2},{4,5},{5,4},{6,7},{7,6},{8,9},{9,8},{10,11... | collective-permute-start | bytes 1572872 | tf_op jit(solution)/shard_map/ppermute | solution.py:329
  163.0 10.7 %collective-permute-start.30 = (bf16[1,4,8,16,512]{4,3,2,1,0:T(8,128)(2,1)S(1)}, bf16[1,4,8,16,512]{4,3,2,1,0:T(8,128)(2,1)S(1)}, u32[]{:S(2)}, u32[]{:S(2)}) collective-permute-start(bf16[1,4,8,16,512]{4,3,2,1,0:T(8,128)(2,1)S(1)} %collective-permute-done.23.refs_6_), channel_id=1, source_target_pairs={{0,1},{1,0},{2,3},{3,2},{4,5},{5,4},{6,7},{7,6},{8,9},{9,8},{10,11... | collective-permute-start | bytes 1572872 | tf_op jit(solution)/shard_map/ppermute | solution.py:329
  163.0 19.1 %collective-permute-start.24 = (bf16[1,4,8,16,512]{4,3,2,1,0:T(8,128)(2,1)S(1)}, bf16[1,4,8,16,512]{4,3,2,1,0:T(8,128)(2,1)S(1)}, u32[]{:S(2)}, u32[]{:S(2)}) collective-permute-start(bf16[1,4,8,16,512]{4,3,2,1,0:T(8,128)(2,1)S(1)} %collective-permute-done.23.refs_6_), channel_id=1, source_target_pairs={{0,2},{1,3},{2,4},{3,5},{4,6},{5,7},{6,0},{7,1},{8,10},{9,11},{10,... | collective-permute-start | bytes 1572872 | tf_op jit(solution)/shard_map/ppermute | solution.py:319
  173.7 8.4 %collective-permute-start.27 = (bf16[1,4,8,16,512]{4,3,2,1,0:T(8,128)(2,1)S(1)}, bf16[1,4,8,16,512]{4,3,2,1,0:T(8,128)(2,1)S(1)}, u32[]{:S(2)}, u32[]{:S(2)}) collective-permute-start(bf16[1,4,8,16,512]{4,3,2,1,0:T(8,128)(2,1)S(1)} %collective-permute-done.22.refs_5_), channel_id=1, source_target_pairs={{0,1},{1,0},{2,3},{3,2},{4,5},{5,4},{6,7},{7,6},{8,9},{9,8},{10,11... | collective-permute-start | bytes 1572872 | tf_op jit(solution)/shard_map/ppermute | solution.py:329
  179.2 2.8 %collective-permute-start.26 = (bf16[1,4,8,16,512]{4,3,2,1,0:T(8,128)(2,1)S(1)}, bf16[1,4,8,16,512]{4,3,2,1,0:T(8,128)(2,1)S(1)}, u32[]{:S(2)}, u32[]{:S(2)}) collective-permute-start(bf16[1,4,8,16,512]{4,3,2,1,0:T(8,128)(2,1)S(1)} %collective-permute-done.20.refs_4_), channel_id=1, source_target_pairs={{0,1},{1,0},{2,3},{3,2},{4,5},{5,4},{6,7},{7,6},{8,9},{9,8},{10,11... | collective-permute-start | bytes 1572872 | tf_op jit(solution)/shard_map/ppermute | solution.py:329
  182.1 1.9 %collective-permute-start.31 = (bf16[1,4,8,16,512]{4,3,2,1,0:T(8,128)(2,1)S(1)}, bf16[1,4,8,16,512]{4,3,2,1,0:T(8,128)(2,1)S(1)}, u32[]{:S(2)}, u32[]{:S(2)}) collective-permute-start(bf16[1,4,8,16,512]{4,3,2,1,0:T(8,128)(2,1)S(1)} %collective-permute-done.24.refs_6_), channel_id=1, source_target_pairs={{0,1},{1,0},{2,3},{3,2},{4,5},{5,4},{6,7},{7,6},{8,9},{9,8},{10,11... | collective-permute-start | bytes 1572872 | tf_op jit(solution)/shard_map/ppermute | solution.py:329
  (6 other events, 116.7 us)
